TPU v7x, 256 devices: a whole 4x4x8 slice. The times are simulated.
256 devices in a mesh: row: 16 (over z, x_lo), col: 16 (over y, x_hi, core).
Axes of the slice: x: 4 (x_hi: 2, x_lo: 2; x = x_hi * 2 + x_lo), y: 4, z: 8, core: 2. Of those that a mesh axis runs over, the one named last changes fastest.
Arguments:
- right_side: float32 [9, 49152], P(None, 'row'), may hold values from -12 to 12
- noise_level: float32 [49152], P('row'), may hold values from 0.5 to 2
- run_index: int32 [49152], P('row'), may hold values from 0 to 24575
- step_index: int32 [49152], P('row'), may hold values from 0 to 127
- run_features: float32 [16, 24576], replicated, may hold values from -5 to 5
Outputs:
- solution_field: float32 [9, 49152], P(None, 'row')
- residual: float32 [9, 49152], P(None, 'row')
All inputs are finite; a program needn't handle non-finite values.
Results may differ from a plain program's by a relative error of at most 0.0003.
Values sent between devices are 32-bit elements; how exact they have to be, the bound alone decides.
No kernel may reach another device: no remote copies, remote signals or barrier semaphores. Data moves between devices by JAX's collectives and lax.ppermute only.
A program may use at most 64 MiB of HBM per device.

v0:
```python
import jax
import jax.numpy as jnp
from jax import lax
from jax.sharding import PartitionSpec as P

ITERS = 2


decay_power = 1.5
decay_offset = 8.0


def kernel_rows(row_feat, col_feat):
    left = row_feat[:-1]
    right = col_feat[:-1]
    cross = jnp.dot(left.T, right, precision=lax.Precision.HIGHEST)
    dist = (
        jnp.sum(left * left, axis=0)[:, None]
        + jnp.sum(right * right, axis=0)[None, :]
        - 2.0 * cross
    )
    spread = row_feat[-1][:, None] + col_feat[-1][None, :] + decay_offset
    return jnp.exp(-0.5 * dist - decay_power * jnp.log(spread / decay_offset))


def apply_rows(vector, row_feat, col_feat):
    width = row_feat.shape[1]
    block = 512
    blocks = row_feat.reshape(row_feat.shape[0], width // block, block).transpose(1, 0, 2)

    def single(features):
        kernel_block = kernel_rows(features, col_feat)
        return jnp.einsum("cw,bw->cb", vector, kernel_block, precision=lax.Precision.HIGHEST)

    result = lax.map(single, blocks)
    return result.transpose(1, 0, 2).reshape(vector.shape[0], width)


def fetch_features(own_feat):
    count_row = lax.axis_size("row")
    count_col = lax.axis_size("col")
    width = own_feat.shape[1] * count_row // count_col
    column = lax.axis_index("col")
    whole = lax.all_gather(own_feat, "row", axis=1, tiled=True)
    return lax.dynamic_slice_in_dim(whole, column * width, width, 1)


def fetch_vector(vector):
    count_row = lax.axis_size("row")
    count_col = lax.axis_size("col")
    width = vector.shape[1] * count_row // count_col
    column = lax.axis_index("col")
    whole = lax.all_gather(vector, "row", axis=1, tiled=True)
    return lax.dynamic_slice_in_dim(whole, column * width, width, 1)


def on_device(right_side, noise_level, run_index, step_index, run_features):
    runs = jnp.take(run_features, run_index, axis=1)
    own_feat = jnp.concatenate([runs, step_index.astype(jnp.float32)[None, :]], axis=0)
    col_feat = fetch_features(own_feat)

    def squares(vector):
        return lax.psum(jnp.sum(vector * vector, axis=1), "row")

    solution_field = jnp.zeros_like(right_side)
    residual = right_side
    direction = right_side
    norm_now = squares(residual)
    for count in range(ITERS):
        col_vector = fetch_vector(direction)
        partial_rows = apply_rows(col_vector, own_feat, col_feat)
        image = lax.psum(partial_rows, "col") + noise_level[None, :] * direction
        step_size = norm_now / lax.psum(jnp.sum(direction * image, axis=1), "row")
        solution_field = solution_field + step_size[:, None] * direction
        residual = residual - step_size[:, None] * image
        norm_next = squares(residual)
        direction = residual + (norm_next / norm_now)[:, None] * direction
        norm_now = norm_next
    return (solution_field, residual)


def solution(mesh):
    return jax.shard_map(
        on_device,
        mesh=mesh,
        in_specs=(P(None, "row"), P("row"), P("row"), P("row"), P()),
        out_specs=(P(None, "row"), P(None, "row")),
        check_vma=False,
    )
```

profile of v0, /device:TPU:1, one launch (start us, length us, event | category | flops | bytes accessed | tf_op | source)
XLA Modules:
  0.0 865.2 jit_solution(5581979871890571595)
XLA Ops:
  8.0 7.6 copy.20
  15.5 12.7 %gather_fusion = f32[3072,16]{1,0:T(8,128)S(1)} fusion(f32[16,24576]{0,1:T(8,128)} %copy.20, s32[3072]{0:T(1024)S(1)} %fusion.71), kind=kCustom, calls=%fused_computation | custom fusion | bytes 405504 | tf_op jit(solution)/shard_map/jit(_take)/gather | solution.py:58
  28.3 1.6 bitcast_select_fusion
  31.6 60.4 %all-gather.6.cloned.1.call-done = f32[9,49152]{1,0:T(8,128)} async-done(((f32[9,3072]{1,0:T(8,128)}), f32[9,49152]{1,0:T(8,128)}) %all-gather.6.cloned.1.call-update) | async-done | bytes 1769488 | tf_op jit(solution)/shard_map/all_gather | solution.py:53
  92.0 0.9 constant_dynamic-slice_fusion.3
  93.0 111.2 %all-gather.4.cloned.1.call-done = f32[17,49152]{1,0:T(8,128)} async-done(((f32[17,3072]{1,0:T(8,128)}), f32[17,49152]{1,0:T(8,128)}) %all-gather.4.cloned.1.call-update) | async-done | bytes 3342352 | tf_op jit(solution)/shard_map/all_gather | solution.py:44
  204.2 1.0 constant_dynamic-slice_fusion.4
  205.2 1.0 fusion.70
  206.2 99.6 %while.24 = (s32[]{:T(128)}, f32[6,9,512]{2,1,0:T(8,128)S(1)}, f32[6,17,512]{2,1,0:T(8,128)S(1)}, f32[3072]{0:T(1024)S(1)}, f32[17,3072]{1,0:T(8,128)S(1)}, /*in...) while((s32[]{:T(128)}, f32[6,9,512]{2,1,0:T(8,128)S(1)}, f32[6,17,512]{2,1,0:T(8,128)S(1)}, ...), condition=%wide.region_5.6_spmd, body=%wide.region_3.5_spmd.sunk | while | flops 486030848 | bytes 13133949 | solution.py:35
  206.2 7.1 fusion.87
  213.3 9.5 %fusion.88 = f32[6,9,512]{2,1,0:T(8,128)S(1)} fusion(f32[6,9,512]{2,1,0:T(8,128)S(1)} %get-tuple-element.274, s32[]{:T(128)} %get-tuple-element.273, f32[9,3072]{1,0:T(8,128)S(1)} %get-tuple-element.287, f32[512,3072]{1,0:T(8,128)} %fusion.87, f32[3072]{0:T(1024)S(1)} %bitcast.75, f32[512]{0:T(512)S(1)} %bitcast.79, ...), kind=kOutput, calls=%fused_computation.23.clone.1 | convolution fusion | flops 184025088 | bytes 6549508 | tf_op jit(solution)/shard_map/while/body/eval_jaxpr/cw,bw->cb/dot_general | solution.py:33
  222.8 7.1 fusion.87
  229.9 9.5 %fusion.88 = f32[6,9,512]{2,1,0:T(8,128)S(1)} fusion(f32[6,9,512]{2,1,0:T(8,128)S(1)} %get-tuple-element.274, s32[]{:T(128)} %get-tuple-element.273, f32[9,3072]{1,0:T(8,128)S(1)} %get-tuple-element.287, f32[512,3072]{1,0:T(8,128)} %fusion.87, f32[3072]{0:T(1024)S(1)} %bitcast.75, f32[512]{0:T(512)S(1)} %bitcast.79, ...), kind=kOutput, calls=%fused_computation.23.clone.1 | convolution fusion | flops 184025088 | bytes 6549508 | tf_op jit(solution)/shard_map/while/body/eval_jaxpr/cw,bw->cb/dot_general | solution.py:33
  239.4 7.1 fusion.87
  246.5 9.5 %fusion.88 = f32[6,9,512]{2,1,0:T(8,128)S(1)} fusion(f32[6,9,512]{2,1,0:T(8,128)S(1)} %get-tuple-element.274, s32[]{:T(128)} %get-tuple-element.273, f32[9,3072]{1,0:T(8,128)S(1)} %get-tuple-element.287, f32[512,3072]{1,0:T(8,128)} %fusion.87, f32[3072]{0:T(1024)S(1)} %bitcast.75, f32[512]{0:T(512)S(1)} %bitcast.79, ...), kind=kOutput, calls=%fused_computation.23.clone.1 | convolution fusion | flops 184025088 | bytes 6549508 | tf_op jit(solution)/shard_map/while/body/eval_jaxpr/cw,bw->cb/dot_general | solution.py:33
  256.0 7.1 fusion.87
  263.1 9.5 %fusion.88 = f32[6,9,512]{2,1,0:T(8,128)S(1)} fusion(f32[6,9,512]{2,1,0:T(8,128)S(1)} %get-tuple-element.274, s32[]{:T(128)} %get-tuple-element.273, f32[9,3072]{1,0:T(8,128)S(1)} %get-tuple-element.287, f32[512,3072]{1,0:T(8,128)} %fusion.87, f32[3072]{0:T(1024)S(1)} %bitcast.75, f32[512]{0:T(512)S(1)} %bitcast.79, ...), kind=kOutput, calls=%fused_computation.23.clone.1 | convolution fusion | flops 184025088 | bytes 6549508 | tf_op jit(solution)/shard_map/while/body/eval_jaxpr/cw,bw->cb/dot_general | solution.py:33
  272.6 7.1 fusion.87
  279.7 9.5 %fusion.88 = f32[6,9,512]{2,1,0:T(8,128)S(1)} fusion(f32[6,9,512]{2,1,0:T(8,128)S(1)} %get-tuple-element.274, s32[]{:T(128)} %get-tuple-element.273, f32[9,3072]{1,0:T(8,128)S(1)} %get-tuple-element.287, f32[512,3072]{1,0:T(8,128)} %fusion.87, f32[3072]{0:T(1024)S(1)} %bitcast.75, f32[512]{0:T(512)S(1)} %bitcast.79, ...), kind=kOutput, calls=%fused_computation.23.clone.1 | convolution fusion | flops 184025088 | bytes 6549508 | tf_op jit(solution)/shard_map/while/body/eval_jaxpr/cw,bw->cb/dot_general | solution.py:33
  289.2 7.1 fusion.87
  296.3 9.5 %fusion.88 = f32[6,9,512]{2,1,0:T(8,128)S(1)} fusion(f32[6,9,512]{2,1,0:T(8,128)S(1)} %get-tuple-element.274, s32[]{:T(128)} %get-tuple-element.273, f32[9,3072]{1,0:T(8,128)S(1)} %get-tuple-element.287, f32[512,3072]{1,0:T(8,128)} %fusion.87, f32[3072]{0:T(1024)S(1)} %bitcast.75, f32[512]{0:T(512)S(1)} %bitcast.79, ...), kind=kOutput, calls=%fused_computation.23.clone.1 | convolution fusion | flops 184025088 | bytes 6549508 | tf_op jit(solution)/shard_map/while/body/eval_jaxpr/cw,bw->cb/dot_general | solution.py:33
  305.9 0.8 copy.25
  306.8 137.7 %all-reduce.4.cloned.1.call-done = f32[9,3072]{1,0:T(8,128)} async-done(((f32[9,3072]{1,0:T(8,128)}), f32[9,3072]{1,0:T(8,128)}) %all-reduce.4.cloned.1.call-update) | async-done | bytes 110608 | tf_op jit(solution)/shard_map/psum | solution.py:72
  444.5 1.1 multiply_reduce_fusion.4
  445.6 27.1 %all-reduce = (f32[9]{0:T(128)S(1)}, f32[9]{0:T(128)S(1)}) all-reduce(f32[9]{0:T(128)S(1)} %get-tuple-element.161, f32[9]{0:T(128)S(1)} %get-tuple-element.160), channel_id=1, replica_groups=mesh['row'=16,'col'=16] {'row'}, use_global_device_ids=true, to_apply=%region_1.2 | all-reduce | flops 18 | bytes 144 | tf_op jit(solution)/shard_map/psum | solution.py:63
  472.7 1.1 multiply_reduce_fusion.3
  473.8 23.9 %psum.45 = f32[9]{0:T(128)S(1)} all-reduce(f32[9]{0:T(128)S(1)} %multiply_reduce_fusion.3), channel_id=1, replica_groups=mesh['row'=16,'col'=16] {'row'}, use_global_device_ids=true, to_apply=%region_10.11 | all-reduce | flops 9 | bytes 72 | tf_op jit(solution)/shard_map/psum | solution.py:63
  497.7 1.7 multiply_add_fusion.2
  499.7 89.4 %all-gather.8.cloned.1.call-done = f32[9,49152]{1,0:T(8,128)} async-done(((f32[9,3072]{1,0:T(8,128)}), f32[9,49152]{1,0:T(8,128)}) %all-gather.8.cloned.1.call-update) | async-done | bytes 1769488 | tf_op jit(solution)/shard_map/all_gather | solution.py:53
  589.1 0.9 constant_dynamic-slice_fusion.2
  590.1 99.6 %while.25 = (s32[]{:T(128)}, f32[6,9,512]{2,1,0:T(8,128)S(1)}, f32[6,17,512]{2,1,0:T(8,128)S(1)}, f32[3072]{0:T(1024)S(1)}, f32[17,3072]{1,0:T(8,128)S(1)}, /*in...) while((s32[]{:T(128)}, f32[6,9,512]{2,1,0:T(8,128)S(1)}, f32[6,17,512]{2,1,0:T(8,128)S(1)}, ...), condition=%wide.region_13.14_spmd, body=%wide.region_11.13_spmd.sunk | while | flops 486030848 | bytes 13133949 | solution.py:35
  590.1 7.1 fusion.92
  597.2 9.5 %fusion.93 = f32[6,9,512]{2,1,0:T(8,128)S(1)} fusion(f32[6,9,512]{2,1,0:T(8,128)S(1)} %get-tuple-element.301, s32[]{:T(128)} %get-tuple-element.300, f32[9,3072]{1,0:T(8,128)S(1)} %get-tuple-element.314, f32[512,3072]{1,0:T(8,128)} %fusion.92, f32[3072]{0:T(1024)S(1)} %bitcast.76, f32[512]{0:T(512)S(1)} %bitcast.80, ...), kind=kOutput, calls=%fused_computation.57.clone.1 | convolution fusion | flops 184025088 | bytes 6549508 | tf_op jit(solution)/shard_map/while/body/eval_jaxpr/cw,bw->cb/dot_general | solution.py:33
  606.7 7.1 fusion.92
  613.8 9.5 %fusion.93 = f32[6,9,512]{2,1,0:T(8,128)S(1)} fusion(f32[6,9,512]{2,1,0:T(8,128)S(1)} %get-tuple-element.301, s32[]{:T(128)} %get-tuple-element.300, f32[9,3072]{1,0:T(8,128)S(1)} %get-tuple-element.314, f32[512,3072]{1,0:T(8,128)} %fusion.92, f32[3072]{0:T(1024)S(1)} %bitcast.76, f32[512]{0:T(512)S(1)} %bitcast.80, ...), kind=kOutput, calls=%fused_computation.57.clone.1 | convolution fusion | flops 184025088 | bytes 6549508 | tf_op jit(solution)/shard_map/while/body/eval_jaxpr/cw,bw->cb/dot_general | solution.py:33
  623.4 7.1 fusion.92
  630.4 9.5 %fusion.93 = f32[6,9,512]{2,1,0:T(8,128)S(1)} fusion(f32[6,9,512]{2,1,0:T(8,128)S(1)} %get-tuple-element.301, s32[]{:T(128)} %get-tuple-element.300, f32[9,3072]{1,0:T(8,128)S(1)} %get-tuple-element.314, f32[512,3072]{1,0:T(8,128)} %fusion.92, f32[3072]{0:T(1024)S(1)} %bitcast.76, f32[512]{0:T(512)S(1)} %bitcast.80, ...), kind=kOutput, calls=%fused_computation.57.clone.1 | convolution fusion | flops 184025088 | bytes 6549508 | tf_op jit(solution)/shard_map/while/body/eval_jaxpr/cw,bw->cb/dot_general | solution.py:33
  639.9 7.1 fusion.92
  647.0 9.5 %fusion.93 = f32[6,9,512]{2,1,0:T(8,128)S(1)} fusion(f32[6,9,512]{2,1,0:T(8,128)S(1)} %get-tuple-element.301, s32[]{:T(128)} %get-tuple-element.300, f32[9,3072]{1,0:T(8,128)S(1)} %get-tuple-element.314, f32[512,3072]{1,0:T(8,128)} %fusion.92, f32[3072]{0:T(1024)S(1)} %bitcast.76, f32[512]{0:T(512)S(1)} %bitcast.80, ...), kind=kOutput, calls=%fused_computation.57.clone.1 | convolution fusion | flops 184025088 | bytes 6549508 | tf_op jit(solution)/shard_map/while/body/eval_jaxpr/cw,bw->cb/dot_general | solution.py:33
  656.5 7.1 fusion.92
  663.6 9.5 %fusion.93 = f32[6,9,512]{2,1,0:T(8,128)S(1)} fusion(f32[6,9,512]{2,1,0:T(8,128)S(1)} %get-tuple-element.301, s32[]{:T(128)} %get-tuple-element.300, f32[9,3072]{1,0:T(8,128)S(1)} %get-tuple-element.314, f32[512,3072]{1,0:T(8,128)} %fusion.92, f32[3072]{0:T(1024)S(1)} %bitcast.76, f32[512]{0:T(512)S(1)} %bitcast.80, ...), kind=kOutput, calls=%fused_computation.57.clone.1 | convolution fusion | flops 184025088 | bytes 6549508 | tf_op jit(solution)/shard_map/while/body/eval_jaxpr/cw,bw->cb/dot_general | solution.py:33
  673.1 7.1 fusion.92
  680.3 9.5 %fusion.93 = f32[6,9,512]{2,1,0:T(8,128)S(1)} fusion(f32[6,9,512]{2,1,0:T(8,128)S(1)} %get-tuple-element.301, s32[]{:T(128)} %get-tuple-element.300, f32[9,3072]{1,0:T(8,128)S(1)} %get-tuple-element.314, f32[512,3072]{1,0:T(8,128)} %fusion.92, f32[3072]{0:T(1024)S(1)} %bitcast.76, f32[512]{0:T(512)S(1)} %bitcast.80, ...), kind=kOutput, calls=%fused_computation.57.clone.1 | convolution fusion | flops 184025088 | bytes 6549508 | tf_op jit(solution)/shard_map/while/body/eval_jaxpr/cw,bw->cb/dot_general | solution.py:33
  689.9 0.8 copy.26
  690.7 138.0 %all-reduce.6.cloned.1.call-done = f32[9,3072]{1,0:T(8,128)} async-done(((f32[9,3072]{1,0:T(8,128)}), f32[9,3072]{1,0:T(8,128)}) %all-reduce.6.cloned.1.call-update) | async-done | bytes 110608 | tf_op jit(solution)/shard_map/psum | solution.py:72
  828.7 1.1 multiply_reduce_fusion.2
  829.8 27.1 %psum.47 = f32[9]{0:T(128)S(1)} all-reduce(f32[9]{0:T(128)S(1)} %multiply_reduce_fusion.2), channel_id=1, replica_groups=mesh['row'=16,'col'=16] {'row'}, use_global_device_ids=true, to_apply=%region_16.17 | all-reduce | flops 9 | bytes 72 | tf_op jit(solution)/shard_map/psum | solution.py:73
  856.9 1.8 multiply_subtract_fusion
  (76 shorter events, 3.5 us)
Async XLA Ops:
  7.2 84.9 %all-gather.6.cloned.1.call-start = ((), (), s32[]{:S(2)}) async-start(), calls=%async_computation.1 | async-start | bytes 3342336 | tf_op jit(solution)/shard_map/all_gather | solution.py:53
  7.9 7.6 copy-start.4
  7.9 196.3 %all-gather.4.cloned.1.call-start = ((), (), s32[]{:S(2)}) async-start(), calls=%async_computation | async-start | bytes 5013504 | tf_op jit(solution)/shard_map/all_gather | solution.py:44
  15.5 14.8 %copy-start.5 = (s32[3072]{0:T(1024)S(1)}, s32[3072]{0:T(1024)}, u32[]{:S(2)}) copy-start(s32[3072]{0:T(1024)} %param.12) | copy-start | bytes 36868
  31.1 413.4 %all-reduce.4.cloned.1.call-start = ((), (), s32[]{:S(2)}) async-start(), calls=%async_computation.2 | async-start | bytes 393216 | tf_op jit(solution)/shard_map/psum | solution.py:72
  206.2 238.3 %copy-start = (f32[9,3072]{1,0:T(8,128)S(1)}, f32[9,3072]{1,0:T(8,128)}, u32[]{:S(2)}) copy-start(f32[9,3072]{1,0:T(8,128)} %param.9) | copy-start | bytes 331780
  206.2 238.3 %copy-start.3 = (f32[3072]{0:T(1024)S(1)}, f32[3072]{0:T(1024)}, u32[]{:S(2)}) copy-start(f32[3072]{0:T(1024)} %param.10) | copy-start | bytes 36868
  306.7 282.4 %all-gather.8.cloned.1.call-start = ((), (), s32[]{:S(2)}) async-start(), calls=%async_computation.3 | async-start | bytes 3342336 | tf_op jit(solution)/shard_map/all_gather | solution.py:53
  499.5 329.2 %all-reduce.6.cloned.1.call-start = ((), (), s32[]{:S(2)}) async-start(), calls=%async_computation.4 | async-start | bytes 393216 | tf_op jit(solution)/shard_map/psum | solution.py:72
  590.1 238.6 %copy-start.2 = (f32[9,3072]{1,0:T(8,128)S(1)}, f32[9,3072]{1,0:T(8,128)}, u32[]{:S(2)}) copy-start(f32[9,3072]{1,0:T(8,128)} %multiply_add_fusion.2) | copy-start | bytes 331780
  590.1 266.8 %copy-start.1 = (f32[9,3072]{1,0:T(8,128)S(1)}, f32[9,3072]{1,0:T(8,128)}, u32[]{:S(2)}) copy-start(f32[9,3072]{1,0:T(8,128)} %all-reduce.4.cloned.1.call-done) | copy-start | bytes 331780
Sparse Core Ops, SparseCore 0:
  9.8 82.2 all-gather.5
  93.8 110.3 all-gather.3
  306.9 137.5 all-reduce.3
  499.6 89.5 all-gather.7
  690.8 137.8 all-reduce.5
where the time goes:
time: 872 us; the launch traced here: 865 us
  waiting for transfers between devices  537 us (62%)
  matrix products  199 us (23%)
  blocking collectives  78.1 us (9%)
  local copies, waits for them, and re-layouts  25.9 us (3%)
  between operations  14 us (2%)
  other arithmetic  10.5 us (1%)
    psum x2, waiting for transfers between devices, on_device(): image = lax.psum(partial_rows, 'col') + noise_level[None, :] * direction  276 us
    all_gather x2, waiting for transfers between devices, fetch_vector(): whole = lax.all_gather(vector, 'row', axis=1, tiled=True)  150 us
    dot_general x12, matrix products, single(): jnp.einsum('cw,bw->cb', vector, kernel_block, precision=lax.Precision.HIG...  114 us
    all_gather x1, waiting for transfers between devices, fetch_features(): whole = lax.all_gather(own_feat, 'row', axis=1, tiled=True)  111 us
    dot_general x12, matrix products, kernel_rows(): cross = jnp.dot(left.T, right, precision=lax.Precision.HIGHEST)  84.7 us
    psum x2, blocking collectives, squares(): return lax.psum(jnp.sum(vector * vector, axis=1), 'row')  51 us
    psum x1, blocking collectives, on_device(): step_size = norm_now / lax.psum(jnp.sum(direction * image, axis=1), 'row')  27.1 us
  transfers between devices with their start and end apart: 5, of which 5 were waited for; matrix products, arithmetic and copies ran while one was open for 3% of the time, Pallas kernels for 0%

commit v1 on v0

v1 whole, which is shorter than its diff:
```python
import functools
import math

import jax
import jax.numpy as jnp
from jax import lax
from jax.experimental import pallas as pl
from jax.experimental.pallas import tpu as pltpu
from jax.sharding import PartitionSpec as P

LANES = 128
SIDE = 16
FEAT = 16
PROBES = 9
ROWS = 16
MORE = 24
DEPTH = 128
LOG2E = 1.4426950408889634
F32 = jnp.float32
BF16 = jnp.bfloat16
VMEM = pltpu.VMEM
MIB = 1024 * 1024


def vspec():
    return pl.BlockSpec(memory_space=VMEM)


def sspec():
    return pl.BlockSpec(memory_space=pltpu.SMEM)


def params(mib=14):
    return pltpu.CompilerParams(vmem_limit_bytes=mib * MIB)


def gather_body(idx_ref, tab_ref, out_ref):
    lane = lax.broadcasted_iota(jnp.int32, (FEAT, LANES), 1)

    def group(g, _):
        base = pl.multiple_of(g * LANES, LANES)
        acc = jnp.zeros((FEAT, LANES), F32)
        for p in range(LANES):
            run = idx_ref[base + p]
            start = pl.multiple_of((run >> 7) * LANES, LANES)
            tile = tab_ref[:, pl.ds(start, LANES)]
            tile = pltpu.roll(tile, (p + LANES) - (run & (LANES - 1)), 1)
            acc = jnp.where(lane == p, tile, acc)
        out_ref[:, pl.ds(base, LANES)] = acc
        return 0

    lax.fori_loop(0, out_ref.shape[1] // LANES, group, 0)


def gather(idx, table):
    n = idx.shape[0]
    return pl.pallas_call(
        gather_body,
        out_shape=jax.ShapeDtypeStruct((FEAT, n), F32),
        in_specs=[sspec(), vspec()],
        out_specs=vspec(),
        compiler_params=params(),
        cost_estimate=pl.CostEstimate(flops=n * 4000, bytes_accessed=4 * table.size, transcendentals=0),
        name="gather",
    )(idx, table)


def thirds(x):
    a = x.astype(BF16).astype(F32)
    b = (x - a).astype(BF16).astype(F32)
    return a, b, x - a - b


def to_lanes(column, first):
    lane = lax.broadcasted_iota(jnp.int32, (PROBES, LANES), 1)
    sub = lax.broadcasted_iota(jnp.int32, (PROBES, LANES), 0)
    return jnp.sum(jnp.where(lane == sub + first, column, 0.0), axis=0, keepdims=True)


def to_column(row, first):
    lane = lax.broadcasted_iota(jnp.int32, (PROBES, LANES), 1)
    sub = lax.broadcasted_iota(jnp.int32, (PROBES, LANES), 0)
    return jnp.sum(jnp.where(lane == sub + first, row, 0.0), axis=1, keepdims=True)


def unpack(v_ref, nat, tiles):
    for t in range(tiles):
        lanes = slice(t * LANES, (t + 1) * LANES)
        nat[0:8, lanes] = v_ref[t // 2, 8 * (t % 2) : 8 * (t % 2) + 8, :]
        m = 8 * tiles + t
        nat[8:9, lanes] = v_ref[m // ROWS, m % ROWS : m % ROWS + 1, :]


def pack_tile(out_ref, res, tile, tiles):
    out_ref[tile // 2, pl.ds(pl.multiple_of(8 * (tile % 2), 8), 8), :] = res[0:8]
    m = 8 * tiles + tile
    out_ref[m // ROWS, pl.ds(m % ROWS, 1), :] = res[8:9]


def clear_rest(out_ref, tiles):
    m = 9 * tiles
    out_ref[m // ROWS, m % ROWS : ROWS, :] = jnp.zeros((ROWS - m % ROWS, LANES), F32)
    for s in range(m // ROWS + 1, SIDE):
        out_ref[s, 0:ROWS, :] = jnp.zeros((ROWS, LANES), F32)


def build_body(lf_ref, ls_ref, rf_ref, rs_ref, b_ref, bj_ref, noise_ref, flag_ref, khi_ref, klo_ref, out_ref,
               left, right, vec, acc, steps, scal, *, pt, qt):
    n = lf_ref.shape[1]
    m = rf_ref.shape[1]
    tiles = m // LANES
    ch = 512

    def operand(features, is_left):
        f = features * math.sqrt(LOG2E)
        a, b, c = thirds(f)
        norm = -0.5 * jnp.sum(f * f, axis=0, keepdims=True)
        if is_left:
            norm = norm + 1.5 * math.log2(8.0)
        na, nb, nc = thirds(norm)
        one = jnp.ones_like(norm)
        if is_left:
            parts = [a, a, b, b, a, c, na, nb, nc, one, one, one]
        else:
            parts = [a, b, a, b, c, a, one, one, one, na, nb, nc]
        pad = jnp.zeros((DEPTH - 6 * FEAT - 6, f.shape[1]), F32)
        return jnp.concatenate(parts + [pad], axis=0)

    def prepare(t, _):
        o = pl.ds(pl.multiple_of(t * ch, ch), ch)
        left[o, :] = jnp.transpose(operand(lf_ref[:, o], True)).astype(BF16)
        step = ls_ref[:, o].astype(F32) + 8.0
        steps[o, :] = jnp.transpose(jnp.broadcast_to(step, (LANES, ch)))
        right[:, o] = operand(rf_ref[:, o], False).astype(BF16)
        v = b_ref[:, o]
        high = v.astype(BF16).astype(F32)
        zero = jnp.zeros((ROWS - PROBES, ch), F32)
        vec[:, o] = jnp.concatenate([high, zero, v - high, zero], axis=0).astype(BF16)
        return 0

    lax.fori_loop(0, n // ch, prepare, 0)
    scal[...] = jnp.zeros_like(scal)

    def column(jq, _):
        oq = pl.ds(pl.multiple_of(jq * qt, qt), qt)
        right_tile = right[:, oq]
        right_step = rs_ref[:, oq].astype(F32)
        acc[...] = jnp.zeros_like(acc)

        def row(ip, _):
            op = pl.ds(pl.multiple_of(ip * pt, pt), pt)
            power = jnp.dot(left[op, :], right_tile, preferred_element_type=F32)
            spread = jnp.concatenate([steps[op, :]] * (qt // LANES), axis=1) + right_step
            root = lax.rsqrt(spread)
            k = jnp.exp2(power) * (root * (root * root))
            high = k.astype(BF16)
            low = (k - high.astype(F32)).astype(BF16)
            khi_ref[op, oq] = high
            klo_ref[op, oq] = low
            v = vec[:, op]
            y = jnp.dot(v, high, preferred_element_type=F32)
            z = jnp.dot(v[0:ROWS], low, preferred_element_type=F32)
            acc[...] += y[0:ROWS] + y[ROWS:] + z
            return 0

        lax.fori_loop(0, n // pt, row, 0, unroll=n // pt)
        res = acc[0:PROBES, :] + flag_ref[0] * (noise_ref[:, oq] * b_ref[:, oq])
        bj = bj_ref[:, oq]
        scal[0:PROBES, 0:1] += jnp.sum(res * bj, axis=1, keepdims=True)
        scal[0:PROBES, 1:2] += jnp.sum(bj * bj, axis=1, keepdims=True)
        for t in range(qt // LANES):
            pack_tile(out_ref, res[:, t * LANES : (t + 1) * LANES], jq * (qt // LANES) + t, tiles)
        return 0

    clear_rest(out_ref, tiles)
    lax.fori_loop(0, m // qt, column, 0)
    line = to_lanes(scal[0:PROBES, 0:1], 0) + to_lanes(scal[0:PROBES, 1:2] * (1.0 / SIDE), 16)
    for s in range(SIDE):
        out_ref[s, ROWS:MORE, :] = jnp.broadcast_to(line, (MORE - ROWS, LANES))


def build(lf, ls, rf, rs, b, bj, noise, flag, pt=512, qt=1024):
    n, m = lf.shape[1], rf.shape[1]
    half = VMEM((n, m), BF16)
    return pl.pallas_call(
        functools.partial(build_body, pt=pt, qt=qt),
        out_shape=(half, half, jax.ShapeDtypeStruct((SIDE, MORE, LANES), F32)),
        in_specs=[vspec()] * 7 + [sspec()],
        out_specs=(vspec(), vspec(), vspec()),
        scratch_shapes=[
            VMEM((n, DEPTH), BF16),
            VMEM((DEPTH, m), BF16),
            VMEM((2 * ROWS, n), BF16),
            VMEM((ROWS, qt), F32),
            VMEM((n, LANES), F32),
            VMEM((ROWS, LANES), F32),
        ],
        compiler_params=params(),
        cost_estimate=pl.CostEstimate(flops=n * m * 1000, bytes_accessed=n * m * 4, transcendentals=2 * n * m),
        name="build",
    )(lf, ls.reshape(1, n), rf, rs.reshape(1, m), b, bj, noise.reshape(1, n), flag)


def apply_body(khi_ref, klo_ref, w_ref, noise_ref, flag_ref, out_ref, nat, vec, *, pt):
    n, m = khi_ref.shape
    tiles = m // LANES
    unpack(w_ref, nat, tiles)
    w = nat[0:PROBES, :]
    high = w.astype(BF16).astype(F32)
    zero = jnp.zeros((ROWS - PROBES, m), F32)
    vec[...] = jnp.concatenate([high, zero, w - high, zero], axis=0).astype(BF16)
    clear_rest(out_ref, n // LANES)
    dims = (((1,), (1,)), ((), ()))

    def row(ip, _):
        op = pl.ds(pl.multiple_of(ip * pt, pt), pt)
        y = lax.dot_general(vec[...], khi_ref[op, :], dims, preferred_element_type=F32)
        z = lax.dot_general(vec[0:ROWS, :], klo_ref[op, :], dims, preferred_element_type=F32)
        res = (y[0:ROWS] + y[ROWS:] + z)[0:PROBES]
        res = res + flag_ref[0] * (noise_ref[:, op] * nat[0:PROBES, op])
        for t in range(pt // LANES):
            pack_tile(out_ref, res[:, t * LANES : (t + 1) * LANES], ip * (pt // LANES) + t, n // LANES)
        return 0

    lax.fori_loop(0, n // pt, row, 0)


def apply(khi, klo, w, noise, flag, pt=512):
    n, m = khi.shape
    khi = pltpu.with_memory_space_constraint(khi, VMEM)
    klo = pltpu.with_memory_space_constraint(klo, VMEM)
    return pl.pallas_call(
        functools.partial(apply_body, pt=pt),
        out_shape=jax.ShapeDtypeStruct((SIDE, ROWS, LANES), F32),
        in_specs=[vspec()] * 4 + [sspec()],
        out_specs=vspec(),
        scratch_shapes=[VMEM((ROWS, m), F32), VMEM((2 * ROWS, m), BF16)],
        compiler_params=params(),
        cost_estimate=pl.CostEstimate(flops=n * m * 600, bytes_accessed=n * m * 4, transcendentals=0),
        name="apply",
    )(khi, klo, w, noise.reshape(1, n), flag)


def first_sum_body(in_ref, chunk_ref, line_ref):
    total = jnp.sum(in_ref[...], axis=0)
    for s in range(SIDE):
        chunk_ref[s] = total[0:ROWS]
        line_ref[s] = total[ROWS:MORE]


def first_sum(got):
    return pl.pallas_call(
        first_sum_body,
        out_shape=(
            jax.ShapeDtypeStruct((SIDE, ROWS, LANES), F32),
            jax.ShapeDtypeStruct((SIDE, MORE - ROWS, LANES), F32),
        ),
        in_specs=[vspec()],
        out_specs=(vspec(), vspec()),
        compiler_params=params(),
        name="first_sum",
    )(got)


def second_sum_body(in_ref, line_ref, out_ref):
    total = jnp.sum(in_ref[...], axis=0)
    line = jnp.sum(line_ref[...], axis=0)
    for s in range(SIDE):
        out_ref[s, 0:ROWS, :] = total
        out_ref[s, ROWS:MORE, :] = line


def second_sum(got, line):
    return pl.pallas_call(
        second_sum_body,
        out_shape=jax.ShapeDtypeStruct((SIDE, MORE, LANES), F32),
        in_specs=[vspec(), vspec()],
        out_specs=vspec(),
        compiler_params=params(),
        name="second_sum",
    )(got, line)


def scalar_body(b_ref, w_ref, z_ref, line_ref, out_ref, nw, nz):
    tiles = b_ref.shape[1] // LANES
    unpack(w_ref, nw, tiles)
    unpack(z_ref, nz, tiles)
    line = jnp.sum(line_ref[...], axis=0)[0:1]
    bw, bb = to_column(line, 0), to_column(line, 16)
    w = nw[0:PROBES, :]
    r = b_ref[...] - (bb / bw) * w
    rr = jnp.sum(r * r, axis=1, keepdims=True)
    rw = jnp.sum(r * w, axis=1, keepdims=True)
    rz = jnp.sum(r * nz[0:PROBES, :], axis=1, keepdims=True)
    out = to_lanes(rr * (1.0 / SIDE), 0) + to_lanes(rw * (1.0 / SIDE), 16) + to_lanes(rz, 32)
    for s in range(SIDE):
        out_ref[s] = jnp.broadcast_to(out, (MORE - ROWS, LANES))


def scalars(b, w, z, line):
    n = b.shape[1]
    return pl.pallas_call(
        scalar_body,
        out_shape=jax.ShapeDtypeStruct((SIDE, MORE - ROWS, LANES), F32),
        in_specs=[vspec()] * 4,
        out_specs=vspec(),
        scratch_shapes=[VMEM((ROWS, n), F32), VMEM((ROWS, n), F32)],
        compiler_params=params(),
        name="scalars",
    )(b, w, z, line)


def finish_body(b_ref, w_ref, a_ref, line_ref, x_ref, r_ref, nw, na):
    tiles = b_ref.shape[1] // LANES
    unpack(w_ref, nw, tiles)
    unpack(a_ref, na, tiles)
    line = jnp.sum(line_ref[...], axis=0)[0:1]
    bw, bb = to_column(line, 0), to_column(line, 16)
    more = jnp.sum(a_ref[:, ROWS:MORE, :], axis=0)[0:1]
    rr, rw, ra = to_column(more, 0), to_column(more, 16), to_column(more, 32)
    first = bb / bw
    beta = rr / bb
    second = rr / ((rw - first * ra) + 2.0 * beta * rw + beta * beta * bw)
    b = b_ref[...]
    w = nw[0:PROBES, :]
    r = b - first * w
    x_ref[...] = first * b + second * (r + beta * b)
    r_ref[...] = r - second * ((w - first * na[0:PROBES, :]) + beta * w)


def finish(b, w, a, line):
    n = b.shape[1]
    out = jax.ShapeDtypeStruct((PROBES, n), F32)
    return pl.pallas_call(
        finish_body,
        out_shape=(out, out),
        in_specs=[vspec()] * 4,
        out_specs=(vspec(), vspec()),
        scratch_shapes=[VMEM((ROWS, n), F32), VMEM((ROWS, n), F32)],
        compiler_params=params(),
        name="finish",
    )(b, w, a, line)


def on_device(right_side, noise_level, run_index, step_index, run_features):
    swap = [(i * SIDE + j, j * SIDE + i) for i in range(SIDE) for j in range(SIDE)]

    def swapped(x):
        return lax.ppermute(x, ("row", "col"), swap)

    def exchange(x, axis):
        return lax.all_to_all(x, axis, 0, 0)

    flag = (lax.axis_index("row") == lax.axis_index("col")).astype(F32).reshape(1)
    other = swapped(jnp.stack([run_index, step_index]))
    other_side = swapped(right_side)
    own_feat = gather(run_index, run_features)
    col_feat = gather(other[0], run_features)
    khi, klo, part = build(own_feat, step_index, col_feat, other[1], right_side, other_side, noise_level, flag)
    chunk, line = first_sum(exchange(part, "row"))
    product = exchange(chunk, "row")
    line = exchange(line, "col")
    own_product = swapped(product)
    part = apply(khi, klo, product, noise_level, flag)
    more = exchange(scalars(right_side, own_product, part, line), "row")
    again = exchange(second_sum(exchange(part, "col"), more), "col")
    return finish(right_side, own_product, again, line)


def solution(mesh):
    return jax.shard_map(
        on_device,
        mesh=mesh,
        in_specs=(P(None, "row"), P("row"), P("row"), P("row"), P()),
        out_specs=(P(None, "row"), P(None, "row")),
        check_vma=False,
    )
```

time: 872 us -> 183 us (0.21)
  waiting for transfers between devices: 537 us -> 6.46 us
  matrix products: 199 us -> 0 us
  Pallas kernels: 0 us -> 54.5 us
  starting transfers between devices: 0.38 us -> 23.6 us
  blocking collectives: 78.1 us -> 64.7 us
  between operations: 14 us -> 0.78 us
  other arithmetic: 10.5 us -> 0.75 us
    psum x2 -> x0, waiting for transfers between devices: 276 us -> none  [on_device(): image = lax.psum(partial_rows, 'col') + noise_level[None, :] * direction]
    all_gather x3 -> x0, waiting for transfers between devices: 261 us -> none  [the longest x2 150 us: fetch_vector(): whole = lax.all_gather(vector, 'row', axis=1, tiled=True)]
    dot_general x24 -> x0, matrix products: 199 us -> none  [the longest x12 114 us: single(): jnp.einsum('cw,bw->cb', vector, kernel_block, precision=lax.Precision.HIG...]
    psum x3 -> x0, blocking collectives: 78.1 us -> none  [the longest x2 51 us: squares(): return lax.psum(jnp.sum(vector * vector, axis=1), 'row')]
    all_to_all x0 -> x4, blocking collectives: none -> 64.7 us  [exchange(): return lax.all_to_all(x, axis, 0, 0)]
    pallas_call x0 -> x8, Pallas kernels: none -> 54.5 us  [the longest x2 21.1 us: gather(): pl.pallas_call(gather_body, out_shape=jax.ShapeDtypeStruct((FEAT, n), F32...]
    unnamed x17 -> x24, local copies, waits for them, and re-layouts: 9.23 us -> 31.5 us
    all_to_all x0 -> x2, starting transfers between devices: none -> 15.3 us  [exchange(): return lax.all_to_all(x, axis, 0, 0)]
  transfers between devices with their start and end apart: 5 -> 5, of which waited for: 5 -> 1; matrix products, arithmetic and copies ran while one was open for 3% -> 0% of each run, Pallas kernels for 0% -> 19%
where the time goes in v1:
time: 183 us; the launch traced here: 182 us
  blocking collectives  64.7 us (35%)
  Pallas kernels  54.5 us (30%)
  local copies, waits for them, and re-layouts  31.5 us (17%)
  starting transfers between devices  23.6 us (13%)
  waiting for transfers between devices  6.46 us (4%)
    all_to_all x4, blocking collectives, exchange(): return lax.all_to_all(x, axis, 0, 0)  64.7 us
    unnamed x24, local copies, waits for them, and re-layouts  31.5 us
    pallas_call x2, Pallas kernels, gather(): pl.pallas_call(gather_body, out_shape=jax.ShapeDtypeStruct((FEAT, n), F32...  21.1 us
    pallas_call x1, Pallas kernels, build(): pl.pallas_call(functools.partial(build_body, pt=pt, qt=qt), out_shape=(ha...  19.1 us
    all_to_all x2, starting transfers between devices, exchange(): return lax.all_to_all(x, axis, 0, 0)  15.3 us
    pallas_call x1, Pallas kernels, apply(): pl.pallas_call(functools.partial(apply_body, pt=pt), out_shape=jax.ShapeD...  11.6 us
    ppermute x3, starting transfers between devices, swapped(): return lax.ppermute(x, ('row', 'col'), swap)  8.34 us
    all_to_all x2, waiting for transfers between devices, exchange(): return lax.all_to_all(x, axis, 0, 0)  6.46 us
  transfers between devices with their start and end apart: 5, of which 1 were waited for; matrix products, arithmetic and copies ran while one was open for 0% of the time, Pallas kernels for 19%

profile of v1, /device:TPU:1, one launch (start us, length us, event | category | flops | bytes accessed | tf_op | source)
XLA Modules:
  0.0 182.4 jit_solution(16387707140524195012)
XLA Ops:
  0.6 0.7 pad_add_fusion
  1.4 4.5 %collective-permute-start = (s32[2,3072]{1,0:T(2,128)S(1)}, s32[2,3072]{1,0:T(2,128)S(1)}, u32[]{:S(2)}, u32[]{:S(2)}) collective-permute-start(s32[2,3072]{1,0:T(2,128)S(1)} %pad_add_fusion), channel_id=1, source_target_pairs={{0,0},{1,16},{2,32},{3,48},{4,64},{5,80},{6,96},{7,112},{8,128},{9... | collective-permute-start | bytes 73736 | tf_op jit(solution)/shard_map/ppermute | solution.py:349
  5.9 1.9 %collective-permute-start.1 = (f32[9,3072]{1,0:T(8,128)}, f32[9,3072]{1,0:T(8,128)S(1)}, u32[]{:S(2)}, u32[]{:S(2)}) collective-permute-start(f32[9,3072]{1,0:T(8,128)} %b_ref.5), channel_id=1, source_target_pairs={{0,0},{1,16},{2,32},{3,48},{4,64},{5,80},{6,96},{7,112},{8,128},{9... | collective-permute-start | bytes 331784 | tf_op jit(solution)/shard_map/ppermute | solution.py:349
  7.8 0.0 copy-start.4
  7.8 1.4 copy-done.4
  9.2 0.0 copy-start.8
  9.2 0.7 copy-done.8
  10.0 10.5 %gather.2.lf_ref = f32[16,3072]{1,0:T(8,128)S(1)} custom-call(s32[3072]{0:T(1024)S(1)} %copy-done.8, f32[16,24576]{1,0:T(8,128)S(1)} %copy-done.4), custom_call_target="tpu_custom_call" | custom-call | flops 12288000 | bytes 1572864 | tf_op jit(solution)/shard_map/gather/pallas_call | solution.py:57
  20.5 0.0 collective-permute-done
  20.5 0.0 copy-start.5
  20.5 1.4 copy-done.5
  21.9 0.0 copy-start.10
  21.9 10.5 %gather.3.rf_ref = f32[16,3072]{1,0:T(8,128)S(1)} custom-call(s32[3072]{0:T(1024)S(1)} %bitcast.6, f32[16,24576]{1,0:T(8,128)S(1)} %copy-done.5), custom_call_target="tpu_custom_call" | custom-call | flops 12288000 | bytes 1572864 | tf_op jit(solution)/shard_map/gather/pallas_call | solution.py:57
  32.5 0.0 collective-permute-done.1.bj_ref
  32.5 0.0 copy-start.6
  32.5 0.9 copy-done.6
  33.4 0.0 copy-start.9
  33.4 0.7 copy-done.9
  34.1 0.0 copy-start.11
  34.1 0.7 copy-done.11
  34.8 19.1 %build.1 = (bf16[3072,3072]{1,0:T(8,128)(2,1)S(1)}, bf16[3072,3072]{1,0:T(8,128)(2,1)S(1)}, f32[16,24,128]{2,1,0:T(8,128)S(1)}) custom-call(f32[16,3072]{1,0:T(8,128)S(1)} %gather.2.lf_ref, s32[1,3072]{1,0:T(1,128)S(1)} %bitcast.10, f32[16,3072]{1,0:T(8,128)S(1)} %gather.3.rf_ref, s32[1,3072]{1,0:T(1,128)S(1)} %get-tuple-element.12.rs_ref, ...), custom_call_target="tpu_custom_call" | custom-call | flops 9437184000 | bytes 37748736 | tf_op jit(solution)/shard_map/build/pallas_call | solution.py:185
  53.9 0.0 copy-start
  54.0 6.5 %copy-done = bf16[3072,3072]{1,0:T(8,128)(2,1)} copy-done((bf16[3072,3072]{1,0:T(8,128)(2,1)}, bf16[3072,3072]{1,0:T(8,128)(2,1)S(1)}, u32[]{:S(2)}) %copy-start) | copy-done | bytes 18874392
  60.4 0.0 copy-start.2
  60.4 6.5 %copy-done.2 = bf16[3072,3072]{1,0:T(8,128)(2,1)} copy-done((bf16[3072,3072]{1,0:T(8,128)(2,1)}, bf16[3072,3072]{1,0:T(8,128)(2,1)S(1)}, u32[]{:S(2)}) %copy-start.2) | copy-done | bytes 18874392
  66.9 25.2 %all_to_all.30.in_ref = f32[16,24,128]{2,1,0:T(8,128)S(1)} all-to-all(f32[16,24,128]{2,1,0:T(8,128)S(1)} %get-tuple-element.7), channel_id=1, replica_groups=mesh['row'=16,'col'=16] {'row'}, dimensions={0} | all-to-all | bytes 393216 | tf_op jit(solution)/shard_map/all_to_all | solution.py:352
  92.1 0.6 first_sum.1
  92.8 11.5 %all_to_all.31.w_ref = f32[16,16,128]{2,1,0:T(8,128)S(1)} all-to-all(f32[16,16,128]{2,1,0:T(8,128)S(1)} %get-tuple-element.8), channel_id=1, replica_groups=mesh['row'=16,'col'=16] {'row'}, dimensions={0} | all-to-all | bytes 262144 | tf_op jit(solution)/shard_map/all_to_all | solution.py:352
  104.3 7.9 %all-to-all-start.3 = ((f32[16,8,128]{2,1,0:T(8,128)}), f32[16,8,128]{2,1,0:T(8,128)S(1)}, u32[]{:S(2)}, u32[]{:S(2)}) async-start(f32[16,8,128]{2,1,0:T(8,128)} %get-tuple-element.11), calls=%async_computation.3 | async-start | bytes 131072 | tf_op jit(solution)/shard_map/all_to_all | solution.py:352
  112.2 1.9 %collective-permute-start.2 = (f32[16,16,128]{2,1,0:T(8,128)S(1)}, f32[16,16,128]{2,1,0:T(8,128)S(1)}, u32[]{:S(2)}, u32[]{:S(2)}) collective-permute-start(f32[16,16,128]{2,1,0:T(8,128)S(1)} %all_to_all.31.w_ref), channel_id=1, source_target_pairs={{0,0},{1,16},{2,32},{3,48},{4,64},{5,80},{6,96},{7,112},{8,128},{9... | collective-permute-start | bytes 393224 | tf_op jit(solution)/shard_map/ppermute | solution.py:349
  114.1 0.0 copy-done.10
  114.2 0.0 copy-start.1
  114.2 6.4 %copy-done.1 = bf16[3072,3072]{1,0:T(8,128)(2,1)S(1)} copy-done((bf16[3072,3072]{1,0:T(8,128)(2,1)S(1)}, bf16[3072,3072]{1,0:T(8,128)(2,1)}, u32[]{:S(2)}) %copy-start.1) | copy-done | bytes 18874392
  120.5 0.0 copy-start.3
  120.5 6.4 %copy-done.3 = bf16[3072,3072]{1,0:T(8,128)(2,1)S(1)} copy-done((bf16[3072,3072]{1,0:T(8,128)(2,1)S(1)}, bf16[3072,3072]{1,0:T(8,128)(2,1)}, u32[]{:S(2)}) %copy-start.3) | copy-done | bytes 18874392
  126.9 0.0 copy-start.7
  126.9 11.6 %apply.1.z_ref = f32[16,16,128]{2,1,0:T(8,128)} custom-call(bf16[3072,3072]{1,0:T(8,128)(2,1)S(1)} %copy-done.1, bf16[3072,3072]{1,0:T(8,128)(2,1)S(1)} %copy-done.3, f32[16,16,128]{2,1,0:T(8,128)S(1)} %all_to_all.31.w_ref, f32[1,3072]{1,0:T(1,128)S(1)} %bitcast.8, f32[1]{0:T(128)} %bitcast.4.flag_ref), custom_call_target="tpu_custom_call" | custom-call | flops 5662310400 | bytes 37748736 | tf_op jit(solution)/shard_map/apply/pallas_call | solution.py:232
  138.5 0.0 all-to-all-done.3.line_ref
  138.5 7.4 %all-to-all-start.2 = ((f32[16,16,128]{2,1,0:T(8,128)}), f32[16,16,128]{2,1,0:T(8,128)S(1)}, u32[]{:S(2)}, u32[]{:S(2)}) async-start(f32[16,16,128]{2,1,0:T(8,128)} %apply.1.z_ref), calls=%async_computation.2 | async-start | bytes 262144 | tf_op jit(solution)/shard_map/all_to_all | solution.py:352
  145.9 0.0 collective-permute-done.2.w_ref
  145.9 0.0 copy-done.7
  145.9 1.2 scalars.1
  147.1 6.5 %all-to-all-done.2.in_ref = f32[16,16,128]{2,1,0:T(8,128)S(1)} async-done(((f32[16,16,128]{2,1,0:T(8,128)}), f32[16,16,128]{2,1,0:T(8,128)S(1)}, u32[]{:S(2)}, u32[]{:S(2)}) %all-to-all-start.2) | async-done | bytes 131104 | tf_op jit(solution)/shard_map/all_to_all | solution.py:352
  153.5 15.2 %all_to_all.32.line_ref = f32[16,8,128]{2,1,0:T(8,128)S(1)} all-to-all(f32[16,8,128]{2,1,0:T(8,128)S(1)} %scalars.1), channel_id=1, replica_groups=mesh['row'=16,'col'=16] {'row'}, dimensions={0} | all-to-all | bytes 131072 | tf_op jit(solution)/shard_map/all_to_all | solution.py:352
  168.8 12.7 %all_to_all.33.a_ref = f32[16,24,128]{2,1,0:T(8,128)S(1)} all-to-all(f32[16,24,128]{2,1,0:T(8,128)S(1)} %second_sum.1), channel_id=1, replica_groups=mesh['row'=16,'col'=16] {'col'}, dimensions={0} | all-to-all | bytes 393216 | tf_op jit(solution)/shard_map/all_to_all | solution.py:352
  181.5 0.9 finish.1
  (2 shorter events, 0.1 us)
Async XLA Ops:
  1.4 19.1 %collective-permute-start = (s32[2,3072]{1,0:T(2,128)S(1)}, s32[2,3072]{1,0:T(2,128)S(1)}, u32[]{:S(2)}, u32[]{:S(2)}) collective-permute-start(s32[2,3072]{1,0:T(2,128)S(1)} %pad_add_fusion), channel_id=1, source_target_pairs={{0,0},{1,16},{2,32},{3,48},{4,64},{5,80},{6,96},{7,112},{8,128},{9... | collective-permute-start | bytes 73736 | tf_op jit(solution)/shard_map/ppermute | solution.py:349
  5.9 26.6 %collective-permute-start.1 = (f32[9,3072]{1,0:T(8,128)}, f32[9,3072]{1,0:T(8,128)S(1)}, u32[]{:S(2)}, u32[]{:S(2)}) collective-permute-start(f32[9,3072]{1,0:T(8,128)} %b_ref.5), channel_id=1, source_target_pairs={{0,0},{1,16},{2,32},{3,48},{4,64},{5,80},{6,96},{7,112},{8,128},{9... | collective-permute-start | bytes 331784 | tf_op jit(solution)/shard_map/ppermute | solution.py:349
  7.8 1.4 copy-start.4
  9.2 0.7 copy-start.8
  20.5 1.4 copy-start.5
  21.9 92.2 %copy-start.10 = (f32[3072]{0:T(1024)S(1)}, f32[3072]{0:T(1024)}, u32[]{:S(2)}) copy-start(f32[3072]{0:T(1024)} %param.6) | copy-start | bytes 36868
  32.5 0.9 copy-start.6
  33.4 0.7 copy-start.9
  34.1 0.7 copy-start.11
  53.9 6.5 %copy-start = (bf16[3072,3072]{1,0:T(8,128)(2,1)}, bf16[3072,3072]{1,0:T(8,128)(2,1)S(1)}, u32[]{:S(2)}) copy-start(bf16[3072,3072]{1,0:T(8,128)(2,1)S(1)} %get-tuple-element.9.khi_ref) | copy-start | bytes 56623108
  60.4 6.5 %copy-start.2 = (bf16[3072,3072]{1,0:T(8,128)(2,1)}, bf16[3072,3072]{1,0:T(8,128)(2,1)S(1)}, u32[]{:S(2)}) copy-start(bf16[3072,3072]{1,0:T(8,128)(2,1)S(1)} %get-tuple-element.10.klo_ref) | copy-start | bytes 56623108
  104.3 34.2 %all-to-all-start.3 = ((f32[16,8,128]{2,1,0:T(8,128)}), f32[16,8,128]{2,1,0:T(8,128)S(1)}, u32[]{:S(2)}, u32[]{:S(2)}) async-start(f32[16,8,128]{2,1,0:T(8,128)} %get-tuple-element.11), calls=%async_computation.3 | async-start | bytes 131072 | tf_op jit(solution)/shard_map/all_to_all | solution.py:352
  112.2 33.6 %collective-permute-start.2 = (f32[16,16,128]{2,1,0:T(8,128)S(1)}, f32[16,16,128]{2,1,0:T(8,128)S(1)}, u32[]{:S(2)}, u32[]{:S(2)}) collective-permute-start(f32[16,16,128]{2,1,0:T(8,128)S(1)} %all_to_all.31.w_ref), channel_id=1, source_target_pairs={{0,0},{1,16},{2,32},{3,48},{4,64},{5,80},{6,96},{7,112},{8,128},{9... | collective-permute-start | bytes 393224 | tf_op jit(solution)/shard_map/ppermute | solution.py:349
  114.2 6.4 %copy-start.1 = (bf16[3072,3072]{1,0:T(8,128)(2,1)S(1)}, bf16[3072,3072]{1,0:T(8,128)(2,1)}, u32[]{:S(2)}) copy-start(bf16[3072,3072]{1,0:T(8,128)(2,1)} %copy-done) | copy-start | bytes 56623108
  120.5 6.4 %copy-start.3 = (bf16[3072,3072]{1,0:T(8,128)(2,1)S(1)}, bf16[3072,3072]{1,0:T(8,128)(2,1)}, u32[]{:S(2)}) copy-start(bf16[3072,3072]{1,0:T(8,128)(2,1)} %copy-done.2) | copy-start | bytes 56623108
  126.9 19.0 %copy-start.7 = (f32[9,3072]{1,0:T(8,128)S(1)}, f32[9,3072]{1,0:T(8,128)}, u32[]{:S(2)}) copy-start(f32[9,3072]{1,0:T(8,128)} %b_ref.5) | copy-start | bytes 331780
  138.5 15.0 %all-to-all-start.2 = ((f32[16,16,128]{2,1,0:T(8,128)}), f32[16,16,128]{2,1,0:T(8,128)S(1)}, u32[]{:S(2)}, u32[]{:S(2)}) async-start(f32[16,16,128]{2,1,0:T(8,128)} %apply.1.z_ref), calls=%async_computation.2 | async-start | bytes 262144 | tf_op jit(solution)/shard_map/all_to_all | solution.py:352

commit v2 on v1

v2 whole, which is shorter than its diff:
```python
import functools
import math

import jax
import jax.numpy as jnp
from jax import lax
from jax.experimental import pallas as pl
from jax.experimental.pallas import tpu as pltpu
from jax.sharding import PartitionSpec as P

LANES = 128
SIDE = 16
FEAT = 16
PROBES = 9
ROWS = 16
BUILD = 10
MORE = 24
PACK = 8
DEPTH = 128
LOG2E = 1.4426950408889634
F32 = jnp.float32
BF16 = jnp.bfloat16
F8 = jnp.float8_e4m3fn
TOP = 240.0
LIFT = 65536.0
VMEM = pltpu.VMEM
MIB = 1024 * 1024


def vspec():
    return pl.BlockSpec(memory_space=VMEM)


def sspec():
    return pl.BlockSpec(memory_space=pltpu.SMEM)


def params(mib=2):
    return pltpu.CompilerParams(vmem_limit_bytes=mib * MIB)


def thirds(x):
    a = x.astype(BF16).astype(F32)
    b = (x - a).astype(BF16).astype(F32)
    return a, b, x - a - b


def to_lanes(column, first):
    lane = lax.broadcasted_iota(jnp.int32, (PROBES, LANES), 1)
    sub = lax.broadcasted_iota(jnp.int32, (PROBES, LANES), 0)
    return jnp.sum(jnp.where(lane == sub + first, column, 0.0), axis=0, keepdims=True)


def to_column(row, first):
    lane = lax.broadcasted_iota(jnp.int32, (PROBES, LANES), 1)
    sub = lax.broadcasted_iota(jnp.int32, (PROBES, LANES), 0)
    return jnp.sum(jnp.where(lane == sub + first, row, 0.0), axis=1, keepdims=True)


def unpack(v_ref, nat, tiles):
    for t in range(tiles):
        lanes = slice(t * LANES, (t + 1) * LANES)
        nat[0:8, lanes] = v_ref[t // 2, 8 * (t % 2) : 8 * (t % 2) + 8, :]
        m = 8 * tiles + t
        nat[8:9, lanes] = v_ref[m // ROWS, m % ROWS : m % ROWS + 1, :]


def pack_tile(out_ref, res, tile, tiles):
    out_ref[tile // 2, pl.ds(pl.multiple_of(8 * (tile % 2), 8), 8), :] = res[0:8]
    m = 8 * tiles + tile
    out_ref[m // ROWS, pl.ds(m % ROWS, 1), :] = res[8:9]


def clear_rest(out_ref, tiles):
    m = 9 * tiles
    out_ref[m // ROWS, m % ROWS : ROWS, :] = jnp.zeros((ROWS - m % ROWS, LANES), F32)
    for s in range(m // ROWS + 1, SIDE):
        out_ref[s, 0:ROWS, :] = jnp.zeros((ROWS, LANES), F32)


def codes(run_index):
    row = ((run_index >> 10) << 7) + (run_index & 127)
    return (((run_index >> 7) & 7) << 12) + row


def by_groups(read, table, rows_a, rows_b, make, groups):
    def fetch(g, rows):
        for p in range(LANES):
            rows[p : p + 1, :] = table[pl.ds(read(g, p) & 4095, 1), :]

    def pair(h, _):
        fetch(2 * h + 1, rows_b)
        make(2 * h, rows_a)
        fetch(jnp.minimum(2 * h + 2, groups - 1), rows_a)
        make(2 * h + 1, rows_b)
        return 0

    fetch(0, rows_a)
    lax.fori_loop(0, groups // 2, pair, 0)


def factors(v):
    zero = jnp.zeros((ROWS - PROBES, v.shape[1]), F32)
    high = v.astype(BF16).astype(F32)
    halves = jnp.concatenate([high, zero, v - high, zero], axis=0).astype(BF16)
    top = jnp.max(jnp.abs(v), axis=1, keepdims=True)
    top = jnp.where(top > 0.0, top, 1.0)
    u = v * (TOP / top)
    coarse = u.astype(F8).astype(F32)
    small = jnp.concatenate([coarse, zero, (u - coarse), zero], axis=0).astype(F8)
    return halves, small, top * (1.0 / (TOP * LIFT))


def selector(blocks):
    src = lax.broadcasted_iota(jnp.int32, (LANES, LANES), 0)
    dst = lax.broadcasted_iota(jnp.int32, (LANES, LANES), 1)
    hit = dst // FEAT == blocks[0]
    for block in blocks[1:]:
        hit = hit | (dst // FEAT == block)
    return jnp.where(hit & (src % FEAT == dst % FEAT), 1.0, 0.0).astype(BF16)


LEFT = ((0, 1, 4), (2, 3), (5,))
RIGHT = ((0, 2, 5), (1, 3), (4,))


def operand(rows, code, picks, is_left):
    lane = lax.broadcasted_iota(jnp.int32, (LANES, LANES), 1)
    group = jnp.transpose(jnp.broadcast_to((code >> 12).astype(F32), (LANES, LANES)))
    f = jnp.where((lane >> 4).astype(F32) == group, rows * math.sqrt(LOG2E), 0.0)
    norm = -0.5 * jnp.sum(f * f, axis=1, keepdims=True)
    if is_left:
        norm = norm + 1.5 * math.log2(8.0)
    out = None
    for part, pick in zip(thirds(f), picks):
        moved = jnp.dot(part.astype(BF16), pick, preferred_element_type=F32)
        out = moved if out is None else out + moved
    first = 6 * FEAT + (0 if is_left else 3)
    ones = 6 * FEAT + (3 if is_left else 0)
    for k, part in enumerate(thirds(norm)):
        out = jnp.where(lane == first + k, part, out)
    return jnp.where((lane >= ones) & (lane < ones + 3), 1.0, out)


def own_body(idx_ref, code_ref, step_ref, tab_ref, b_ref, table, left, steps, vec, small, scale, rows_a, rows_b):
    n = left.shape[0]
    groups = tab_ref.shape[1] // LANES
    for t in range(groups // PACK):
        tiles = [tab_ref[:, (PACK * t + g) * LANES : (PACK * t + g + 1) * LANES] for g in range(PACK)]
        table[t * LANES : (t + 1) * LANES, :] = jnp.transpose(jnp.concatenate(tiles, axis=0))
    picks = [selector(blocks) for blocks in LEFT]

    def make(t, rows):
        o = pl.ds(pl.multiple_of(t * LANES, LANES), LANES)
        left[o, :] = operand(rows[...], code_ref[pl.ds(t, 1), :], picks, True).astype(BF16)
        step = step_ref[pl.ds(t, 1), :].astype(F32) + 8.0
        steps[o, :] = jnp.transpose(jnp.broadcast_to(step, (LANES, LANES)))

    by_groups(lambda g, p: idx_ref[g, p], table, rows_a, rows_b, make, n // LANES)
    vec[...], small[...], factor = factors(b_ref[...])
    scale[...] = jnp.concatenate([jnp.broadcast_to(factor, (PROBES, LANES)), jnp.zeros((ROWS - PROBES, LANES), F32)], axis=0)


def own(code, step, table, b):
    n = b.shape[1]
    packed = table.shape[1] // PACK
    return pl.pallas_call(
        own_body,
        out_shape=(
            VMEM((packed, LANES), F32),
            VMEM((n, LANES), BF16),
            VMEM((n, LANES), F32),
            VMEM((2 * ROWS, n), BF16),
            VMEM((2 * ROWS, n), F8),
            VMEM((ROWS, LANES), F32),
        ),
        in_specs=[sspec()] + [vspec()] * 4,
        out_specs=(vspec(),) * 6,
        scratch_shapes=[VMEM((LANES, LANES), F32), VMEM((LANES, LANES), F32)],
        compiler_params=params(4),
        cost_estimate=pl.CostEstimate(flops=n * 6000, bytes_accessed=4 * table.size, transcendentals=0),
        name="own",
    )(code, code, step, table, b)


def build_body(idx_ref, other_ref, table, left, steps, vec, small, scale, b_ref, noise_ref, flag_ref,
               khi_ref, klo_ref, out_ref, rows_a, rows_b, right, right_steps, acc, acc8, *, pt, qt):
    n, m = khi_ref.shape
    tiles = m // LANES
    picks = [selector(blocks) for blocks in RIGHT]

    def make(t, rows):
        o = pl.ds(pl.multiple_of(t * LANES, LANES), LANES)
        part = operand(rows[...], other_ref[0, pl.ds(t, 1), :], picks, False)
        right[:, o] = jnp.transpose(part).astype(BF16)
        right_steps[0:1, o] = other_ref[1, pl.ds(t, 1), :].astype(F32)

    by_groups(lambda g, p: idx_ref[0, g, p], table, rows_a, rows_b, make, tiles)

    def column(jq, _):
        oq = pl.ds(pl.multiple_of(jq * qt, qt), qt)
        right_tile = right[:, oq]
        right_step = right_steps[0:1, oq]
        acc[...] = jnp.zeros_like(acc)
        acc8[...] = jnp.zeros_like(acc8)

        def row(ip, _):
            op = pl.ds(pl.multiple_of(ip * pt, pt), pt)
            power = jnp.dot(left[op, :], right_tile, preferred_element_type=F32)
            spread = jnp.concatenate([steps[op, :]] * (qt // LANES), axis=1) + right_step
            root = lax.rsqrt(spread)
            k = jnp.exp2(power) * (root * (root * root))
            high = k.astype(BF16)
            low = ((k - high.astype(F32)) * LIFT).astype(F8)
            khi_ref[op, oq] = high
            klo_ref[op, oq] = low
            acc[...] += jnp.dot(vec[:, op], high, preferred_element_type=F32)
            acc8[...] += jnp.dot(small[:, op], low, preferred_element_type=F32)
            return 0

        lax.fori_loop(0, n // pt, row, 0, unroll=n // pt)
        res = acc[0:ROWS, :] + acc[ROWS:, :] + scale[:, 0:1] * (acc8[0:ROWS, :] + acc8[ROWS:, :])
        res = res[0:PROBES] + flag_ref[0] * (noise_ref[:, oq] * b_ref[:, oq])
        for t in range(qt // LANES):
            pack_tile(out_ref, res[:, t * LANES : (t + 1) * LANES], jq * (qt // LANES) + t, tiles)
        return 0

    clear_rest(out_ref, tiles)
    lax.fori_loop(0, m // qt, column, 0)


def build(other, table, left, steps, vec, small, scale, b, noise, flag, pt=3072, qt=256):
    n = b.shape[1]
    m = other.shape[1] * LANES
    return pl.pallas_call(
        functools.partial(build_body, pt=pt, qt=qt),
        out_shape=(VMEM((n, m), BF16), VMEM((n, m), F8), jax.ShapeDtypeStruct((SIDE, ROWS, LANES), F32)),
        in_specs=[sspec()] + [vspec()] * 9 + [sspec()],
        out_specs=(vspec(),) * 3,
        scratch_shapes=[
            VMEM((LANES, LANES), F32),
            VMEM((LANES, LANES), F32),
            VMEM((DEPTH, m), BF16),
            VMEM((8, m), F32),
            VMEM((2 * ROWS, qt), F32),
            VMEM((2 * ROWS, qt), F32),
        ],
        compiler_params=params(BUILD),
        cost_estimate=pl.CostEstimate(flops=n * m * 1000, bytes_accessed=n * m * 3, transcendentals=2 * n * m),
        name="build",
    )(other, other, table, left, steps, vec, small, scale, b, noise.reshape(1, n), flag)


def apply_body(khi_ref, klo_ref, w_ref, noise_ref, flag_ref, out_ref, nat, vec, small, *, pt):
    n, m = khi_ref.shape
    unpack(w_ref, nat, m // LANES)
    vec[...], small[...], scale = factors(nat[0:PROBES, :])
    clear_rest(out_ref, n // LANES)
    dims = (((1,), (1,)), ((), ()))

    def row(ip, _):
        op = pl.ds(pl.multiple_of(ip * pt, pt), pt)
        y = lax.dot_general(vec[...], khi_ref[op, :], dims, preferred_element_type=F32)
        z = lax.dot_general(small[...], klo_ref[op, :], dims, preferred_element_type=F32)
        res = (y[0:ROWS] + y[ROWS:])[0:PROBES] + scale * (z[0:ROWS] + z[ROWS:])[0:PROBES]
        res = res + flag_ref[0] * (noise_ref[:, op] * nat[0:PROBES, op])
        for t in range(pt // LANES):
            pack_tile(out_ref, res[:, t * LANES : (t + 1) * LANES], ip * (pt // LANES) + t, n // LANES)
        return 0

    lax.fori_loop(0, n // pt, row, 0)


def apply(khi, klo, w, noise, flag, pt=512):
    n, m = khi.shape
    khi = pltpu.with_memory_space_constraint(khi, VMEM)
    klo = pltpu.with_memory_space_constraint(klo, VMEM)
    return pl.pallas_call(
        functools.partial(apply_body, pt=pt),
        out_shape=jax.ShapeDtypeStruct((SIDE, ROWS, LANES), F32),
        in_specs=[vspec()] * 4 + [sspec()],
        out_specs=vspec(),
        scratch_shapes=[VMEM((ROWS, m), F32), VMEM((2 * ROWS, m), BF16), VMEM((2 * ROWS, m), F8)],
        compiler_params=params(4),
        cost_estimate=pl.CostEstimate(flops=n * m * 600, bytes_accessed=n * m * 3, transcendentals=0),
        name="apply",
    )(khi, klo, w, noise.reshape(1, n), flag)


def first_sum_body(in_ref, out_ref):
    total = jnp.sum(in_ref[...], axis=0)
    for s in range(SIDE):
        out_ref[s] = total


def first_sum(got):
    return pl.pallas_call(
        first_sum_body,
        out_shape=jax.ShapeDtypeStruct((SIDE, ROWS, LANES), F32),
        in_specs=[vspec()],
        out_specs=vspec(),
        compiler_params=params(),
        name="first_sum",
    )(got)


def scalar_body(b_ref, w_ref, z_ref, out_ref, nw, nz):
    tiles = b_ref.shape[1] // LANES
    unpack(w_ref, nw, tiles)
    unpack(z_ref, nz, tiles)
    b, w, z = b_ref[...], nw[0:PROBES, :], nz[0:PROBES, :]

    def dot(x, y):
        return jnp.sum(x * y, axis=1, keepdims=True)

    ww, bw = dot(w, w), dot(b, w)
    near = jnp.where(ww > 0.0, bw / ww, 0.0)
    r = b - near * w
    line = jnp.zeros((1, LANES), F32)
    for k, value in enumerate((dot(b, b), bw, ww, near, dot(r, r), dot(r, w), dot(r, z), dot(w, z))):
        line = line + to_lanes(value, ROWS * k)
    for s in range(SIDE):
        out_ref[s] = jnp.broadcast_to(line, (MORE - ROWS, LANES))


def scalars(b, w, z):
    n = b.shape[1]
    return pl.pallas_call(
        scalar_body,
        out_shape=jax.ShapeDtypeStruct((SIDE, MORE - ROWS, LANES), F32),
        in_specs=[vspec()] * 3,
        out_specs=vspec(),
        scratch_shapes=[VMEM((ROWS, n), F32), VMEM((ROWS, n), F32)],
        compiler_params=params(),
        name="scalars",
    )(b, w, z)


def second_sum_body(in_ref, line_ref, out_ref):
    total = jnp.sum(in_ref[...], axis=0)
    blocks = jnp.concatenate([line_ref[s, 0:1, :] for s in range(SIDE)], axis=0)

    def part(k):
        return blocks if k == 0 else pltpu.roll(blocks, LANES - ROWS * k, 1)

    def over(x):
        return jnp.sum(x, axis=0, keepdims=True)

    bb, bw, ww, near, rr, rw, rz, wz = (part(k) for k in range(8))
    all_bb, all_bw = over(bb), over(bw)
    shift = near - all_bb / all_bw
    lines = [over(rz + shift * wz), over(rr + shift * (2.0 * rw + shift * ww)), over(rw + shift * ww), all_bb, all_bw]
    lines = jnp.concatenate(lines + [jnp.zeros((3, LANES), F32)], axis=0)
    for s in range(SIDE):
        out_ref[s, 0:ROWS, :] = total
        out_ref[s, ROWS:MORE, :] = lines


def second_sum(got, line):
    return pl.pallas_call(
        second_sum_body,
        out_shape=jax.ShapeDtypeStruct((SIDE, MORE, LANES), F32),
        in_specs=[vspec(), vspec()],
        out_specs=vspec(),
        compiler_params=params(),
        name="second_sum",
    )(got, line)


def finish_body(b_ref, w_ref, a_ref, x_ref, r_ref, nw, na):
    tiles = b_ref.shape[1] // LANES
    unpack(w_ref, nw, tiles)
    unpack(a_ref, na, tiles)
    rz = to_column(jnp.sum(a_ref[:, ROWS:MORE, :], axis=0)[0:1], 0)
    rr, rw, bb, bw = (to_column(a_ref[0, ROWS + k : ROWS + k + 1, :], 0) for k in range(1, 5))
    first = bb / bw
    beta = rr / bb
    second = rr / ((rw - first * rz) + 2.0 * beta * rw + beta * beta * bw)
    b = b_ref[...]
    w = nw[0:PROBES, :]
    r = b - first * w
    x_ref[...] = first * b + second * (r + beta * b)
    r_ref[...] = r - second * ((w - first * na[0:PROBES, :]) + beta * w)


def finish(b, w, a):
    n = b.shape[1]
    out = jax.ShapeDtypeStruct((PROBES, n), F32)
    return pl.pallas_call(
        finish_body,
        out_shape=(out, out),
        in_specs=[vspec()] * 3,
        out_specs=(vspec(), vspec()),
        scratch_shapes=[VMEM((ROWS, n), F32), VMEM((ROWS, n), F32)],
        compiler_params=params(),
        name="finish",
    )(b, w, a)


def on_device(right_side, noise_level, run_index, step_index, run_features):
    swap = [(i * SIDE + j, j * SIDE + i) for i in range(SIDE) for j in range(SIDE)]

    def swapped(x):
        return lax.ppermute(x, ("row", "col"), swap)

    def exchange(x, axis):
        return lax.all_to_all(x, axis, 0, 0)

    flag = (lax.axis_index("row") == lax.axis_index("col")).astype(F32).reshape(1)
    tiles = run_index.shape[0] // LANES
    code = codes(run_index).reshape(tiles, LANES)
    step = step_index.reshape(tiles, LANES)
    other = swapped(jnp.stack([code, step]))
    mine = own(code, step, run_features, right_side)
    khi, klo, part = build(other, *mine, right_side, noise_level, flag)
    product = exchange(first_sum(exchange(part, "row")), "row")
    own_product = swapped(product)
    part = apply(khi, klo, product, noise_level, flag)
    summed = exchange(part, "col")
    line = exchange(scalars(right_side, own_product, part), "row")
    again = exchange(second_sum(summed, line), "col")
    return finish(right_side, own_product, again)


def solution(mesh):
    return jax.shard_map(
        on_device,
        mesh=mesh,
        in_specs=(P(None, "row"), P("row"), P("row"), P("row"), P()),
        out_specs=(P(None, "row"), P(None, "row")),
        check_vma=False,
    )
```

time: 183 us -> 129 us (0.70)
  local copies, waits for them, and re-layouts: 31.5 us -> 3.04 us
  Pallas kernels: 54.5 us -> 43.8 us
  blocking collectives: 64.7 us -> 55.9 us
  starting transfers between devices: 23.6 us -> 16.9 us
    unnamed x24 -> x10, local copies, waits for them, and re-layouts: 31.5 us -> 3.04 us
    all_to_all x4, blocking collectives: 64.7 us -> 55.9 us  [exchange(): return lax.all_to_all(x, axis, 0, 0)]
    pallas_call x5 -> x4, Pallas kernels: 41.7 us -> 33.2 us  [the longest x1 25.3 us: build(): pl.pallas_call(functools.partial(build_body, pt=pt, qt=qt), out_shape=(VM...]
    all_to_all x2 -> x1, starting transfers between devices: 15.3 us -> 7.08 us  [exchange(): return lax.all_to_all(x, axis, 0, 0)]
    pallas_call x1, Pallas kernels: 11.6 us -> 9.31 us  [apply(): pl.pallas_call(functools.partial(apply_body, pt=pt), out_shape=jax.ShapeD...]
    ppermute x3 -> x2, starting transfers between devices: 8.34 us -> 9.86 us  [swapped(): return lax.ppermute(x, ('row', 'col'), swap)]
    all_to_all x2 -> x1, waiting for transfers between devices: 6.46 us -> 6.41 us  [exchange(): return lax.all_to_all(x, axis, 0, 0)]
  transfers between devices with their start and end apart: 5 -> 3, of which waited for: 1 -> 1; matrix products, arithmetic and copies ran while one was open for 0% -> 0% of each run, Pallas kernels for 19% -> 14%
where the time goes in v2:
time: 129 us; the launch traced here: 128 us
  blocking collectives  55.9 us (43%)
  Pallas kernels  43.8 us (34%)
  starting transfers between devices  16.9 us (13%)
  waiting for transfers between devices  6.42 us (5%)
  local copies, waits for them, and re-layouts  3.04 us (2%)
  other arithmetic  1.43 us (1%)
    all_to_all x4, blocking collectives, exchange(): return lax.all_to_all(x, axis, 0, 0)  55.9 us
    pallas_call x1, Pallas kernels, build(): pl.pallas_call(functools.partial(build_body, pt=pt, qt=qt), out_shape=(VM...  25.3 us
    ppermute x2, starting transfers between devices, swapped(): return lax.ppermute(x, ('row', 'col'), swap)  9.86 us
    pallas_call x1, Pallas kernels, apply(): pl.pallas_call(functools.partial(apply_body, pt=pt), out_shape=jax.ShapeD...  9.31 us
    all_to_all x1, starting transfers between devices, exchange(): return lax.all_to_all(x, axis, 0, 0)  7.08 us
    pallas_call x1, Pallas kernels, own(): pl.pallas_call(own_body, out_shape=(VMEM((packed, LANES), F32), VMEM((n,...  6.91 us
    all_to_all x1, waiting for transfers between devices, exchange(): return lax.all_to_all(x, axis, 0, 0)  6.41 us
    unnamed x10, local copies, waits for them, and re-layouts  3.04 us
  transfers between devices with their start and end apart: 3, of which 1 were waited for; matrix products, arithmetic and copies ran while one was open for 0% of the time, Pallas kernels for 14%

profile of v2, /device:TPU:1, one launch (start us, length us, event | category | flops | bytes accessed | tf_op | source)
XLA Modules:
  0.0 128.2 jit_solution(4097510010890157873)
XLA Ops:
  0.6 0.0 copy-start.4
  0.6 0.7 fusion
  1.4 0.7 pad_add_fusion
  2.1 4.5 %collective-permute-start = (s32[2,24,128]{2,1,0:T(8,128)S(1)}, s32[2,24,128]{2,1,0:T(8,128)S(1)}, u32[]{:S(2)}, u32[]{:S(2)}) collective-permute-start(s32[2,24,128]{2,1,0:T(8,128)S(1)} %pad_add_fusion), channel_id=1, source_target_pairs={{0,0},{1,16},{2,32},{3,48},{4,64},{5,80},{6,96},{7,112},{8,128},{9... | collective-permute-start | bytes 73736 | tf_op jit(solution)/shard_map/ppermute | solution.py:404
  6.6 0.0 copy-start
  6.6 0.9 copy-done
  7.5 0.0 copy-start.2
  7.5 1.4 %copy-done.2 = f32[16,24576]{1,0:T(8,128)S(1)} copy-done((f32[16,24576]{1,0:T(8,128)S(1)}, f32[16,24576]{1,0:T(8,128)}, u32[]{:S(2)}) %copy-start.2) | copy-done | bytes 1572888
  8.9 0.0 copy-start.3
  8.9 0.7 copy-done.3
  9.6 0.0 copy-start.1
  9.6 6.9 %own.1 = (f32[3072,128]{1,0:T(8,128)S(1)}, bf16[3072,128]{1,0:T(8,128)(2,1)S(1)}, f32[3072,128]{1,0:T(8,128)S(1)}, bf16[32,3072]{1,0:T(8,128)(2,1)S(1)}, f8e4m3f...) custom-call(s32[24,128]{1,0:T(8,128)S(1)} %get-tuple-element.20.idx_ref.code_ref, ...), custom_call_target="tpu_custom_call" | custom-call | flops 18432000 | bytes 1572864 | tf_op jit(solution)/shard_map/own/pallas_call | solution.py:167
  16.6 0.0 collective-permute-done.idx_ref.other_ref
  16.6 0.0 copy-done.4
  16.6 0.0 copy-done.1
  16.6 25.3 %build.1 = (bf16[3072,3072]{1,0:T(8,128)(2,1)S(1)}, f8e4m3fn[3072,3072]{1,0:T(32,128)(4,1)S(1)}, f32[16,16,128]{2,1,0:T(8,128)S(1)}) custom-call(s32[2,24,128]{2,1,0:T(8,128)S(1)} %collective-permute-done.idx_ref.other_ref, s32[2,24,128]{2,1,0:T(8,128)S(1)} %collective-permute-done.idx_ref.other_ref, f32[3072,128]{1,0:T(8,128)S(1)} %get-tuple-element.11.table, ...), custom_call_target="tpu_custom_call" | custom-call | flops 9437184000 | bytes 28311552 | tf_op jit(solution)/shard_map/build/pallas_call | solution.py:235
  41.9 17.8 %all_to_all.25.in_ref = f32[16,16,128]{2,1,0:T(8,128)S(1)} all-to-all(f32[16,16,128]{2,1,0:T(8,128)S(1)} %get-tuple-element.17), channel_id=1, replica_groups=mesh['row'=16,'col'=16] {'row'}, dimensions={0} | all-to-all | bytes 262144 | tf_op jit(solution)/shard_map/all_to_all | solution.py:407
  59.7 11.1 %all_to_all.26.w_ref = f32[16,16,128]{2,1,0:T(8,128)S(1)} all-to-all(f32[16,16,128]{2,1,0:T(8,128)S(1)} %first_sum.1), channel_id=1, replica_groups=mesh['row'=16,'col'=16] {'row'}, dimensions={0} | all-to-all | bytes 262144 | tf_op jit(solution)/shard_map/all_to_all | solution.py:407
  70.8 5.4 %collective-permute-start.1 = (f32[16,16,128]{2,1,0:T(8,128)S(1)}, f32[16,16,128]{2,1,0:T(8,128)S(1)}, u32[]{:S(2)}, u32[]{:S(2)}) collective-permute-start(f32[16,16,128]{2,1,0:T(8,128)S(1)} %all_to_all.26.w_ref), channel_id=1, source_target_pairs={{0,0},{1,16},{2,32},{3,48},{4,64},{5,80},{6,96},{7,112},{8,128},{9... | collective-permute-start | bytes 393224 | tf_op jit(solution)/shard_map/ppermute | solution.py:404
  76.2 9.3 %apply.1.z_ref = f32[16,16,128]{2,1,0:T(8,128)} custom-call(bf16[3072,3072]{1,0:T(8,128)(2,1)S(1)} %get-tuple-element.18.khi_ref, f8e4m3fn[3072,3072]{1,0:T(32,128)(4,1)S(1)} %get-tuple-element.19.klo_ref, f32[16,16,128]{2,1,0:T(8,128)S(1)} %all_to_all.26.w_ref, f32[1,3072]{1,0:T(1,128)S(1)} %bitcast.11, f32[1]{0:T(128)} %bitcast.5.flag_ref), custom_call_target="tpu_custom_call" | custom-call | flops 5662310400 | bytes 28311552 | tf_op jit(solution)/shard_map/apply/pallas_call | solution.py:278
  85.5 7.1 %all-to-all-start.2 = ((f32[16,16,128]{2,1,0:T(8,128)}), f32[16,16,128]{2,1,0:T(8,128)S(1)}, u32[]{:S(2)}, u32[]{:S(2)}) async-start(f32[16,16,128]{2,1,0:T(8,128)} %apply.1.z_ref), calls=%async_computation.2 | async-start | bytes 262144 | tf_op jit(solution)/shard_map/all_to_all | solution.py:407
  92.6 0.0 collective-permute-done.1.w_ref
  92.6 1.2 scalars.1
  93.8 6.4 %all-to-all-done.2.in_ref = f32[16,16,128]{2,1,0:T(8,128)S(1)} async-done(((f32[16,16,128]{2,1,0:T(8,128)}), f32[16,16,128]{2,1,0:T(8,128)S(1)}, u32[]{:S(2)}, u32[]{:S(2)}) %all-to-all-start.2) | async-done | bytes 131104 | tf_op jit(solution)/shard_map/all_to_all | solution.py:407
  100.2 14.2 %all_to_all.27.line_ref = f32[16,8,128]{2,1,0:T(8,128)S(1)} all-to-all(f32[16,8,128]{2,1,0:T(8,128)S(1)} %scalars.1), channel_id=1, replica_groups=mesh['row'=16,'col'=16] {'row'}, dimensions={0} | all-to-all | bytes 131072 | tf_op jit(solution)/shard_map/all_to_all | solution.py:407
  114.5 0.1 second_sum.1
  114.6 12.7 %all_to_all.28.a_ref = f32[16,24,128]{2,1,0:T(8,128)S(1)} all-to-all(f32[16,24,128]{2,1,0:T(8,128)S(1)} %second_sum.1), channel_id=1, replica_groups=mesh['row'=16,'col'=16] {'col'}, dimensions={0} | all-to-all | bytes 393216 | tf_op jit(solution)/shard_map/all_to_all | solution.py:407
  127.3 0.9 finish.1
  (1 shorter events, 0.0 us)
Async XLA Ops:
  0.6 15.9 %copy-start.4 = (f32[3072]{0:T(1024)S(1)}, f32[3072]{0:T(1024)}, u32[]{:S(2)}) copy-start(f32[3072]{0:T(1024)} %param.6) | copy-start | bytes 36868
  2.1 14.5 %collective-permute-start = (s32[2,24,128]{2,1,0:T(8,128)S(1)}, s32[2,24,128]{2,1,0:T(8,128)S(1)}, u32[]{:S(2)}, u32[]{:S(2)}) collective-permute-start(s32[2,24,128]{2,1,0:T(8,128)S(1)} %pad_add_fusion), channel_id=1, source_target_pairs={{0,0},{1,16},{2,32},{3,48},{4,64},{5,80},{6,96},{7,112},{8,128},{9... | collective-permute-start | bytes 73736 | tf_op jit(solution)/shard_map/ppermute | solution.py:404
  6.6 0.9 copy-start
  7.5 1.4 %copy-start.2 = (f32[16,24576]{1,0:T(8,128)S(1)}, f32[16,24576]{1,0:T(8,128)}, u32[]{:S(2)}) copy-start(f32[16,24576]{1,0:T(8,128)} %tab_ref.1) | copy-start | bytes 4718596
  8.9 0.7 copy-start.3
  9.6 6.9 %copy-start.1 = (f32[9,3072]{1,0:T(8,128)S(1)}, f32[9,3072]{1,0:T(8,128)}, u32[]{:S(2)}) copy-start(f32[9,3072]{1,0:T(8,128)} %b_ref.7) | copy-start | bytes 331780
  70.8 21.8 %collective-permute-start.1 = (f32[16,16,128]{2,1,0:T(8,128)S(1)}, f32[16,16,128]{2,1,0:T(8,128)S(1)}, u32[]{:S(2)}, u32[]{:S(2)}) collective-permute-start(f32[16,16,128]{2,1,0:T(8,128)S(1)} %all_to_all.26.w_ref), channel_id=1, source_target_pairs={{0,0},{1,16},{2,32},{3,48},{4,64},{5,80},{6,96},{7,112},{8,128},{9... | collective-permute-start | bytes 393224 | tf_op jit(solution)/shard_map/ppermute | solution.py:404
  85.5 14.7 %all-to-all-start.2 = ((f32[16,16,128]{2,1,0:T(8,128)}), f32[16,16,128]{2,1,0:T(8,128)S(1)}, u32[]{:S(2)}, u32[]{:S(2)}) async-start(f32[16,16,128]{2,1,0:T(8,128)} %apply.1.z_ref), calls=%async_computation.2 | async-start | bytes 262144 | tf_op jit(solution)/shard_map/all_to_all | solution.py:407

commit v3 on v2

v3 whole, which is shorter than its diff:
```python
import functools
import math

import jax
import jax.numpy as jnp
from jax import lax
from jax.experimental import pallas as pl
from jax.experimental.pallas import tpu as pltpu
from jax.sharding import PartitionSpec as P

LANES = 128
SIDE = 16
FEAT = 16
PROBES = 9
ROWS = 16
BUILD = 8
BOTH = 32
MORE = 40
LINES = 8
GROUP = 4096
DEPTH = 128
LOG2E = 1.4426950408889634
F32 = jnp.float32
BF16 = jnp.bfloat16
F8 = jnp.float8_e4m3fn
TOP = 240.0
LIFT = 65536.0
VMEM = pltpu.VMEM
MIB = 1024 * 1024


def vspec():
    return pl.BlockSpec(memory_space=VMEM)


def sspec():
    return pl.BlockSpec(memory_space=pltpu.SMEM)


def params(mib=2):
    return pltpu.CompilerParams(vmem_limit_bytes=mib * MIB)


def thirds(x):
    a = x.astype(BF16).astype(F32)
    b = (x - a).astype(BF16).astype(F32)
    return a, b, x - a - b


def to_column(row, first):
    lane = lax.broadcasted_iota(jnp.int32, (PROBES, LANES), 1)
    sub = lax.broadcasted_iota(jnp.int32, (PROBES, LANES), 0)
    return jnp.sum(jnp.where(lane == sub + first, row, 0.0), axis=1, keepdims=True)


def unpack(v_ref, nat, tiles, first=0):
    for t in range(tiles):
        lanes = slice(t * LANES, (t + 1) * LANES)
        row = first + 8 * (t % 2)
        nat[0:8, lanes] = v_ref[t // 2, row : row + 8, :]
        m = 8 * tiles + t
        row = first + m % ROWS
        nat[8:9, lanes] = v_ref[m // ROWS, row : row + 1, :]


def pack_tile(out_ref, res, tile, tiles):
    out_ref[tile // 2, pl.ds(pl.multiple_of(8 * (tile % 2), 8), 8), :] = res[0:8]
    m = 8 * tiles + tile
    out_ref[m // ROWS, pl.ds(m % ROWS, 1), :] = res[8:9]


def clear_rest(out_ref, tiles):
    m = 9 * tiles
    out_ref[m // ROWS, m % ROWS : ROWS, :] = jnp.zeros((ROWS - m % ROWS, LANES), F32)
    for s in range(m // ROWS + 1, SIDE):
        out_ref[s, 0:ROWS, :] = jnp.zeros((ROWS, LANES), F32)


def factors(v):
    zero = jnp.zeros((ROWS - PROBES, v.shape[1]), F32)
    high = v.astype(BF16).astype(F32)
    halves = jnp.concatenate([high, zero, v - high, zero], axis=0).astype(BF16)
    top = jnp.max(jnp.abs(v), axis=1, keepdims=True)
    top = jnp.where(top > 0.0, top, 1.0)
    u = v * (TOP / top)
    coarse = u.astype(F8).astype(F32)
    small = jnp.concatenate([coarse, zero, (u - coarse), zero], axis=0).astype(F8)
    return halves, small, top * (1.0 / (TOP * LIFT))


def own_body(idx_ref, run_ref, step_ref, tab_ref, out_ref, tab, table, runs, steps, rows_a, rows_b, sems):
    tiles = out_ref.shape[0] // (FEAT + 1)
    groups = tab_ref.shape[1] // GROUP
    width = GROUP // 4
    loads = [pltpu.make_async_copy(run_ref, runs, sems.at[0]), pltpu.make_async_copy(step_ref, steps, sems.at[1])]
    for load in loads:
        load.start()
    parts = []
    for c in range(4):
        for g in range(groups):
            at = pl.ds(g * GROUP + c * width, width)
            parts.append(pltpu.make_async_copy(tab_ref.at[:, at], tab.at[:, at], sems.at[2 + c * groups + g]))
    for part in parts:
        part.start()
    blank = jnp.zeros((LANES - groups * FEAT, LANES), F32)
    for c in range(4):
        for part in parts[c * groups : (c + 1) * groups]:
            part.wait()
        for t in range(c * (width // LANES), (c + 1) * (width // LANES)):
            pieces = [tab[:, g * GROUP + t * LANES : g * GROUP + (t + 1) * LANES] for g in range(groups)]
            table[t * LANES : (t + 1) * LANES, :] = jnp.transpose(jnp.concatenate(pieces + [blank], axis=0))
    for load in loads:
        load.wait()
    out_ref[FEAT * tiles :, :] = steps[...].astype(F32)
    lane = (lax.broadcasted_iota(jnp.int32, (LANES, LANES), 1) >> 4).astype(F32)
    pick = lax.broadcasted_iota(jnp.int32, (FEAT, LANES), 1) & (FEAT - 1)
    pick = jnp.where(pick == lax.broadcasted_iota(jnp.int32, (FEAT, LANES), 0), 1.0, 0.0).astype(BF16)

    def fetch(t, rows):
        for p in range(LANES):
            rows[p : p + 1, :] = table[pl.ds(idx_ref[t, p] & (GROUP - 1), 1), :]

    def make(t, rows):
        group = (runs[pl.ds(t, 1), :] >> 12).astype(F32)
        group = jnp.transpose(jnp.broadcast_to(group, (LANES, LANES)))
        mine = jnp.where(lane == group, rows[...], 0.0)
        got = None
        for part in thirds(mine):
            moved = lax.dot_general(pick, part.astype(BF16), (((1,), (1,)), ((), ())), preferred_element_type=F32)
            got = moved if got is None else got + moved
        out_ref[pl.ds(t, FEAT, stride=tiles), :] = got

    def pair(h, _):
        fetch(2 * h + 1, rows_b)
        make(2 * h, rows_a)
        fetch(jnp.minimum(2 * h + 2, tiles - 1), rows_a)
        make(2 * h + 1, rows_b)
        return 0

    fetch(0, rows_a)
    lax.fori_loop(0, tiles // 2, pair, 0)


def hbm(x):
    return pltpu.with_memory_space_constraint(x, pltpu.HBM)


def own(run, step, table):
    tiles = run.shape[0]
    ids = VMEM((tiles, LANES), jnp.int32)
    rows = VMEM((LANES, LANES), F32)
    anywhere = pl.BlockSpec(memory_space=pl.ANY)
    return pl.pallas_call(
        own_body,
        out_shape=jax.ShapeDtypeStruct(((FEAT + 1) * tiles, LANES), F32),
        in_specs=[sspec()] + [anywhere] * 3,
        out_specs=vspec(),
        scratch_shapes=[
            VMEM(table.shape, F32),
            VMEM((GROUP, LANES), F32),
            ids,
            ids,
            rows,
            rows,
            pltpu.SemaphoreType.DMA((2 + 4 * (table.shape[1] // GROUP),)),
        ],
        compiler_params=params(8),
        cost_estimate=pl.CostEstimate(flops=tiles * 800000, bytes_accessed=4 * table.size, transcendentals=0),
        name="own",
    )(run, hbm(run), hbm(step), hbm(table))


def operand(f, is_left):
    f = f * math.sqrt(LOG2E)
    a, b, c = thirds(f)
    norm = -0.5 * jnp.sum(f * f, axis=0, keepdims=True)
    if is_left:
        norm = norm + 1.5 * math.log2(8.0)
    na, nb, nc = thirds(norm)
    one = jnp.ones_like(norm)
    if is_left:
        parts = [a, a, b, b, a, c, na, nb, nc, one, one, one]
    else:
        parts = [a, b, a, b, c, a, one, one, one, na, nb, nc]
    return jnp.concatenate(parts + [jnp.zeros((DEPTH - 6 * FEAT - 6, f.shape[1]), F32)], axis=0)


def pack(out_ref, v, tiles):
    clear_rest(out_ref, tiles)
    for t in range(tiles):
        pack_tile(out_ref, v[:, t * LANES : (t + 1) * LANES], t, tiles)


def left_body(feat, b_ref, left, steps, vec, small, scale, packed):
    tiles = feat.shape[0] // (FEAT + 1)
    for t in range(tiles):
        o = slice(t * LANES, (t + 1) * LANES)
        left[o, :] = jnp.transpose(operand(feat[pl.ds(t, FEAT, stride=tiles), :], True)).astype(BF16)
        step = feat[FEAT * tiles + t : FEAT * tiles + t + 1, :] + 8.0
        steps[o, :] = jnp.transpose(jnp.broadcast_to(step, (LANES, LANES)))
    vec[...], small[...], factor = factors(b_ref[...])
    scale[...] = jnp.concatenate([jnp.broadcast_to(factor, (PROBES, LANES)), jnp.zeros((ROWS - PROBES, LANES), F32)], axis=0)
    pack(packed, b_ref[...], tiles)


def left_side(feat, b):
    n = b.shape[1]
    return pl.pallas_call(
        left_body,
        out_shape=(
            VMEM((n, LANES), BF16),
            VMEM((n, LANES), F32),
            VMEM((2 * ROWS, n), BF16),
            VMEM((2 * ROWS, n), F8),
            VMEM((ROWS, LANES), F32),
            jax.ShapeDtypeStruct((SIDE, ROWS, LANES), F32),
        ),
        in_specs=[vspec()] * 2,
        out_specs=(vspec(),) * 6,
        compiler_params=params(4),
        cost_estimate=pl.CostEstimate(flops=n * 1000, bytes_accessed=400 * n, transcendentals=0),
        name="left_side",
    )(feat, b)


def build_body(feat, left, steps, vec, small, scale, b_ref, noise_ref, flag_ref,
               khi_ref, klo_ref, out_ref, right, right_steps, acc, acc8, *, pt, qt):
    n, m = khi_ref.shape
    tiles = m // LANES
    for t in range(tiles):
        o = slice(t * LANES, (t + 1) * LANES)
        right[:, o] = operand(feat[pl.ds(t, FEAT, stride=tiles), :], False).astype(BF16)
        right_steps[0:1, o] = feat[FEAT * tiles + t : FEAT * tiles + t + 1, :]

    def column(jq, _):
        oq = pl.ds(pl.multiple_of(jq * qt, qt), qt)
        right_tile = right[:, oq]
        right_step = right_steps[0:1, oq]
        acc[...] = jnp.zeros_like(acc)
        acc8[...] = jnp.zeros_like(acc8)

        def row(ip, _):
            op = pl.ds(pl.multiple_of(ip * pt, pt), pt)
            power = jnp.dot(left[op, :], right_tile, preferred_element_type=F32)
            spread = jnp.concatenate([steps[op, :]] * (qt // LANES), axis=1) + right_step
            root = lax.rsqrt(spread)
            k = jnp.exp2(power) * (root * (root * root))
            high = k.astype(BF16)
            low = ((k - high.astype(F32)) * LIFT).astype(F8)
            khi_ref[op, oq] = high
            klo_ref[op, oq] = low
            acc[...] += jnp.dot(vec[:, op], high, preferred_element_type=F32)
            acc8[...] += jnp.dot(small[:, op], low, preferred_element_type=F32)
            return 0

        lax.fori_loop(0, n // pt, row, 0, unroll=n // pt)
        res = acc[0:ROWS, :] + acc[ROWS:, :] + scale[:, 0:1] * (acc8[0:ROWS, :] + acc8[ROWS:, :])
        res = res[0:PROBES] + flag_ref[0] * (noise_ref[:, oq] * b_ref[:, oq])
        for t in range(qt // LANES):
            pack_tile(out_ref, res[:, t * LANES : (t + 1) * LANES], jq * (qt // LANES) + t, tiles)
        return 0

    clear_rest(out_ref, tiles)
    lax.fori_loop(0, m // qt, column, 0)


def build(feat, left, steps, vec, small, scale, b, noise, flag, pt=3072, qt=256):
    n = b.shape[1]
    m = feat.shape[0] // (FEAT + 1) * LANES
    return pl.pallas_call(
        functools.partial(build_body, pt=pt, qt=qt),
        out_shape=(VMEM((n, m), BF16), VMEM((n, m), F8), jax.ShapeDtypeStruct((SIDE, ROWS, LANES), F32)),
        in_specs=[vspec()] * 8 + [sspec()],
        out_specs=(vspec(),) * 3,
        scratch_shapes=[
            VMEM((DEPTH, m), BF16),
            VMEM((8, m), F32),
            VMEM((2 * ROWS, qt), F32),
            VMEM((2 * ROWS, qt), F32),
        ],
        compiler_params=params(BUILD),
        cost_estimate=pl.CostEstimate(flops=n * m * 1000, bytes_accessed=n * m * 3, transcendentals=2 * n * m),
        name="build",
    )(feat, left, steps, vec, small, scale, b, noise.reshape(1, n), flag)


def apply_body(khi_ref, klo_ref, w_ref, noise_ref, flag_ref, out_ref, nat, vec, small, *, pt):
    n, m = khi_ref.shape
    unpack(w_ref, nat, m // LANES)
    vec[...], small[...], scale = factors(nat[0:PROBES, :])
    clear_rest(out_ref, n // LANES)
    for s in range(SIDE):
        out_ref[s, ROWS:BOTH, :] = flag_ref[0] * w_ref[s]
    dims = (((1,), (1,)), ((), ()))

    def row(ip, _):
        op = pl.ds(pl.multiple_of(ip * pt, pt), pt)
        y = lax.dot_general(vec[...], khi_ref[op, :], dims, preferred_element_type=F32)
        z = lax.dot_general(small[...], klo_ref[op, :], dims, preferred_element_type=F32)
        res = (y[0:ROWS] + y[ROWS:])[0:PROBES] + scale * (z[0:ROWS] + z[ROWS:])[0:PROBES]
        res = res + flag_ref[0] * (noise_ref[:, op] * nat[0:PROBES, op])
        for t in range(pt // LANES):
            pack_tile(out_ref, res[:, t * LANES : (t + 1) * LANES], ip * (pt // LANES) + t, n // LANES)
        return 0

    lax.fori_loop(0, n // pt, row, 0)


def apply(khi, klo, w, noise, flag, pt=512):
    n, m = khi.shape
    khi = pltpu.with_memory_space_constraint(khi, VMEM)
    klo = pltpu.with_memory_space_constraint(klo, VMEM)
    return pl.pallas_call(
        functools.partial(apply_body, pt=pt),
        out_shape=jax.ShapeDtypeStruct((SIDE, BOTH, LANES), F32),
        in_specs=[vspec()] * 4 + [sspec()],
        out_specs=vspec(),
        scratch_shapes=[VMEM((ROWS, m), F32), VMEM((2 * ROWS, m), BF16), VMEM((2 * ROWS, m), F8)],
        compiler_params=params(4),
        cost_estimate=pl.CostEstimate(flops=n * m * 600, bytes_accessed=n * m * 3, transcendentals=0),
        name="apply",
    )(khi, klo, w, noise.reshape(1, n), flag)


def first_sum_body(in_ref, out_ref):
    total = jnp.sum(in_ref[...], axis=0)
    for s in range(SIDE):
        out_ref[s] = total


def first_sum(got):
    return pl.pallas_call(
        first_sum_body,
        out_shape=jax.ShapeDtypeStruct((SIDE, ROWS, LANES), F32),
        in_specs=[vspec()],
        out_specs=vspec(),
        compiler_params=params(),
        name="first_sum",
    )(got)


def places(which):
    lane = lax.broadcasted_iota(jnp.int32, (ROWS, LANES), 1)
    row = lax.broadcasted_iota(jnp.int32, (ROWS, LANES), 0)
    return lane == jnp.where(which < 8 * 24 // ROWS, row & 7, 8)


def joined(blocks, first):
    def part(k):
        return blocks if k == 0 else pltpu.roll(blocks, LANES - ROWS * k, 1)

    def over(x):
        return jnp.sum(x, axis=0, keepdims=True)

    bb, bw, ww, near, rr, rw, rz, wz = (part(k) for k in range(8))
    all_bb, all_bw, all_ww = over(bb), over(bw), over(ww)
    middle = all_bb / all_bw if first else jnp.where(all_ww > 0.0, all_bw / all_ww, 0.0)
    shift = near - middle
    return (all_bb, all_bw, all_ww, middle, over(rr + shift * (2.0 * rw + shift * ww)), over(rw + shift * ww),
            over(rz + shift * wz), over(wz))


def put(lines):
    lane = lax.broadcasted_iota(jnp.int32, (1, LANES), 1)
    out = jnp.zeros((1, LANES), F32)
    for k, line in enumerate(lines):
        line = jnp.where(lane < PROBES, line, 0.0)
        out = out + (line if k == 0 else pltpu.roll(line, ROWS * k, 1))
    return out


def chunk_body(in_ref, b_ref, which_ref, chunk_ref, line_ref):
    total = jnp.sum(in_ref[...], axis=0)
    chunk_ref[...] = total
    which = which_ref[0]
    b, z, w = b_ref[which], total[0:ROWS], total[ROWS:BOTH]
    here = places(which)

    def dot(x, y):
        return jnp.sum(jnp.where(here, jnp.sum(x * y, axis=1, keepdims=True), 0.0), axis=0, keepdims=True)

    ww, bw = dot(w, w), dot(b, w)
    near = jnp.where(ww > 0.0, bw / ww, 0.0)
    r = b - jnp.sum(jnp.where(here, near, 0.0), axis=1, keepdims=True) * w
    line = put((dot(b, b), bw, ww, near, dot(r, r), dot(r, w), dot(r, z), dot(w, z)))
    for s in range(SIDE):
        line_ref[s] = jnp.broadcast_to(line, (LINES, LANES))


def chunk_sums(got, b, which):
    return pl.pallas_call(
        chunk_body,
        out_shape=(jax.ShapeDtypeStruct((BOTH, LANES), F32), jax.ShapeDtypeStruct((SIDE, LINES, LANES), F32)),
        in_specs=[vspec(), vspec(), sspec()],
        out_specs=(vspec(), vspec()),
        compiler_params=params(),
        name="chunk_sums",
    )(got, b, which)


def join_body(chunk_ref, line_ref, out_ref):
    line = put(joined(jnp.concatenate([line_ref[s, 0:1, :] for s in range(SIDE)], axis=0), False))
    for s in range(SIDE):
        out_ref[s, 0:BOTH, :] = chunk_ref[...]
        out_ref[s, BOTH:MORE, :] = jnp.broadcast_to(line, (MORE - BOTH, LANES))


def join(chunk, line):
    return pl.pallas_call(
        join_body,
        out_shape=jax.ShapeDtypeStruct((SIDE, MORE, LANES), F32),
        in_specs=[vspec(), vspec()],
        out_specs=vspec(),
        compiler_params=params(),
        name="join",
    )(chunk, line)


def finish_body(b_ref, a_ref, x_ref, r_ref, nw, na):
    tiles = b_ref.shape[1] // LANES
    unpack(a_ref, na, tiles)
    unpack(a_ref, nw, tiles, ROWS)
    lines = joined(jnp.concatenate([a_ref[s, BOTH : BOTH + 1, :] for s in range(SIDE)], axis=0), True)
    bb, bw, _, first, rr, rw, rz, _ = (to_column(line, 0) for line in lines)
    beta = rr / bb
    second = rr / ((rw - first * rz) + 2.0 * beta * rw + beta * beta * bw)
    b = b_ref[...]
    w = nw[0:PROBES, :]
    r = b - first * w
    x_ref[...] = first * b + second * (r + beta * b)
    r_ref[...] = r - second * ((w - first * na[0:PROBES, :]) + beta * w)


def finish(b, a):
    n = b.shape[1]
    out = jax.ShapeDtypeStruct((PROBES, n), F32)
    return pl.pallas_call(
        finish_body,
        out_shape=(out, out),
        in_specs=[vspec()] * 2,
        out_specs=(vspec(), vspec()),
        scratch_shapes=[VMEM((ROWS, n), F32), VMEM((ROWS, n), F32)],
        compiler_params=params(),
        name="finish",
    )(b, a)


def on_device(right_side, noise_level, run_index, step_index, run_features):
    swap = [(i * SIDE + j, j * SIDE + i) for i in range(SIDE) for j in range(SIDE)]

    def exchange(x, axis):
        return lax.all_to_all(x, axis, 0, 0)

    flag = (lax.axis_index("row") == lax.axis_index("col")).astype(F32).reshape(1)
    which = lax.axis_index("col").reshape(1)
    tiles = run_index.shape[0] // LANES
    feat = own(run_index.reshape(tiles, LANES), step_index.reshape(tiles, LANES), run_features)
    other = lax.ppermute(feat, ("row", "col"), swap)
    *mine, packed = left_side(feat, right_side)
    khi, klo, part = build(other, *mine, right_side, noise_level, flag)
    product = exchange(first_sum(exchange(part, "row")), "row")
    both = exchange(apply(khi, klo, product, noise_level, flag), "col")
    chunk, line = chunk_sums(both, packed, which)
    again = exchange(join(chunk, exchange(line, "row")), "col")
    return finish(right_side, again)


def solution(mesh):
    return jax.shard_map(
        on_device,
        mesh=mesh,
        in_specs=(P(None, "row"), P("row"), P("row"), P("row"), P()),
        out_specs=(P(None, "row"), P(None, "row")),
        check_vma=False,
    )
```

time: 129 us -> 139 us (1.078)
  blocking collectives: 55.9 us -> 91.3 us
  starting transfers between devices: 16.9 us -> 4.51 us
  Pallas kernels: 43.8 us -> 37.5 us
  waiting for transfers between devices: 6.42 us -> 1.98 us
  other arithmetic: 1.43 us -> 0 us
    all_to_all x4 -> x5, blocking collectives: 55.9 us -> 91.3 us  [exchange(): return lax.all_to_all(x, axis, 0, 0)]
    pallas_call x1, Pallas kernels: 25.3 us -> 17.8 us  [build(): pl.pallas_call(functools.partial(build_body, pt=pt, qt=qt), out_shape=(VM...]
    all_to_all x1 -> x0, starting transfers between devices: 7.08 us -> none  [exchange(): return lax.all_to_all(x, axis, 0, 0)]
    all_to_all x1 -> x0, waiting for transfers between devices: 6.41 us -> none  [exchange(): return lax.all_to_all(x, axis, 0, 0)]
    ppermute x2 -> x1, starting transfers between devices: 9.86 us -> 4.51 us  [on_device(): other = lax.ppermute(feat, ('row', 'col'), swap)]
    ppermute x2 -> x1, waiting for transfers between devices: 0.01 us -> 1.98 us  [on_device(): other = lax.ppermute(feat, ('row', 'col'), swap)]
    pallas_call x4 -> x5, Pallas kernels: 9.14 us -> 11 us  [the longest x1 8.7 us: own(): pl.pallas_call(own_body, out_shape=jax.ShapeDtypeStruct(((FEAT + 1) * til...]
    unnamed x10 -> x6, local copies, waits for them, and re-layouts: 3.04 us -> 2.56 us
  transfers between devices with their start and end apart: 3 -> 1, of which waited for: 1 -> 1; matrix products, arithmetic and copies ran while one was open for 0% -> 0% of each run, Pallas kernels for 14% -> 1%
where the time goes in v3:
time: 139 us; the launch traced here: 138 us
  blocking collectives  91.3 us (66%)
  Pallas kernels  37.5 us (27%)
  starting transfers between devices  4.51 us (3%)
  local copies, waits for them, and re-layouts  2.56 us (2%)
  waiting for transfers between devices  1.98 us (1%)
    all_to_all x5, blocking collectives, exchange(): return lax.all_to_all(x, axis, 0, 0)  91.3 us
    pallas_call x1, Pallas kernels, build(): pl.pallas_call(functools.partial(build_body, pt=pt, qt=qt), out_shape=(VM...  17.8 us
    pallas_call x1, Pallas kernels, own(): pl.pallas_call(own_body, out_shape=jax.ShapeDtypeStruct(((FEAT + 1) * til...  8.7 us
    pallas_call x1, Pallas kernels, apply(): pl.pallas_call(functools.partial(apply_body, pt=pt), out_shape=jax.ShapeD...  8.65 us
    ppermute x1, starting transfers between devices, on_device(): other = lax.ppermute(feat, ('row', 'col'), swap)  4.51 us
  transfers between devices with their start and end apart: 1, of which 1 were waited for; matrix products, arithmetic and copies ran while one was open for 0% of the time, Pallas kernels for 1%

profile of v3, /device:TPU:1, one launch (start us, length us, event | category | flops | bytes accessed | tf_op | source)
XLA Modules:
  0.0 138.4 jit_solution(10411728030921182509)
XLA Ops:
  0.6 8.7 %own.1.feat = f32[408,128]{1,0:T(8,128)S(1)} custom-call(s32[24,128]{1,0:T(8,128)} %bitcast.7, s32[24,128]{1,0:T(8,128)} %bitcast.8, s32[24,128]{1,0:T(8,128)} %bitcast.9, f32[16,24576]{1,0:T(8,128)} %tab_ref.1), custom_call_target="tpu_custom_call" | custom-call | flops 19200000 | bytes 1572864 | tf_op jit(solution)/shard_map/own/pallas_call | solution.py:153
  9.3 4.5 %collective-permute-start = (f32[408,128]{1,0:T(8,128)S(1)}, f32[408,128]{1,0:T(8,128)S(1)}, u32[]{:S(2)}, u32[]{:S(2)}) collective-permute-start(f32[408,128]{1,0:T(8,128)S(1)} %own.1.feat), channel_id=1, source_target_pairs={{0,0},{1,16},{2,32},{3,48},{4,64},{5,80},{6,96},{7,112},{8,128},{9... | collective-permute-start | bytes 626696 | tf_op jit(solution)/shard_map/ppermute | solution.py:458
  13.9 0.0 copy-start
  13.9 0.9 copy-done
  14.8 0.8 left_side.1
  15.6 2.0 %collective-permute-done.feat = f32[408,128]{1,0:T(8,128)S(1)} collective-permute-done((f32[408,128]{1,0:T(8,128)S(1)}, f32[408,128]{1,0:T(8,128)S(1)}, u32[]{:S(2)}, u32[]{:S(2)}) %collective-permute-start) | collective-permute-done | bytes 208928 | tf_op jit(solution)/shard_map/ppermute | solution.py:458
  17.6 0.0 copy-start.1
  17.6 0.9 copy-done.1
  18.5 0.0 copy-start.2
  18.5 0.7 copy-done.2
  19.2 17.8 %build.1 = (bf16[3072,3072]{1,0:T(8,128)(2,1)S(1)}, f8e4m3fn[3072,3072]{1,0:T(32,128)(4,1)S(1)}, f32[16,16,128]{2,1,0:T(8,128)S(1)}) custom-call(f32[408,128]{1,0:T(8,128)S(1)} %collective-permute-done.feat, bf16[3072,128]{1,0:T(8,128)(2,1)S(1)} %get-tuple-element.13.left, f32[3072,128]{1,0:T(8,128)S(1)} %get-tuple-element.14.steps, ...), custom_call_target="tpu_custom_call" | custom-call | flops 9437184000 | bytes 28311552 | tf_op jit(solution)/shard_map/build/pallas_call | solution.py:270
  37.0 38.1 %all_to_all.25.in_ref = f32[16,16,128]{2,1,0:T(8,128)S(1)} all-to-all(f32[16,16,128]{2,1,0:T(8,128)S(1)} %get-tuple-element.20), channel_id=1, replica_groups=mesh['row'=16,'col'=16] {'row'}, dimensions={0} | all-to-all | bytes 262144 | tf_op jit(solution)/shard_map/all_to_all | solution.py:452
  75.1 11.1 %all_to_all.26.w_ref = f32[16,16,128]{2,1,0:T(8,128)S(1)} all-to-all(f32[16,16,128]{2,1,0:T(8,128)S(1)} %first_sum.1), channel_id=1, replica_groups=mesh['row'=16,'col'=16] {'row'}, dimensions={0} | all-to-all | bytes 262144 | tf_op jit(solution)/shard_map/all_to_all | solution.py:452
  86.2 8.7 %apply.1 = f32[16,32,128]{2,1,0:T(8,128)S(1)} custom-call(bf16[3072,3072]{1,0:T(8,128)(2,1)S(1)} %get-tuple-element.18.khi_ref, f8e4m3fn[3072,3072]{1,0:T(32,128)(4,1)S(1)} %get-tuple-element.19.klo_ref, f32[16,16,128]{2,1,0:T(8,128)S(1)} %all_to_all.26.w_ref, f32[1,3072]{1,0:T(1,128)S(1)} %bitcast.6, f32[1]{0:T(128)} %bitcast.3.flag_ref), custom_call_target="tpu_custom_call" | custom-call | flops 5662310400 | bytes 28311552 | tf_op jit(solution)/shard_map/apply/pallas_call | solution.py:313
  94.9 17.7 %all_to_all.27.in_ref = f32[16,32,128]{2,1,0:T(8,128)S(1)} all-to-all(f32[16,32,128]{2,1,0:T(8,128)S(1)} %apply.1), channel_id=1, replica_groups=mesh['row'=16,'col'=16] {'col'}, dimensions={0} | all-to-all | bytes 524288 | tf_op jit(solution)/shard_map/all_to_all | solution.py:452
  112.6 0.3 chunk_sums.1
  112.9 10.6 %all_to_all.28.line_ref = f32[16,8,128]{2,1,0:T(8,128)S(1)} all-to-all(f32[16,8,128]{2,1,0:T(8,128)S(1)} %get-tuple-element.23), channel_id=1, replica_groups=mesh['row'=16,'col'=16] {'row'}, dimensions={0} | all-to-all | bytes 131072 | tf_op jit(solution)/shard_map/all_to_all | solution.py:452
  123.6 0.2 join.1
  123.7 13.7 %all_to_all.29.a_ref = f32[16,40,128]{2,1,0:T(8,128)S(1)} all-to-all(f32[16,40,128]{2,1,0:T(8,128)S(1)} %join.1), channel_id=1, replica_groups=mesh['row'=16,'col'=16] {'col'}, dimensions={0} | all-to-all | bytes 655360 | tf_op jit(solution)/shard_map/all_to_all | solution.py:452
  137.5 1.0 finish.1
  (1 shorter events, 0.0 us)
Async XLA Ops:
  9.3 8.2 %collective-permute-start = (f32[408,128]{1,0:T(8,128)S(1)}, f32[408,128]{1,0:T(8,128)S(1)}, u32[]{:S(2)}, u32[]{:S(2)}) collective-permute-start(f32[408,128]{1,0:T(8,128)S(1)} %own.1.feat), channel_id=1, source_target_pairs={{0,0},{1,16},{2,32},{3,48},{4,64},{5,80},{6,96},{7,112},{8,128},{9... | collective-permute-start | bytes 626696 | tf_op jit(solution)/shard_map/ppermute | solution.py:458
  13.9 0.9 copy-start
  17.6 0.9 copy-start.1
  18.5 0.7 copy-start.2

commit v4 on v3

--- a/solution.py
+++ b/solution.py
@@ -88,86 +88,29 @@
     return halves, small, top * (1.0 / (TOP * LIFT))
 
 
-def own_body(idx_ref, run_ref, step_ref, tab_ref, out_ref, tab, table, runs, steps, rows_a, rows_b, sems):
-    tiles = out_ref.shape[0] // (FEAT + 1)
-    groups = tab_ref.shape[1] // GROUP
-    width = GROUP // 4
-    loads = [pltpu.make_async_copy(run_ref, runs, sems.at[0]), pltpu.make_async_copy(step_ref, steps, sems.at[1])]
-    for load in loads:
-        load.start()
-    parts = []
-    for c in range(4):
-        for g in range(groups):
-            at = pl.ds(g * GROUP + c * width, width)
-            parts.append(pltpu.make_async_copy(tab_ref.at[:, at], tab.at[:, at], sems.at[2 + c * groups + g]))
-    for part in parts:
-        part.start()
-    blank = jnp.zeros((LANES - groups * FEAT, LANES), F32)
-    for c in range(4):
-        for part in parts[c * groups : (c + 1) * groups]:
-            part.wait()
-        for t in range(c * (width // LANES), (c + 1) * (width // LANES)):
-            pieces = [tab[:, g * GROUP + t * LANES : g * GROUP + (t + 1) * LANES] for g in range(groups)]
-            table[t * LANES : (t + 1) * LANES, :] = jnp.transpose(jnp.concatenate(pieces + [blank], axis=0))
-    for load in loads:
-        load.wait()
-    out_ref[FEAT * tiles :, :] = steps[...].astype(F32)
-    lane = (lax.broadcasted_iota(jnp.int32, (LANES, LANES), 1) >> 4).astype(F32)
-    pick = lax.broadcasted_iota(jnp.int32, (FEAT, LANES), 1) & (FEAT - 1)
-    pick = jnp.where(pick == lax.broadcasted_iota(jnp.int32, (FEAT, LANES), 0), 1.0, 0.0).astype(BF16)
-
-    def fetch(t, rows):
+def fetch_features(read, table, runs, rows, use):
+    tiles = rows.shape[0] // LANES
+
+    def fetch(t, _):
+        base = pl.multiple_of(t * LANES, LANES)
         for p in range(LANES):
-            rows[p : p + 1, :] = table[pl.ds(idx_ref[t, p] & (GROUP - 1), 1), :]
-
-    def make(t, rows):
-        group = (runs[pl.ds(t, 1), :] >> 12).astype(F32)
-        group = jnp.transpose(jnp.broadcast_to(group, (LANES, LANES)))
-        mine = jnp.where(lane == group, rows[...], 0.0)
-        got = None
-        for part in thirds(mine):
-            moved = lax.dot_general(pick, part.astype(BF16), (((1,), (1,)), ((), ())), preferred_element_type=F32)
-            got = moved if got is None else got + moved
-        out_ref[pl.ds(t, FEAT, stride=tiles), :] = got
-
-    def pair(h, _):
-        fetch(2 * h + 1, rows_b)
-        make(2 * h, rows_a)
-        fetch(jnp.minimum(2 * h + 2, tiles - 1), rows_a)
-        make(2 * h + 1, rows_b)
+            rows[pl.ds(base + p, 1), :] = table[pl.ds(read(t, p) & (GROUP - 1), 1), :]
         return 0
 
-    fetch(0, rows_a)
-    lax.fori_loop(0, tiles // 2, pair, 0)
-
-
-def hbm(x):
-    return pltpu.with_memory_space_constraint(x, pltpu.HBM)
-
-
-def own(run, step, table):
-    tiles = run.shape[0]
-    ids = VMEM((tiles, LANES), jnp.int32)
-    rows = VMEM((LANES, LANES), F32)
-    anywhere = pl.BlockSpec(memory_space=pl.ANY)
-    return pl.pallas_call(
-        own_body,
-        out_shape=jax.ShapeDtypeStruct(((FEAT + 1) * tiles, LANES), F32),
-        in_specs=[sspec()] + [anywhere] * 3,
-        out_specs=vspec(),
-        scratch_shapes=[
-            VMEM(table.shape, F32),
-            VMEM((GROUP, LANES), F32),
-            ids,
-            ids,
-            rows,
-            rows,
-            pltpu.SemaphoreType.DMA((2 + 4 * (table.shape[1] // GROUP),)),
-        ],
-        compiler_params=params(8),
-        cost_estimate=pl.CostEstimate(flops=tiles * 800000, bytes_accessed=4 * table.size, transcendentals=0),
-        name="own",
-    )(run, hbm(run), hbm(step), hbm(table))
+    lax.fori_loop(0, tiles, fetch, 0)
+    for t in range(tiles):
+        turned = jnp.transpose(rows[t * LANES : (t + 1) * LANES, :])
+        group = runs[t : t + 1, :] >> 12
+        f = turned[0:FEAT]
+        for g in range(1, LANES // FEAT):
+            f = jnp.where(group == g, turned[g * FEAT : (g + 1) * FEAT], f)
+        use(t, f)
+
+
+def pack(out_ref, v, tiles):
+    clear_rest(out_ref, tiles)
+    for t in range(tiles):
+        pack_tile(out_ref, v[:, t * LANES : (t + 1) * LANES], t, tiles)
 
 
 def operand(f, is_left):
@@ -185,29 +128,55 @@
     return jnp.concatenate(parts + [jnp.zeros((DEPTH - 6 * FEAT - 6, f.shape[1]), F32)], axis=0)
 
 
-def pack(out_ref, v, tiles):
-    clear_rest(out_ref, tiles)
-    for t in range(tiles):
-        pack_tile(out_ref, v[:, t * LANES : (t + 1) * LANES], t, tiles)
-
-
-def left_body(feat, b_ref, left, steps, vec, small, scale, packed):
-    tiles = feat.shape[0] // (FEAT + 1)
-    for t in range(tiles):
+def own_body(idx_ref, run_ref, step_ref, tab_ref, b_ref, table, left, steps, vec, small, scale, packed,
+             tab, runs, own_steps, b, rows, sems):
+    groups = tab_ref.shape[1] // GROUP
+    width = GROUP // 4
+    loads = [
+        pltpu.make_async_copy(run_ref, runs, sems.at[0]),
+        pltpu.make_async_copy(step_ref, own_steps, sems.at[1]),
+        pltpu.make_async_copy(b_ref, b, sems.at[2]),
+    ]
+    parts = []
+    for c in range(4):
+        for g in range(groups):
+            at = pl.ds(g * GROUP + c * width, width)
+            parts.append(pltpu.make_async_copy(tab_ref.at[:, at], tab.at[:, at], sems.at[3 + c * groups + g]))
+    for part in parts + loads:
+        part.start()
+    blank = jnp.zeros((LANES - groups * FEAT, LANES), F32)
+    for c in range(4):
+        for part in parts[c * groups : (c + 1) * groups]:
+            part.wait()
+        for t in range(c * (width // LANES), (c + 1) * (width // LANES)):
+            pieces = [tab[:, g * GROUP + t * LANES : g * GROUP + (t + 1) * LANES] for g in range(groups)]
+            table[t * LANES : (t + 1) * LANES, :] = jnp.transpose(jnp.concatenate(pieces + [blank], axis=0))
+    for load in loads:
+        load.wait()
+
+    def use(t, f):
         o = slice(t * LANES, (t + 1) * LANES)
-        left[o, :] = jnp.transpose(operand(feat[pl.ds(t, FEAT, stride=tiles), :], True)).astype(BF16)
-        step = feat[FEAT * tiles + t : FEAT * tiles + t + 1, :] + 8.0
+        left[o, :] = jnp.transpose(operand(f, True)).astype(BF16)
+        step = own_steps[t : t + 1, :].astype(F32) + 8.0
         steps[o, :] = jnp.transpose(jnp.broadcast_to(step, (LANES, LANES)))
-    vec[...], small[...], factor = factors(b_ref[...])
+
+    fetch_features(lambda t, p: idx_ref[t, p], table, runs, rows, use)
+    vec[...], small[...], factor = factors(b[...])
     scale[...] = jnp.concatenate([jnp.broadcast_to(factor, (PROBES, LANES)), jnp.zeros((ROWS - PROBES, LANES), F32)], axis=0)
-    pack(packed, b_ref[...], tiles)
-
-
-def left_side(feat, b):
+    pack(packed, b[...], runs.shape[0])
+
+
+def hbm(x):
+    return pltpu.with_memory_space_constraint(x, pltpu.HBM)
+
+
+def own(run, step, table, b):
     n = b.shape[1]
-    return pl.pallas_call(
-        left_body,
+    ids = VMEM(run.shape, jnp.int32)
+    return pl.pallas_call(
+        own_body,
         out_shape=(
+            VMEM((GROUP, LANES), F32),
             VMEM((n, LANES), BF16),
             VMEM((n, LANES), F32),
             VMEM((2 * ROWS, n), BF16),
@@ -215,22 +184,33 @@
             VMEM((ROWS, LANES), F32),
             jax.ShapeDtypeStruct((SIDE, ROWS, LANES), F32),
         ),
-        in_specs=[vspec()] * 2,
-        out_specs=(vspec(),) * 6,
-        compiler_params=params(4),
-        cost_estimate=pl.CostEstimate(flops=n * 1000, bytes_accessed=400 * n, transcendentals=0),
-        name="left_side",
-    )(feat, b)
-
-
-def build_body(feat, left, steps, vec, small, scale, b_ref, noise_ref, flag_ref,
-               khi_ref, klo_ref, out_ref, right, right_steps, acc, acc8, *, pt, qt):
+        in_specs=[sspec()] + [pl.BlockSpec(memory_space=pl.ANY)] * 4,
+        out_specs=(vspec(),) * 7,
+        scratch_shapes=[
+            VMEM(table.shape, F32),
+            ids,
+            ids,
+            VMEM(b.shape, F32),
+            VMEM((n, LANES), F32),
+            pltpu.SemaphoreType.DMA((3 + 4 * (table.shape[1] // GROUP),)),
+        ],
+        compiler_params=params(12),
+        cost_estimate=pl.CostEstimate(flops=n * 6000, bytes_accessed=4 * table.size, transcendentals=0),
+        name="own",
+    )(run, hbm(run), hbm(step), hbm(table), hbm(b))
+
+
+def build_body(idx_ref, other, table, left, steps, vec, small, scale, b_ref, noise_ref, flag_ref,
+               khi_ref, klo_ref, out_ref, rows, right, right_steps, acc, acc8, *, pt, qt):
     n, m = khi_ref.shape
     tiles = m // LANES
-    for t in range(tiles):
+
+    def use(t, f):
         o = slice(t * LANES, (t + 1) * LANES)
-        right[:, o] = operand(feat[pl.ds(t, FEAT, stride=tiles), :], False).astype(BF16)
-        right_steps[0:1, o] = feat[FEAT * tiles + t : FEAT * tiles + t + 1, :]
+        right[:, o] = operand(f, False).astype(BF16)
+        right_steps[0:1, o] = other[1, t : t + 1, :].astype(F32)
+
+    fetch_features(lambda t, p: idx_ref[0, t, p], table, other.at[0], rows, use)
 
     def column(jq, _):
         oq = pl.ds(pl.multiple_of(jq * qt, qt), qt)
@@ -264,15 +244,16 @@
     lax.fori_loop(0, m // qt, column, 0)
 
 
-def build(feat, left, steps, vec, small, scale, b, noise, flag, pt=3072, qt=256):
+def build(other, table, left, steps, vec, small, scale, b, noise, flag, pt=3072, qt=256):
     n = b.shape[1]
-    m = feat.shape[0] // (FEAT + 1) * LANES
+    m = other.shape[1] * LANES
     return pl.pallas_call(
         functools.partial(build_body, pt=pt, qt=qt),
         out_shape=(VMEM((n, m), BF16), VMEM((n, m), F8), jax.ShapeDtypeStruct((SIDE, ROWS, LANES), F32)),
-        in_specs=[vspec()] * 8 + [sspec()],
+        in_specs=[sspec()] + [vspec()] * 9 + [sspec()],
         out_specs=(vspec(),) * 3,
         scratch_shapes=[
+            VMEM((m, LANES), F32),
             VMEM((DEPTH, m), BF16),
             VMEM((8, m), F32),
             VMEM((2 * ROWS, qt), F32),
@@ -281,7 +262,7 @@
         compiler_params=params(BUILD),
         cost_estimate=pl.CostEstimate(flops=n * m * 1000, bytes_accessed=n * m * 3, transcendentals=2 * n * m),
         name="build",
-    )(feat, left, steps, vec, small, scale, b, noise.reshape(1, n), flag)
+    )(other, other, table, left, steps, vec, small, scale, b, noise.reshape(1, n), flag)
 
 
 def apply_body(khi_ref, klo_ref, w_ref, noise_ref, flag_ref, out_ref, nat, vec, small, *, pt):
@@ -454,9 +435,10 @@
     flag = (lax.axis_index("row") == lax.axis_index("col")).astype(F32).reshape(1)
     which = lax.axis_index("col").reshape(1)
     tiles = run_index.shape[0] // LANES
-    feat = own(run_index.reshape(tiles, LANES), step_index.reshape(tiles, LANES), run_features)
-    other = lax.ppermute(feat, ("row", "col"), swap)
-    *mine, packed = left_side(feat, right_side)
+    run = run_index.reshape(tiles, LANES)
+    step = step_index.reshape(tiles, LANES)
+    other = lax.ppermute(jnp.stack([run, step]), ("row", "col"), swap)
+    *mine, packed = own(run, step, run_features, right_side)
     khi, klo, part = build(other, *mine, right_side, noise_level, flag)
     product = exchange(first_sum(exchange(part, "row")), "row")
     both = exchange(apply(khi, klo, product, noise_level, flag), "col")

time: 139 us -> 121 us (0.87)
  blocking collectives: 91.3 us -> 72.2 us
  Pallas kernels: 37.5 us -> 41.1 us
  waiting for transfers between devices: 1.98 us -> 0.01 us
    all_to_all x5, blocking collectives: 91.3 us -> 72.2 us  [exchange(): return lax.all_to_all(x, axis, 0, 0)]
    pallas_call x1, Pallas kernels: 17.8 us -> 22.4 us  [build(): pl.pallas_call(functools.partial(build_body, pt=pt, qt=qt), out_shape=(VM...]
    ppermute x1, waiting for transfers between devices: 1.98 us -> 0.01 us  [on_device(): other = lax.ppermute(jnp.stack([run, step]), ('row', 'col'), swap)]
    pallas_call x2 -> x1, Pallas kernels: 9.48 us -> 8.56 us  [own(): pl.pallas_call(own_body, out_shape=(VMEM((GROUP, LANES), F32), VMEM((n, L...]
  transfers between devices with their start and end apart: 1 -> 1, of which waited for: 1 -> 0; matrix products, arithmetic and copies ran while one was open for 0% -> 0% of each run, Pallas kernels for 1% -> 7%
where the time goes in v4:
time: 121 us
  blocking collectives  72.2 us (60%)
  Pallas kernels  41.1 us (34%)
  starting transfers between devices  4.5 us (4%)
  local copies, waits for them, and re-layouts  1.63 us (1%)
    all_to_all x5, blocking collectives, exchange(): return lax.all_to_all(x, axis, 0, 0)  72.2 us
    pallas_call x1, Pallas kernels, build(): pl.pallas_call(functools.partial(build_body, pt=pt, qt=qt), out_shape=(VM...  22.4 us
    pallas_call x1, Pallas kernels, apply(): pl.pallas_call(functools.partial(apply_body, pt=pt), out_shape=jax.ShapeD...  8.65 us
    pallas_call x1, Pallas kernels, own(): pl.pallas_call(own_body, out_shape=(VMEM((GROUP, LANES), F32), VMEM((n, L...  8.56 us
    ppermute x1, starting transfers between devices, on_device(): other = lax.ppermute(jnp.stack([run, step]), ('row', 'col'), swap)  4.5 us
  transfers between devices with their start and end apart: 1, of which 0 were waited for; matrix products, arithmetic and copies ran while one was open for 0% of the time, Pallas kernels for 7%

profile of v4, /device:TPU:1, one launch (start us, length us, event | category | flops | bytes accessed | tf_op | source)
XLA Modules:
  0.0 120.9 jit_solution(17948134682377960009)
XLA Ops:
  0.6 0.7 pad_add_fusion
  1.4 4.5 %collective-permute-start = (s32[2,24,128]{2,1,0:T(8,128)S(1)}, s32[2,24,128]{2,1,0:T(8,128)S(1)}, u32[]{:S(2)}, u32[]{:S(2)}) collective-permute-start(s32[2,24,128]{2,1,0:T(8,128)S(1)} %pad_add_fusion), channel_id=1, source_target_pairs={{0,0},{1,16},{2,32},{3,48},{4,64},{5,80},{6,96},{7,112},{8,128},{9... | collective-permute-start | bytes 73736 | tf_op jit(solution)/shard_map/ppermute | solution.py:440
  5.9 8.6 %own.1 = (f32[4096,128]{1,0:T(8,128)S(1)}, bf16[3072,128]{1,0:T(8,128)(2,1)S(1)}, f32[3072,128]{1,0:T(8,128)S(1)}, bf16[32,3072]{1,0:T(8,128)(2,1)S(1)}, f8e4m3f...) custom-call(s32[24,128]{1,0:T(8,128)} %bitcast.10, s32[24,128]{1,0:T(8,128)} %bitcast.11, ...), custom_call_target="tpu_custom_call" | custom-call | flops 18432000 | bytes 1572864 | tf_op jit(solution)/shard_map/own/pallas_call | solution.py:176
  14.4 0.0 collective-permute-done.idx_ref.other
  14.4 0.0 copy-start
  14.5 0.9 copy-done
  15.4 0.0 copy-start.1
  15.4 0.7 copy-done.1
  16.1 22.4 %build.1 = (bf16[3072,3072]{1,0:T(8,128)(2,1)S(1)}, f8e4m3fn[3072,3072]{1,0:T(32,128)(4,1)S(1)}, f32[16,16,128]{2,1,0:T(8,128)S(1)}) custom-call(s32[2,24,128]{2,1,0:T(8,128)S(1)} %collective-permute-done.idx_ref.other, s32[2,24,128]{2,1,0:T(8,128)S(1)} %collective-permute-done.idx_ref.other, f32[4096,128]{1,0:T(8,128)S(1)} %get-tuple-element.14.table, ...), custom_call_target="tpu_custom_call" | custom-call | flops 9437184000 | bytes 28311552 | tf_op jit(solution)/shard_map/build/pallas_call | solution.py:250
  38.5 17.8 %all_to_all.25.in_ref = f32[16,16,128]{2,1,0:T(8,128)S(1)} all-to-all(f32[16,16,128]{2,1,0:T(8,128)S(1)} %get-tuple-element.22), channel_id=1, replica_groups=mesh['row'=16,'col'=16] {'row'}, dimensions={0} | all-to-all | bytes 262144 | tf_op jit(solution)/shard_map/all_to_all | solution.py:433
  56.3 11.1 %all_to_all.26.w_ref = f32[16,16,128]{2,1,0:T(8,128)S(1)} all-to-all(f32[16,16,128]{2,1,0:T(8,128)S(1)} %first_sum.1), channel_id=1, replica_groups=mesh['row'=16,'col'=16] {'row'}, dimensions={0} | all-to-all | bytes 262144 | tf_op jit(solution)/shard_map/all_to_all | solution.py:433
  67.4 8.6 %apply.1 = f32[16,32,128]{2,1,0:T(8,128)S(1)} custom-call(bf16[3072,3072]{1,0:T(8,128)(2,1)S(1)} %get-tuple-element.20.khi_ref, f8e4m3fn[3072,3072]{1,0:T(32,128)(4,1)S(1)} %get-tuple-element.21.klo_ref, f32[16,16,128]{2,1,0:T(8,128)S(1)} %all_to_all.26.w_ref, f32[1,3072]{1,0:T(1,128)S(1)} %bitcast.8, f32[1]{0:T(128)} %bitcast.5.flag_ref), custom_call_target="tpu_custom_call" | custom-call | flops 5662310400 | bytes 28311552 | tf_op jit(solution)/shard_map/apply/pallas_call | solution.py:294
  76.1 18.9 %all_to_all.27.in_ref = f32[16,32,128]{2,1,0:T(8,128)S(1)} all-to-all(f32[16,32,128]{2,1,0:T(8,128)S(1)} %apply.1), channel_id=1, replica_groups=mesh['row'=16,'col'=16] {'col'}, dimensions={0} | all-to-all | bytes 524288 | tf_op jit(solution)/shard_map/all_to_all | solution.py:433
  95.0 0.3 chunk_sums.1
  95.4 10.6 %all_to_all.28.line_ref = f32[16,8,128]{2,1,0:T(8,128)S(1)} all-to-all(f32[16,8,128]{2,1,0:T(8,128)S(1)} %get-tuple-element.25), channel_id=1, replica_groups=mesh['row'=16,'col'=16] {'row'}, dimensions={0} | all-to-all | bytes 131072 | tf_op jit(solution)/shard_map/all_to_all | solution.py:433
  106.0 0.2 join.1
  106.2 13.7 %all_to_all.29.a_ref = f32[16,40,128]{2,1,0:T(8,128)S(1)} all-to-all(f32[16,40,128]{2,1,0:T(8,128)S(1)} %join.1), channel_id=1, replica_groups=mesh['row'=16,'col'=16] {'col'}, dimensions={0} | all-to-all | bytes 655360 | tf_op jit(solution)/shard_map/all_to_all | solution.py:433
  119.9 1.0 finish.1
  (1 shorter events, 0.0 us)
Async XLA Ops:
  1.4 13.1 %collective-permute-start = (s32[2,24,128]{2,1,0:T(8,128)S(1)}, s32[2,24,128]{2,1,0:T(8,128)S(1)}, u32[]{:S(2)}, u32[]{:S(2)}) collective-permute-start(s32[2,24,128]{2,1,0:T(8,128)S(1)} %pad_add_fusion), channel_id=1, source_target_pairs={{0,0},{1,16},{2,32},{3,48},{4,64},{5,80},{6,96},{7,112},{8,128},{9... | collective-permute-start | bytes 73736 | tf_op jit(solution)/shard_map/ppermute | solution.py:440
  14.4 0.9 copy-start
  15.4 0.7 copy-start.1

commit v5 on v4

--- a/solution.py
+++ b/solution.py
@@ -3,6 +3,7 @@
 
 import jax
 import jax.numpy as jnp
+import numpy as np
 from jax import lax
 from jax.experimental import pallas as pl
 from jax.experimental.pallas import tpu as pltpu
@@ -18,7 +19,9 @@
 MORE = 40
 LINES = 8
 GROUP = 4096
-DEPTH = 128
+DEPTH = 256
+RANK = 24
+STEPS = 128
 LOG2E = 1.4426950408889634
 F32 = jnp.float32
 BF16 = jnp.bfloat16
@@ -88,23 +91,18 @@
     return halves, small, top * (1.0 / (TOP * LIFT))
 
 
-def fetch_features(read, table, runs, rows, use):
-    tiles = rows.shape[0] // LANES
-
-    def fetch(t, _):
-        base = pl.multiple_of(t * LANES, LANES)
-        for p in range(LANES):
-            rows[pl.ds(base + p, 1), :] = table[pl.ds(read(t, p) & (GROUP - 1), 1), :]
-        return 0
-
-    lax.fori_loop(0, tiles, fetch, 0)
-    for t in range(tiles):
-        turned = jnp.transpose(rows[t * LANES : (t + 1) * LANES, :])
-        group = runs[t : t + 1, :] >> 12
-        f = turned[0:FEAT]
-        for g in range(1, LANES // FEAT):
-            f = jnp.where(group == g, turned[g * FEAT : (g + 1) * FEAT], f)
-        use(t, f)
+def fetch(read, table, rows, t, at):
+    for p in range(LANES):
+        rows[pl.ds(at + p, 1), :] = table[pl.ds(read(t, p) & (GROUP - 1), 1), :]
+
+
+def turn(rows, run):
+    turned = jnp.transpose(rows)
+    group = run >> 12
+    f = turned[0:FEAT]
+    for g in range(1, LANES // FEAT):
+        f = jnp.where(group == g, turned[g * FEAT : (g + 1) * FEAT], f)
+    return f
 
 
 def pack(out_ref, v, tiles):
@@ -118,30 +116,34 @@
     a, b, c = thirds(f)
     norm = -0.5 * jnp.sum(f * f, axis=0, keepdims=True)
     if is_left:
-        norm = norm + 1.5 * math.log2(8.0)
+        norm = norm + math.log2(LIFT)
     na, nb, nc = thirds(norm)
     one = jnp.ones_like(norm)
     if is_left:
         parts = [a, a, b, b, a, c, na, nb, nc, one, one, one]
     else:
         parts = [a, b, a, b, c, a, one, one, one, na, nb, nc]
-    return jnp.concatenate(parts + [jnp.zeros((DEPTH - 6 * FEAT - 6, f.shape[1]), F32)], axis=0)
-
-
-def own_body(idx_ref, run_ref, step_ref, tab_ref, b_ref, table, left, steps, vec, small, scale, packed,
-             tab, runs, own_steps, b, rows, sems):
+    return jnp.concatenate(parts + [jnp.zeros((2, f.shape[1]), F32)], axis=0)
+
+
+def own_body(idx_ref, flag_ref, run_ref, step_ref, tab_ref, b_ref, noise_ref, decay_ref, right_ref,
+             right_decay, table, left, vec, small, scale, extra_b, extra, packed,
+             tab, runs, own_steps, b, noise, decay, rows, sems):
     groups = tab_ref.shape[1] // GROUP
     width = GROUP // 4
     loads = [
         pltpu.make_async_copy(run_ref, runs, sems.at[0]),
         pltpu.make_async_copy(step_ref, own_steps, sems.at[1]),
         pltpu.make_async_copy(b_ref, b, sems.at[2]),
+        pltpu.make_async_copy(noise_ref, noise, sems.at[3]),
+        pltpu.make_async_copy(decay_ref, decay, sems.at[4]),
+        pltpu.make_async_copy(right_ref, right_decay, sems.at[5]),
     ]
     parts = []
     for c in range(4):
         for g in range(groups):
             at = pl.ds(g * GROUP + c * width, width)
-            parts.append(pltpu.make_async_copy(tab_ref.at[:, at], tab.at[:, at], sems.at[3 + c * groups + g]))
+            parts.append(pltpu.make_async_copy(tab_ref.at[:, at], tab.at[:, at], sems.at[6 + c * groups + g]))
     for part in parts + loads:
         part.start()
     blank = jnp.zeros((LANES - groups * FEAT, LANES), F32)
@@ -154,79 +156,113 @@
     for load in loads:
         load.wait()
 
-    def use(t, f):
+    tiles = runs.shape[0]
+
+    def get(t, _):
+        fetch(lambda t, p: idx_ref[t, p], table, rows, t, pl.multiple_of(t * LANES, LANES))
+        return 0
+
+    lax.fori_loop(0, tiles, get, 0)
+    for t in range(tiles):
         o = slice(t * LANES, (t + 1) * LANES)
-        left[o, :] = jnp.transpose(operand(f, True)).astype(BF16)
-        step = own_steps[t : t + 1, :].astype(F32) + 8.0
-        steps[o, :] = jnp.transpose(jnp.broadcast_to(step, (LANES, LANES)))
-
-    fetch_features(lambda t, p: idx_ref[t, p], table, runs, rows, use)
+        f = turn(rows[o, :], runs[t : t + 1, :])
+        hot = one_hot(own_steps[t : t + 1, :])
+        terms = jnp.dot(decay[...].astype(BF16), hot, preferred_element_type=F32)
+        left[o, 0:LANES] = jnp.transpose(jnp.concatenate([operand(f, True), terms], axis=0)).astype(BF16)
+        left[o, LANES:] = jnp.transpose(hot.astype(F32)).astype(BF16)
     vec[...], small[...], factor = factors(b[...])
     scale[...] = jnp.concatenate([jnp.broadcast_to(factor, (PROBES, LANES)), jnp.zeros((ROWS - PROBES, LANES), F32)], axis=0)
-    pack(packed, b[...], runs.shape[0])
+    pack(packed, b[...], tiles)
+    extra[...] = flag_ref[0] * noise[...]
+    extra_b[...] = flag_ref[0] * noise[...] * b[...]
+
+
+def decay_tables():
+    rest = np.array([[-1.5 * math.log2((s + t + 8.0) / 8.0) for t in range(STEPS)] for s in range(STEPS)])
+
+    def rounded(x):
+        return x.astype(BF16).astype(np.float64)
+
+    left, right = [], []
+    for _ in range(RANK):
+        s, t = divmod(int(np.argmax(np.abs(rest))), STEPS)
+        a, b = rounded(rest[:, t] / rest[s, t]), rounded(rest[s, :])
+        left.append(a)
+        right.append(b)
+        rest = rest - np.outer(a, b)
+    return np.array(left).astype(np.float32), np.concatenate([np.array(right), rounded(rest)]).astype(np.float32)
+
+
+def one_hot(step):
+    row = lax.broadcasted_iota(jnp.int32, (STEPS, LANES), 0)
+    return jnp.where(row == step, 1.0, 0.0).astype(BF16)
 
 
 def hbm(x):
     return pltpu.with_memory_space_constraint(x, pltpu.HBM)
 
 
-def own(run, step, table, b):
+def own(run, step, table, b, noise, flag, decay, right_decay):
     n = b.shape[1]
     ids = VMEM(run.shape, jnp.int32)
     return pl.pallas_call(
         own_body,
         out_shape=(
+            VMEM(right_decay.shape, F32),
             VMEM((GROUP, LANES), F32),
-            VMEM((n, LANES), BF16),
-            VMEM((n, LANES), F32),
+            VMEM((n, DEPTH), BF16),
             VMEM((2 * ROWS, n), BF16),
             VMEM((2 * ROWS, n), F8),
             VMEM((ROWS, LANES), F32),
+            VMEM((PROBES, n), F32),
+            VMEM((1, n), F32),
             jax.ShapeDtypeStruct((SIDE, ROWS, LANES), F32),
         ),
-        in_specs=[sspec()] + [pl.BlockSpec(memory_space=pl.ANY)] * 4,
-        out_specs=(vspec(),) * 7,
+        in_specs=[sspec()] * 2 + [pl.BlockSpec(memory_space=pl.ANY)] * 7,
+        out_specs=(vspec(),) * 9,
         scratch_shapes=[
             VMEM(table.shape, F32),
             ids,
             ids,
             VMEM(b.shape, F32),
+            VMEM((1, n), F32),
+            VMEM(decay.shape, F32),
             VMEM((n, LANES), F32),
-            pltpu.SemaphoreType.DMA((3 + 4 * (table.shape[1] // GROUP),)),
+            pltpu.SemaphoreType.DMA((6 + 4 * (table.shape[1] // GROUP),)),
         ],
         compiler_params=params(12),
         cost_estimate=pl.CostEstimate(flops=n * 6000, bytes_accessed=4 * table.size, transcendentals=0),
         name="own",
-    )(run, hbm(run), hbm(step), hbm(table), hbm(b))
-
-
-def build_body(idx_ref, other, table, left, steps, vec, small, scale, b_ref, noise_ref, flag_ref,
-               khi_ref, klo_ref, out_ref, rows, right, right_steps, acc, acc8, *, pt, qt):
+    )(run, flag, *(hbm(x) for x in (run, step, table, b, noise.reshape(1, n), decay, right_decay)))
+
+
+def build_body(idx_ref, other, decay, table, left, vec, small, scale, extra_b,
+               khi_ref, klo_ref, out_ref, rows, right, acc, acc8, *, pt, qt):
     n, m = khi_ref.shape
     tiles = m // LANES
-
-    def use(t, f):
-        o = slice(t * LANES, (t + 1) * LANES)
-        right[:, o] = operand(f, False).astype(BF16)
-        right_steps[0:1, o] = other[1, t : t + 1, :].astype(F32)
-
-    fetch_features(lambda t, p: idx_ref[0, t, p], table, other.at[0], rows, use)
+    per = qt // LANES
+
+    def ready(jq, slot):
+        for k in range(per):
+            t = jq * per + k
+            o = slice(k * LANES, (k + 1) * LANES)
+            fetch(lambda t, p: idx_ref[0, t, p], table, rows, t, k * LANES)
+            f = turn(rows[o, :], other[0, pl.ds(t, 1), :])
+            terms = jnp.dot(decay[...].astype(BF16), one_hot(other[1, pl.ds(t, 1), :]), preferred_element_type=F32)
+            right[slot, :, o] = jnp.concatenate([operand(f, False), terms], axis=0).astype(BF16)
 
     def column(jq, _):
         oq = pl.ds(pl.multiple_of(jq * qt, qt), qt)
-        right_tile = right[:, oq]
-        right_step = right_steps[0:1, oq]
+        right_tile = right[jq % 2]
         acc[...] = jnp.zeros_like(acc)
         acc8[...] = jnp.zeros_like(acc8)
 
         def row(ip, _):
             op = pl.ds(pl.multiple_of(ip * pt, pt), pt)
             power = jnp.dot(left[op, :], right_tile, preferred_element_type=F32)
-            spread = jnp.concatenate([steps[op, :]] * (qt // LANES), axis=1) + right_step
-            root = lax.rsqrt(spread)
-            k = jnp.exp2(power) * (root * (root * root))
+            k = jnp.exp2(power)
             high = k.astype(BF16)
-            low = ((k - high.astype(F32)) * LIFT).astype(F8)
+            low = (k - high.astype(F32)).astype(BF16).astype(F8)
             khi_ref[op, oq] = high
             klo_ref[op, oq] = low
             acc[...] += jnp.dot(vec[:, op], high, preferred_element_type=F32)
@@ -234,38 +270,39 @@
             return 0
 
         lax.fori_loop(0, n // pt, row, 0, unroll=n // pt)
-        res = acc[0:ROWS, :] + acc[ROWS:, :] + scale[:, 0:1] * (acc8[0:ROWS, :] + acc8[ROWS:, :])
-        res = res[0:PROBES] + flag_ref[0] * (noise_ref[:, oq] * b_ref[:, oq])
+        res = (acc[0:ROWS, :] + acc[ROWS:, :]) * (1.0 / LIFT) + scale[:, 0:1] * (acc8[0:ROWS, :] + acc8[ROWS:, :])
+        res = res[0:PROBES] + extra_b[:, oq]
         for t in range(qt // LANES):
             pack_tile(out_ref, res[:, t * LANES : (t + 1) * LANES], jq * (qt // LANES) + t, tiles)
+        ready(jnp.minimum(jq + 1, m // qt - 1), (jq + 1) % 2)
         return 0
 
     clear_rest(out_ref, tiles)
+    ready(0, 0)
     lax.fori_loop(0, m // qt, column, 0)
 
 
-def build(other, table, left, steps, vec, small, scale, b, noise, flag, pt=3072, qt=256):
-    n = b.shape[1]
+def build(other, decay, table, left, vec, small, scale, extra_b, pt=3072, qt=256):
+    n = left.shape[0]
     m = other.shape[1] * LANES
     return pl.pallas_call(
         functools.partial(build_body, pt=pt, qt=qt),
         out_shape=(VMEM((n, m), BF16), VMEM((n, m), F8), jax.ShapeDtypeStruct((SIDE, ROWS, LANES), F32)),
-        in_specs=[sspec()] + [vspec()] * 9 + [sspec()],
+        in_specs=[sspec()] + [vspec()] * 8,
         out_specs=(vspec(),) * 3,
         scratch_shapes=[
-            VMEM((m, LANES), F32),
-            VMEM((DEPTH, m), BF16),
-            VMEM((8, m), F32),
+            VMEM((qt, LANES), F32),
+            VMEM((2, DEPTH, qt), BF16),
             VMEM((2 * ROWS, qt), F32),
             VMEM((2 * ROWS, qt), F32),
         ],
         compiler_params=params(BUILD),
         cost_estimate=pl.CostEstimate(flops=n * m * 1000, bytes_accessed=n * m * 3, transcendentals=2 * n * m),
         name="build",
-    )(other, other, table, left, steps, vec, small, scale, b, noise.reshape(1, n), flag)
-
-
-def apply_body(khi_ref, klo_ref, w_ref, noise_ref, flag_ref, out_ref, nat, vec, small, *, pt):
+    )(other, other, decay, table, left, vec, small, scale, extra_b)
+
+
+def apply_body(khi_ref, klo_ref, w_ref, extra, flag_ref, out_ref, nat, vec, small, *, pt):
     n, m = khi_ref.shape
     unpack(w_ref, nat, m // LANES)
     vec[...], small[...], scale = factors(nat[0:PROBES, :])
@@ -278,8 +315,8 @@
         op = pl.ds(pl.multiple_of(ip * pt, pt), pt)
         y = lax.dot_general(vec[...], khi_ref[op, :], dims, preferred_element_type=F32)
         z = lax.dot_general(small[...], klo_ref[op, :], dims, preferred_element_type=F32)
-        res = (y[0:ROWS] + y[ROWS:])[0:PROBES] + scale * (z[0:ROWS] + z[ROWS:])[0:PROBES]
-        res = res + flag_ref[0] * (noise_ref[:, op] * nat[0:PROBES, op])
+        res = (y[0:ROWS] + y[ROWS:])[0:PROBES] * (1.0 / LIFT) + scale * (z[0:ROWS] + z[ROWS:])[0:PROBES]
+        res = res + extra[:, op] * nat[0:PROBES, op]
         for t in range(pt // LANES):
             pack_tile(out_ref, res[:, t * LANES : (t + 1) * LANES], ip * (pt // LANES) + t, n // LANES)
         return 0
@@ -287,7 +324,7 @@
     lax.fori_loop(0, n // pt, row, 0)
 
 
-def apply(khi, klo, w, noise, flag, pt=512):
+def apply(khi, klo, w, extra, flag, pt=512):
     n, m = khi.shape
     khi = pltpu.with_memory_space_constraint(khi, VMEM)
     klo = pltpu.with_memory_space_constraint(klo, VMEM)
@@ -300,7 +337,7 @@
         compiler_params=params(4),
         cost_estimate=pl.CostEstimate(flops=n * m * 600, bytes_accessed=n * m * 3, transcendentals=0),
         name="apply",
-    )(khi, klo, w, noise.reshape(1, n), flag)
+    )(khi, klo, w, extra, flag)
 
 
 def first_sum_body(in_ref, out_ref):
@@ -438,10 +475,11 @@
     run = run_index.reshape(tiles, LANES)
     step = step_index.reshape(tiles, LANES)
     other = lax.ppermute(jnp.stack([run, step]), ("row", "col"), swap)
-    *mine, packed = own(run, step, run_features, right_side)
-    khi, klo, part = build(other, *mine, right_side, noise_level, flag)
+    decays = (jnp.asarray(x) for x in decay_tables())
+    *mine, extra, packed = own(run, step, run_features, right_side, noise_level, flag, *decays)
+    khi, klo, part = build(other, *mine)
     product = exchange(first_sum(exchange(part, "row")), "row")
-    both = exchange(apply(khi, klo, product, noise_level, flag), "col")
+    both = exchange(apply(khi, klo, product, extra, flag), "col")
     chunk, line = chunk_sums(both, packed, which)
     again = exchange(join(chunk, exchange(line, "row")), "col")
     return finish(right_side, again)

time: 121 us -> 115 us (0.950)
  Pallas kernels: 41.1 us -> 36.5 us
  local copies, waits for them, and re-layouts: 1.63 us -> 0.01 us
    pallas_call x1, Pallas kernels: 22.4 us -> 18.9 us  [build(): pl.pallas_call(functools.partial(build_body, pt=pt, qt=qt), out_shape=(VM...]
    unnamed x4 -> x2, local copies, waits for them, and re-layouts: 1.63 us -> 0.01 us
  transfers between devices with their start and end apart: 1 -> 1, of which waited for: 0 -> 0; matrix products, arithmetic and copies ran while one was open for 0% -> 0% of each run, Pallas kernels for 7% -> 6%
where the time goes in v5:
time: 115 us
  blocking collectives  72.3 us (63%)
  Pallas kernels  36.5 us (32%)
  starting transfers between devices  4.5 us (4%)
    all_to_all x5, blocking collectives, exchange(): return lax.all_to_all(x, axis, 0, 0)  72.3 us
    pallas_call x1, Pallas kernels, build(): pl.pallas_call(functools.partial(build_body, pt=pt, qt=qt), out_shape=(VM...  18.9 us
    pallas_call x1, Pallas kernels, apply(): pl.pallas_call(functools.partial(apply_body, pt=pt), out_shape=jax.ShapeD...  8.65 us
    pallas_call x1, Pallas kernels, own(): pl.pallas_call(own_body, out_shape=(VMEM(right_decay.shape, F32), VMEM((G...  7.42 us
    ppermute x1, starting transfers between devices, on_device(): other = lax.ppermute(jnp.stack([run, step]), ('row', 'col'), swap)  4.5 us
  transfers between devices with their start and end apart: 1, of which 0 were waited for; matrix products, arithmetic and copies ran while one was open for 0% of the time, Pallas kernels for 6%

profile of v5, /device:TPU:1, one launch (start us, length us, event | category | flops | bytes accessed | tf_op | source)
XLA Modules:
  0.0 114.8 jit_solution(519192801146817669)
XLA Ops:
  0.6 0.7 pad_add_fusion
  1.4 4.5 %collective-permute-start = (s32[2,24,128]{2,1,0:T(8,128)S(1)}, s32[2,24,128]{2,1,0:T(8,128)S(1)}, u32[]{:S(2)}, u32[]{:S(2)}) collective-permute-start(s32[2,24,128]{2,1,0:T(8,128)S(1)} %pad_add_fusion), channel_id=1, source_target_pairs={{0,0},{1,16},{2,32},{3,48},{4,64},{5,80},{6,96},{7,112},{8,128},{9... | collective-permute-start | bytes 73736 | tf_op jit(solution)/shard_map/ppermute | solution.py:477
  5.9 7.4 %own.1 = (f32[152,128]{1,0:T(8,128)S(1)}, f32[4096,128]{1,0:T(8,128)S(1)}, bf16[3072,256]{1,0:T(8,128)(2,1)S(1)}, bf16[32,3072]{1,0:T(8,128)(2,1)S(1)}, f8e4m3fn...) custom-call(s32[24,128]{1,0:T(8,128)} %bitcast.8, ...), custom_call_target="tpu_custom_call" | custom-call | flops 18432000 | bytes 1572864 | tf_op jit(solution)/shard_map/own/pallas_call | solution.py:208
  13.3 0.0 collective-permute-done.idx_ref.other
  13.3 18.9 %build.1 = (bf16[3072,3072]{1,0:T(8,128)(2,1)S(1)}, f8e4m3fn[3072,3072]{1,0:T(32,128)(4,1)S(1)}, f32[16,16,128]{2,1,0:T(8,128)S(1)}) custom-call(s32[2,24,128]{2,1,0:T(8,128)S(1)} %collective-permute-done.idx_ref.other, s32[2,24,128]{2,1,0:T(8,128)S(1)} %collective-permute-done.idx_ref.other, f32[152,128]{1,0:T(8,128)S(1)} %get-tuple-element.16.decay, ...), custom_call_target="tpu_custom_call" | custom-call | flops 9437184000 | bytes 28311552 | tf_op jit(solution)/shard_map/build/pallas_call | solution.py:288
  32.2 18.6 %all_to_all.25.in_ref = f32[16,16,128]{2,1,0:T(8,128)S(1)} all-to-all(f32[16,16,128]{2,1,0:T(8,128)S(1)} %get-tuple-element.25), channel_id=1, replica_groups=mesh['row'=16,'col'=16] {'row'}, dimensions={0} | all-to-all | bytes 262144 | tf_op jit(solution)/shard_map/all_to_all | solution.py:470
  50.9 11.1 %all_to_all.26.w_ref = f32[16,16,128]{2,1,0:T(8,128)S(1)} all-to-all(f32[16,16,128]{2,1,0:T(8,128)S(1)} %first_sum.1), channel_id=1, replica_groups=mesh['row'=16,'col'=16] {'row'}, dimensions={0} | all-to-all | bytes 262144 | tf_op jit(solution)/shard_map/all_to_all | solution.py:470
  62.0 8.7 %apply.1 = f32[16,32,128]{2,1,0:T(8,128)S(1)} custom-call(bf16[3072,3072]{1,0:T(8,128)(2,1)S(1)} %get-tuple-element.23.khi_ref, f8e4m3fn[3072,3072]{1,0:T(32,128)(4,1)S(1)} %get-tuple-element.24.klo_ref, f32[16,16,128]{2,1,0:T(8,128)S(1)} %all_to_all.26.w_ref, f32[1,3072]{1,0:T(1,128)S(1)} %get-tuple-element.26.extra, f32[1]{0:T(128)} %bitcast.3.flag_ref), custom_call_target="tpu_custom_call" | custom-call | flops 5662310400 | bytes 28311552 | tf_op jit(solution)/shard_map/apply/pallas_call | solution.py:331
  70.7 0.0 copy-start
  70.7 18.3 %all_to_all.27.in_ref = f32[16,32,128]{2,1,0:T(8,128)S(1)} all-to-all(f32[16,32,128]{2,1,0:T(8,128)S(1)} %apply.1), channel_id=1, replica_groups=mesh['row'=16,'col'=16] {'col'}, dimensions={0} | all-to-all | bytes 524288 | tf_op jit(solution)/shard_map/all_to_all | solution.py:470
  88.9 0.3 chunk_sums.1
  89.3 10.6 %all_to_all.28.line_ref = f32[16,8,128]{2,1,0:T(8,128)S(1)} all-to-all(f32[16,8,128]{2,1,0:T(8,128)S(1)} %get-tuple-element.29), channel_id=1, replica_groups=mesh['row'=16,'col'=16] {'row'}, dimensions={0} | all-to-all | bytes 131072 | tf_op jit(solution)/shard_map/all_to_all | solution.py:470
  99.9 0.2 join.1
  100.1 13.7 %all_to_all.29.a_ref = f32[16,40,128]{2,1,0:T(8,128)S(1)} all-to-all(f32[16,40,128]{2,1,0:T(8,128)S(1)} %join.1), channel_id=1, replica_groups=mesh['row'=16,'col'=16] {'col'}, dimensions={0} | all-to-all | bytes 655360 | tf_op jit(solution)/shard_map/all_to_all | solution.py:470
  113.8 0.0 copy-done
  113.8 1.0 finish.1
  (1 shorter events, 0.0 us)
Async XLA Ops:
  1.4 11.9 %collective-permute-start = (s32[2,24,128]{2,1,0:T(8,128)S(1)}, s32[2,24,128]{2,1,0:T(8,128)S(1)}, u32[]{:S(2)}, u32[]{:S(2)}) collective-permute-start(s32[2,24,128]{2,1,0:T(8,128)S(1)} %pad_add_fusion), channel_id=1, source_target_pairs={{0,0},{1,16},{2,32},{3,48},{4,64},{5,80},{6,96},{7,112},{8,128},{9... | collective-permute-start | bytes 73736 | tf_op jit(solution)/shard_map/ppermute | solution.py:477
  70.7 43.1 %copy-start = (f32[9,3072]{1,0:T(8,128)S(1)}, f32[9,3072]{1,0:T(8,128)}, u32[]{:S(2)}) copy-start(f32[9,3072]{1,0:T(8,128)} %b_ref.3) | copy-start | bytes 331780

commit v6 on v5

--- a/solution.py
+++ b/solution.py
@@ -14,7 +14,7 @@
 FEAT = 16
 PROBES = 9
 ROWS = 16
-BUILD = 8
+BUILD = 12
 BOTH = 32
 MORE = 40
 LINES = 8
@@ -127,25 +127,36 @@
 
 
 def own_body(idx_ref, flag_ref, run_ref, step_ref, tab_ref, b_ref, noise_ref, decay_ref, right_ref,
-             right_decay, table, left, vec, small, scale, extra_b, extra, packed,
-             tab, runs, own_steps, b, noise, decay, rows, sems):
+             ids, right_decay, table, left, vec, small, scale, extra_b, extra, packed,
+             tab, b, noise, decay, terms, rows, sems):
     groups = tab_ref.shape[1] // GROUP
     width = GROUP // 4
-    loads = [
-        pltpu.make_async_copy(run_ref, runs, sems.at[0]),
-        pltpu.make_async_copy(step_ref, own_steps, sems.at[1]),
-        pltpu.make_async_copy(b_ref, b, sems.at[2]),
-        pltpu.make_async_copy(noise_ref, noise, sems.at[3]),
-        pltpu.make_async_copy(decay_ref, decay, sems.at[4]),
-        pltpu.make_async_copy(right_ref, right_decay, sems.at[5]),
-    ]
+    tiles = run_ref.shape[0]
+    pairs = [(step_ref, ids.at[1]), (decay_ref, decay), (b_ref, b), (noise_ref, noise), (run_ref, ids.at[0])]
+    pairs.append((right_ref, right_decay))
+    loads = [pltpu.make_async_copy(src, dst, sems.at[k]) for k, (src, dst) in enumerate(pairs)]
     parts = []
     for c in range(4):
         for g in range(groups):
             at = pl.ds(g * GROUP + c * width, width)
             parts.append(pltpu.make_async_copy(tab_ref.at[:, at], tab.at[:, at], sems.at[6 + c * groups + g]))
-    for part in parts + loads:
+    for part in loads + parts:
         part.start()
+    loads[0].wait()
+    loads[1].wait()
+    table_left = decay[...].astype(BF16)
+    for t in range(tiles):
+        o = slice(t * LANES, (t + 1) * LANES)
+        hot = one_hot(ids[1, t : t + 1, :])
+        terms[:, o] = jnp.dot(table_left, hot, preferred_element_type=F32)
+        left[o, LANES:] = jnp.transpose(hot.astype(F32)).astype(BF16)
+    loads[2].wait()
+    loads[3].wait()
+    vec[...], small[...], factor = factors(b[...])
+    scale[...] = jnp.concatenate([jnp.broadcast_to(factor, (PROBES, LANES)), jnp.zeros((ROWS - PROBES, LANES), F32)], axis=0)
+    pack(packed, b[...], tiles)
+    extra[...] = flag_ref[0] * noise[...]
+    extra_b[...] = flag_ref[0] * noise[...] * b[...]
     blank = jnp.zeros((LANES - groups * FEAT, LANES), F32)
     for c in range(4):
         for part in parts[c * groups : (c + 1) * groups]:
@@ -153,10 +164,8 @@
         for t in range(c * (width // LANES), (c + 1) * (width // LANES)):
             pieces = [tab[:, g * GROUP + t * LANES : g * GROUP + (t + 1) * LANES] for g in range(groups)]
             table[t * LANES : (t + 1) * LANES, :] = jnp.transpose(jnp.concatenate(pieces + [blank], axis=0))
-    for load in loads:
-        load.wait()
-
-    tiles = runs.shape[0]
+    loads[4].wait()
+    loads[5].wait()
 
     def get(t, _):
         fetch(lambda t, p: idx_ref[t, p], table, rows, t, pl.multiple_of(t * LANES, LANES))
@@ -165,16 +174,8 @@
     lax.fori_loop(0, tiles, get, 0)
     for t in range(tiles):
         o = slice(t * LANES, (t + 1) * LANES)
-        f = turn(rows[o, :], runs[t : t + 1, :])
-        hot = one_hot(own_steps[t : t + 1, :])
-        terms = jnp.dot(decay[...].astype(BF16), hot, preferred_element_type=F32)
-        left[o, 0:LANES] = jnp.transpose(jnp.concatenate([operand(f, True), terms], axis=0)).astype(BF16)
-        left[o, LANES:] = jnp.transpose(hot.astype(F32)).astype(BF16)
-    vec[...], small[...], factor = factors(b[...])
-    scale[...] = jnp.concatenate([jnp.broadcast_to(factor, (PROBES, LANES)), jnp.zeros((ROWS - PROBES, LANES), F32)], axis=0)
-    pack(packed, b[...], tiles)
-    extra[...] = flag_ref[0] * noise[...]
-    extra_b[...] = flag_ref[0] * noise[...] * b[...]
+        f = turn(rows[o, :], ids[0, t : t + 1, :])
+        left[o, 0:LANES] = jnp.transpose(jnp.concatenate([operand(f, True), terms[:, o]], axis=0)).astype(BF16)
 
 
 def decay_tables():
@@ -204,10 +205,10 @@
 
 def own(run, step, table, b, noise, flag, decay, right_decay):
     n = b.shape[1]
-    ids = VMEM(run.shape, jnp.int32)
     return pl.pallas_call(
         own_body,
         out_shape=(
+            VMEM((2, *run.shape), jnp.int32),
             VMEM(right_decay.shape, F32),
             VMEM((GROUP, LANES), F32),
             VMEM((n, DEPTH), BF16),
@@ -219,14 +220,13 @@
             jax.ShapeDtypeStruct((SIDE, ROWS, LANES), F32),
         ),
         in_specs=[sspec()] * 2 + [pl.BlockSpec(memory_space=pl.ANY)] * 7,
-        out_specs=(vspec(),) * 9,
+        out_specs=(vspec(),) * 10,
         scratch_shapes=[
             VMEM(table.shape, F32),
-            ids,
-            ids,
             VMEM(b.shape, F32),
             VMEM((1, n), F32),
             VMEM(decay.shape, F32),
+            VMEM((RANK, n), F32),
             VMEM((n, LANES), F32),
             pltpu.SemaphoreType.DMA((6 + 4 * (table.shape[1] // GROUP),)),
         ],
@@ -282,7 +282,7 @@
     lax.fori_loop(0, m // qt, column, 0)
 
 
-def build(other, decay, table, left, vec, small, scale, extra_b, pt=3072, qt=256):
+def build(other, decay, table, left, vec, small, scale, extra_b, pt=3072, qt=512):
     n = left.shape[0]
     m = other.shape[1] * LANES
     return pl.pallas_call(
@@ -474,10 +474,9 @@
     tiles = run_index.shape[0] // LANES
     run = run_index.reshape(tiles, LANES)
     step = step_index.reshape(tiles, LANES)
-    other = lax.ppermute(jnp.stack([run, step]), ("row", "col"), swap)
     decays = (jnp.asarray(x) for x in decay_tables())
-    *mine, extra, packed = own(run, step, run_features, right_side, noise_level, flag, *decays)
-    khi, klo, part = build(other, *mine)
+    ids, *mine, extra, packed = own(run, step, run_features, right_side, noise_level, flag, *decays)
+    khi, klo, part = build(lax.ppermute(ids, ("row", "col"), swap), *mine)
     product = exchange(first_sum(exchange(part, "row")), "row")
     both = exchange(apply(khi, klo, product, extra, flag), "col")
     chunk, line = chunk_sums(both, packed, which)

time: 115 us -> 118 us (1.026)
  blocking collectives: 72.3 us -> 76.7 us
  Pallas kernels: 36.5 us -> 34.4 us
  waiting for transfers between devices: 0.01 us -> 1.5 us
    all_to_all x5, blocking collectives: 72.3 us -> 76.7 us  [exchange(): return lax.all_to_all(x, axis, 0, 0)]
    pallas_call x1, Pallas kernels: 18.9 us -> 16.5 us  [build(): pl.pallas_call(functools.partial(build_body, pt=pt, qt=qt), out_shape=(VM...]
    ppermute x1, waiting for transfers between devices: 0.01 us -> 1.5 us  [on_device(): khi, klo, part = build(lax.ppermute(ids, ('row', 'col'), swap), *mine)]
  transfers between devices with their start and end apart: 1 -> 1, of which waited for: 0 -> 1; matrix products, arithmetic and copies ran while one was open for 0% -> 0% of each run, Pallas kernels for 6% -> 0%
where the time goes in v6:
time: 118 us
  blocking collectives  76.7 us (65%)
  Pallas kernels  34.4 us (29%)
  starting transfers between devices  4.51 us (4%)
  waiting for transfers between devices  1.5 us (1%)
    all_to_all x5, blocking collectives, exchange(): return lax.all_to_all(x, axis, 0, 0)  76.7 us
    pallas_call x1, Pallas kernels, build(): pl.pallas_call(functools.partial(build_body, pt=pt, qt=qt), out_shape=(VM...  16.5 us
    pallas_call x1, Pallas kernels, apply(): pl.pallas_call(functools.partial(apply_body, pt=pt), out_shape=jax.ShapeD...  8.65 us
    pallas_call x1, Pallas kernels, own(): pl.pallas_call(own_body, out_shape=(VMEM((2, *run.shape), jnp.int32), VME...  7.72 us
    ppermute x1, starting transfers between devices, on_device(): khi, klo, part = build(lax.ppermute(ids, ('row', 'col'), swap), *mine)  4.51 us
  transfers between devices with their start and end apart: 1, of which 1 were waited for; matrix products, arithmetic and copies ran while one was open for 0% of the time, Pallas kernels for 0%

profile of v6, /device:TPU:1, one launch (start us, length us, event | category | flops | bytes accessed | tf_op | source)
XLA Modules:
  0.0 117.7 jit_solution(15855060456954377370)
XLA Ops:
  0.6 7.7 %own.1 = (s32[2,24,128]{2,1,0:T(8,128)S(1)}, f32[152,128]{1,0:T(8,128)S(1)}, f32[4096,128]{1,0:T(8,128)S(1)}, bf16[3072,256]{1,0:T(8,128)(2,1)S(1)}, bf16[32,307...) custom-call(s32[24,128]{1,0:T(8,128)} %bitcast.5, ...), custom_call_target="tpu_custom_call" | custom-call | flops 18432000 | bytes 1572864 | tf_op jit(solution)/shard_map/own/pallas_call | solution.py:208
  8.4 4.5 %collective-permute-start = (s32[2,24,128]{2,1,0:T(8,128)S(1)}, s32[2,24,128]{2,1,0:T(8,128)S(1)}, u32[]{:S(2)}, u32[]{:S(2)}) collective-permute-start(s32[2,24,128]{2,1,0:T(8,128)S(1)} %get-tuple-element.17), channel_id=1, source_target_pairs={{0,0},{1,16},{2,32},{3,48},{4,64},{5,80},{6,96},{7,112},{8,128},{9... | collective-permute-start | bytes 73736 | tf_op jit(solution)/shard_map/ppermute | solution.py:479
  12.9 1.5 %collective-permute-done.idx_ref.other = s32[2,24,128]{2,1,0:T(8,128)S(1)} collective-permute-done((s32[2,24,128]{2,1,0:T(8,128)S(1)}, s32[2,24,128]{2,1,0:T(8,128)S(1)}, u32[]{:S(2)}, u32[]{:S(2)}) %collective-permute-start) | collective-permute-done | bytes 24608 | tf_op jit(solution)/shard_map/ppermute | solution.py:479
  14.4 16.5 %build.1 = (bf16[3072,3072]{1,0:T(8,128)(2,1)S(1)}, f8e4m3fn[3072,3072]{1,0:T(32,128)(4,1)S(1)}, f32[16,16,128]{2,1,0:T(8,128)S(1)}) custom-call(s32[2,24,128]{2,1,0:T(8,128)S(1)} %collective-permute-done.idx_ref.other, s32[2,24,128]{2,1,0:T(8,128)S(1)} %collective-permute-done.idx_ref.other, f32[152,128]{1,0:T(8,128)S(1)} %get-tuple-element.18.decay, ...), custom_call_target="tpu_custom_call" | custom-call | flops 9437184000 | bytes 28311552 | tf_op jit(solution)/shard_map/build/pallas_call | solution.py:288
  30.9 24.5 %all_to_all.25.in_ref = f32[16,16,128]{2,1,0:T(8,128)S(1)} all-to-all(f32[16,16,128]{2,1,0:T(8,128)S(1)} %get-tuple-element.27), channel_id=1, replica_groups=mesh['row'=16,'col'=16] {'row'}, dimensions={0} | all-to-all | bytes 262144 | tf_op jit(solution)/shard_map/all_to_all | solution.py:470
  55.4 11.1 %all_to_all.26.w_ref = f32[16,16,128]{2,1,0:T(8,128)S(1)} all-to-all(f32[16,16,128]{2,1,0:T(8,128)S(1)} %first_sum.1), channel_id=1, replica_groups=mesh['row'=16,'col'=16] {'row'}, dimensions={0} | all-to-all | bytes 262144 | tf_op jit(solution)/shard_map/all_to_all | solution.py:470
  66.5 8.7 %apply.1 = f32[16,32,128]{2,1,0:T(8,128)S(1)} custom-call(bf16[3072,3072]{1,0:T(8,128)(2,1)S(1)} %get-tuple-element.25.khi_ref, f8e4m3fn[3072,3072]{1,0:T(32,128)(4,1)S(1)} %get-tuple-element.26.klo_ref, f32[16,16,128]{2,1,0:T(8,128)S(1)} %all_to_all.26.w_ref, f32[1,3072]{1,0:T(1,128)S(1)} %get-tuple-element.28.extra, f32[1]{0:T(128)} %bitcast.1.flag_ref), custom_call_target="tpu_custom_call" | custom-call | flops 5662310400 | bytes 28311552 | tf_op jit(solution)/shard_map/apply/pallas_call | solution.py:331
  75.2 0.0 copy-start
  75.2 16.7 %all_to_all.27.in_ref = f32[16,32,128]{2,1,0:T(8,128)S(1)} all-to-all(f32[16,32,128]{2,1,0:T(8,128)S(1)} %apply.1), channel_id=1, replica_groups=mesh['row'=16,'col'=16] {'col'}, dimensions={0} | all-to-all | bytes 524288 | tf_op jit(solution)/shard_map/all_to_all | solution.py:470
  91.9 0.3 chunk_sums.1
  92.2 10.6 %all_to_all.28.line_ref = f32[16,8,128]{2,1,0:T(8,128)S(1)} all-to-all(f32[16,8,128]{2,1,0:T(8,128)S(1)} %get-tuple-element.31), channel_id=1, replica_groups=mesh['row'=16,'col'=16] {'row'}, dimensions={0} | all-to-all | bytes 131072 | tf_op jit(solution)/shard_map/all_to_all | solution.py:470
  102.9 0.2 join.1
  103.0 13.7 %all_to_all.29.a_ref = f32[16,40,128]{2,1,0:T(8,128)S(1)} all-to-all(f32[16,40,128]{2,1,0:T(8,128)S(1)} %join.1), channel_id=1, replica_groups=mesh['row'=16,'col'=16] {'col'}, dimensions={0} | all-to-all | bytes 655360 | tf_op jit(solution)/shard_map/all_to_all | solution.py:470
  116.8 0.0 copy-done
  116.8 1.0 finish.1
  (1 shorter events, 0.0 us)
Async XLA Ops:
  8.4 6.0 %collective-permute-start = (s32[2,24,128]{2,1,0:T(8,128)S(1)}, s32[2,24,128]{2,1,0:T(8,128)S(1)}, u32[]{:S(2)}, u32[]{:S(2)}) collective-permute-start(s32[2,24,128]{2,1,0:T(8,128)S(1)} %get-tuple-element.17), channel_id=1, source_target_pairs={{0,0},{1,16},{2,32},{3,48},{4,64},{5,80},{6,96},{7,112},{8,128},{9... | collective-permute-start | bytes 73736 | tf_op jit(solution)/shard_map/ppermute | solution.py:479
  75.2 41.6 %copy-start = (f32[9,3072]{1,0:T(8,128)S(1)}, f32[9,3072]{1,0:T(8,128)}, u32[]{:S(2)}) copy-start(f32[9,3072]{1,0:T(8,128)} %b_ref.3) | copy-start | bytes 331780

commit v7 on v6

--- a/solution.py
+++ b/solution.py
@@ -127,8 +127,8 @@
 
 
 def own_body(idx_ref, flag_ref, run_ref, step_ref, tab_ref, b_ref, noise_ref, decay_ref, right_ref,
-             ids, right_decay, table, left, vec, small, scale, extra_b, extra, packed,
-             tab, b, noise, decay, terms, rows, sems):
+             right_decay, table, left, vec, small, scale, extra_b, extra, packed,
+             ids, tab, b, noise, decay, terms, rows, sems):
     groups = tab_ref.shape[1] // GROUP
     width = GROUP // 4
     tiles = run_ref.shape[0]
@@ -208,7 +208,6 @@
     return pl.pallas_call(
         own_body,
         out_shape=(
-            VMEM((2, *run.shape), jnp.int32),
             VMEM(right_decay.shape, F32),
             VMEM((GROUP, LANES), F32),
             VMEM((n, DEPTH), BF16),
@@ -220,8 +219,9 @@
             jax.ShapeDtypeStruct((SIDE, ROWS, LANES), F32),
         ),
         in_specs=[sspec()] * 2 + [pl.BlockSpec(memory_space=pl.ANY)] * 7,
-        out_specs=(vspec(),) * 10,
+        out_specs=(vspec(),) * 9,
         scratch_shapes=[
+            VMEM((2, *run.shape), jnp.int32),
             VMEM(table.shape, F32),
             VMEM(b.shape, F32),
             VMEM((1, n), F32),
@@ -475,8 +475,9 @@
     run = run_index.reshape(tiles, LANES)
     step = step_index.reshape(tiles, LANES)
     decays = (jnp.asarray(x) for x in decay_tables())
-    ids, *mine, extra, packed = own(run, step, run_features, right_side, noise_level, flag, *decays)
-    khi, klo, part = build(lax.ppermute(ids, ("row", "col"), swap), *mine)
+    other = lax.ppermute(jnp.stack([run, step]), ("row", "col"), swap)
+    *mine, extra, packed = own(run, step, run_features, right_side, noise_level, flag, *decays)
+    khi, klo, part = build(other, *mine)
     product = exchange(first_sum(exchange(part, "row")), "row")
     both = exchange(apply(khi, klo, product, extra, flag), "col")
     chunk, line = chunk_sums(both, packed, which)

time: 118 us -> 113 us (0.958)
  blocking collectives: 76.7 us -> 72.3 us
  waiting for transfers between devices: 1.5 us -> 0.01 us
    all_to_all x5, blocking collectives: 76.7 us -> 72.3 us  [exchange(): return lax.all_to_all(x, axis, 0, 0)]
    ppermute x1, waiting for transfers between devices: 1.5 us -> 0.01 us  [on_device(): other = lax.ppermute(jnp.stack([run, step]), ('row', 'col'), swap)]
  transfers between devices with their start and end apart: 1 -> 1, of which waited for: 1 -> 0; matrix products, arithmetic and copies ran while one was open for 0% -> 0% of each run, Pallas kernels for 0% -> 7%
where the time goes in v7:
time: 113 us; the launch traced here: 112 us
  blocking collectives  72.3 us (64%)
  Pallas kernels  33.9 us (30%)
  starting transfers between devices  4.5 us (4%)
    all_to_all x5, blocking collectives, exchange(): return lax.all_to_all(x, axis, 0, 0)  72.3 us
    pallas_call x1, Pallas kernels, build(): pl.pallas_call(functools.partial(build_body, pt=pt, qt=qt), out_shape=(VM...  16 us
    pallas_call x1, Pallas kernels, apply(): pl.pallas_call(functools.partial(apply_body, pt=pt), out_shape=jax.ShapeD...  8.65 us
    pallas_call x1, Pallas kernels, own(): pl.pallas_call(own_body, out_shape=(VMEM(right_decay.shape, F32), VMEM((G...  7.73 us
    ppermute x1, starting transfers between devices, on_device(): other = lax.ppermute(jnp.stack([run, step]), ('row', 'col'), swap)  4.5 us
  transfers between devices with their start and end apart: 1, of which 0 were waited for; matrix products, arithmetic and copies ran while one was open for 0% of the time, Pallas kernels for 7%

profile of v7, /device:TPU:1, one launch (start us, length us, event | category | flops | bytes accessed | tf_op | source)
XLA Modules:
  0.0 112.2 jit_solution(2853861988377393774)
XLA Ops:
  0.6 0.7 pad_add_fusion
  1.4 4.5 %collective-permute-start = (s32[2,24,128]{2,1,0:T(8,128)S(1)}, s32[2,24,128]{2,1,0:T(8,128)S(1)}, u32[]{:S(2)}, u32[]{:S(2)}) collective-permute-start(s32[2,24,128]{2,1,0:T(8,128)S(1)} %pad_add_fusion), channel_id=1, source_target_pairs={{0,0},{1,16},{2,32},{3,48},{4,64},{5,80},{6,96},{7,112},{8,128},{9... | collective-permute-start | bytes 73736 | tf_op jit(solution)/shard_map/ppermute | solution.py:478
  5.9 7.7 %own.1 = (f32[152,128]{1,0:T(8,128)S(1)}, f32[4096,128]{1,0:T(8,128)S(1)}, bf16[3072,256]{1,0:T(8,128)(2,1)S(1)}, bf16[32,3072]{1,0:T(8,128)(2,1)S(1)}, f8e4m3fn...) custom-call(s32[24,128]{1,0:T(8,128)} %bitcast.8, ...), custom_call_target="tpu_custom_call" | custom-call | flops 18432000 | bytes 1572864 | tf_op jit(solution)/shard_map/own/pallas_call | solution.py:208
  13.6 0.0 collective-permute-done.idx_ref.other
  13.6 16.0 %build.1 = (bf16[3072,3072]{1,0:T(8,128)(2,1)S(1)}, f8e4m3fn[3072,3072]{1,0:T(32,128)(4,1)S(1)}, f32[16,16,128]{2,1,0:T(8,128)S(1)}) custom-call(s32[2,24,128]{2,1,0:T(8,128)S(1)} %collective-permute-done.idx_ref.other, s32[2,24,128]{2,1,0:T(8,128)S(1)} %collective-permute-done.idx_ref.other, f32[152,128]{1,0:T(8,128)S(1)} %get-tuple-element.16.decay, ...), custom_call_target="tpu_custom_call" | custom-call | flops 9437184000 | bytes 28311552 | tf_op jit(solution)/shard_map/build/pallas_call | solution.py:288
  29.6 18.3 %all_to_all.25.in_ref = f32[16,16,128]{2,1,0:T(8,128)S(1)} all-to-all(f32[16,16,128]{2,1,0:T(8,128)S(1)} %get-tuple-element.25), channel_id=1, replica_groups=mesh['row'=16,'col'=16] {'row'}, dimensions={0} | all-to-all | bytes 262144 | tf_op jit(solution)/shard_map/all_to_all | solution.py:470
  47.9 11.1 %all_to_all.26.w_ref = f32[16,16,128]{2,1,0:T(8,128)S(1)} all-to-all(f32[16,16,128]{2,1,0:T(8,128)S(1)} %first_sum.1), channel_id=1, replica_groups=mesh['row'=16,'col'=16] {'row'}, dimensions={0} | all-to-all | bytes 262144 | tf_op jit(solution)/shard_map/all_to_all | solution.py:470
  59.0 8.7 %apply.1 = f32[16,32,128]{2,1,0:T(8,128)S(1)} custom-call(bf16[3072,3072]{1,0:T(8,128)(2,1)S(1)} %get-tuple-element.23.khi_ref, f8e4m3fn[3072,3072]{1,0:T(32,128)(4,1)S(1)} %get-tuple-element.24.klo_ref, f32[16,16,128]{2,1,0:T(8,128)S(1)} %all_to_all.26.w_ref, f32[1,3072]{1,0:T(1,128)S(1)} %get-tuple-element.26.extra, f32[1]{0:T(128)} %bitcast.3.flag_ref), custom_call_target="tpu_custom_call" | custom-call | flops 5662310400 | bytes 28311552 | tf_op jit(solution)/shard_map/apply/pallas_call | solution.py:331
  67.7 0.0 copy-start
  67.7 18.6 %all_to_all.27.in_ref = f32[16,32,128]{2,1,0:T(8,128)S(1)} all-to-all(f32[16,32,128]{2,1,0:T(8,128)S(1)} %apply.1), channel_id=1, replica_groups=mesh['row'=16,'col'=16] {'col'}, dimensions={0} | all-to-all | bytes 524288 | tf_op jit(solution)/shard_map/all_to_all | solution.py:470
  86.3 0.3 chunk_sums.1
  86.7 10.6 %all_to_all.28.line_ref = f32[16,8,128]{2,1,0:T(8,128)S(1)} all-to-all(f32[16,8,128]{2,1,0:T(8,128)S(1)} %get-tuple-element.29), channel_id=1, replica_groups=mesh['row'=16,'col'=16] {'row'}, dimensions={0} | all-to-all | bytes 131072 | tf_op jit(solution)/shard_map/all_to_all | solution.py:470
  97.3 0.2 join.1
  97.5 13.7 %all_to_all.29.a_ref = f32[16,40,128]{2,1,0:T(8,128)S(1)} all-to-all(f32[16,40,128]{2,1,0:T(8,128)S(1)} %join.1), channel_id=1, replica_groups=mesh['row'=16,'col'=16] {'col'}, dimensions={0} | all-to-all | bytes 655360 | tf_op jit(solution)/shard_map/all_to_all | solution.py:470
  111.2 0.0 copy-done
  111.2 1.0 finish.1
  (1 shorter events, 0.0 us)
Async XLA Ops:
  1.4 12.3 %collective-permute-start = (s32[2,24,128]{2,1,0:T(8,128)S(1)}, s32[2,24,128]{2,1,0:T(8,128)S(1)}, u32[]{:S(2)}, u32[]{:S(2)}) collective-permute-start(s32[2,24,128]{2,1,0:T(8,128)S(1)} %pad_add_fusion), channel_id=1, source_target_pairs={{0,0},{1,16},{2,32},{3,48},{4,64},{5,80},{6,96},{7,112},{8,128},{9... | collective-permute-start | bytes 73736 | tf_op jit(solution)/shard_map/ppermute | solution.py:478
  67.7 43.5 %copy-start = (f32[9,3072]{1,0:T(8,128)S(1)}, f32[9,3072]{1,0:T(8,128)}, u32[]{:S(2)}) copy-start(f32[9,3072]{1,0:T(8,128)} %b_ref.3) | copy-start | bytes 331780

commit v8 on v7

--- a/solution.py
+++ b/solution.py
@@ -93,12 +93,11 @@
 
 def fetch(read, table, rows, t, at):
     for p in range(LANES):
-        rows[pl.ds(at + p, 1), :] = table[pl.ds(read(t, p) & (GROUP - 1), 1), :]
-
-
-def turn(rows, run):
+        rows[pl.ds(at + p, 1), :] = table[pl.ds(read(t, p), 1), :]
+
+
+def turn(rows, group):
     turned = jnp.transpose(rows)
-    group = run >> 12
     f = turned[0:FEAT]
     for g in range(1, LANES // FEAT):
         f = jnp.where(group == g, turned[g * FEAT : (g + 1) * FEAT], f)
@@ -126,20 +125,19 @@
     return jnp.concatenate(parts + [jnp.zeros((2, f.shape[1]), F32)], axis=0)
 
 
-def own_body(idx_ref, flag_ref, run_ref, step_ref, tab_ref, b_ref, noise_ref, decay_ref, right_ref,
+def own_body(idx_ref, flag_ref, ids_ref, tab_ref, b_ref, noise_ref, decay_ref, right_ref,
              right_decay, table, left, vec, small, scale, extra_b, extra, packed,
              ids, tab, b, noise, decay, terms, rows, sems):
     groups = tab_ref.shape[1] // GROUP
     width = GROUP // 4
-    tiles = run_ref.shape[0]
-    pairs = [(step_ref, ids.at[1]), (decay_ref, decay), (b_ref, b), (noise_ref, noise), (run_ref, ids.at[0])]
-    pairs.append((right_ref, right_decay))
+    tiles = ids_ref.shape[1]
+    pairs = [(ids_ref, ids), (decay_ref, decay), (b_ref, b), (noise_ref, noise), (right_ref, right_decay)]
     loads = [pltpu.make_async_copy(src, dst, sems.at[k]) for k, (src, dst) in enumerate(pairs)]
     parts = []
     for c in range(4):
         for g in range(groups):
             at = pl.ds(g * GROUP + c * width, width)
-            parts.append(pltpu.make_async_copy(tab_ref.at[:, at], tab.at[:, at], sems.at[6 + c * groups + g]))
+            parts.append(pltpu.make_async_copy(tab_ref.at[:, at], tab.at[:, at], sems.at[5 + c * groups + g]))
     for part in loads + parts:
         part.start()
     loads[0].wait()
@@ -147,7 +145,7 @@
     table_left = decay[...].astype(BF16)
     for t in range(tiles):
         o = slice(t * LANES, (t + 1) * LANES)
-        hot = one_hot(ids[1, t : t + 1, :])
+        hot = one_hot(ids[2, t : t + 1, :])
         terms[:, o] = jnp.dot(table_left, hot, preferred_element_type=F32)
         left[o, LANES:] = jnp.transpose(hot.astype(F32)).astype(BF16)
     loads[2].wait()
@@ -165,16 +163,15 @@
             pieces = [tab[:, g * GROUP + t * LANES : g * GROUP + (t + 1) * LANES] for g in range(groups)]
             table[t * LANES : (t + 1) * LANES, :] = jnp.transpose(jnp.concatenate(pieces + [blank], axis=0))
     loads[4].wait()
-    loads[5].wait()
 
     def get(t, _):
-        fetch(lambda t, p: idx_ref[t, p], table, rows, t, pl.multiple_of(t * LANES, LANES))
+        fetch(lambda t, p: idx_ref[0, t, p], table, rows, t, pl.multiple_of(t * LANES, LANES))
         return 0
 
     lax.fori_loop(0, tiles, get, 0)
     for t in range(tiles):
         o = slice(t * LANES, (t + 1) * LANES)
-        f = turn(rows[o, :], ids[0, t : t + 1, :])
+        f = turn(rows[o, :], ids[1, t : t + 1, :])
         left[o, 0:LANES] = jnp.transpose(jnp.concatenate([operand(f, True), terms[:, o]], axis=0)).astype(BF16)
 
 
@@ -203,7 +200,7 @@
     return pltpu.with_memory_space_constraint(x, pltpu.HBM)
 
 
-def own(run, step, table, b, noise, flag, decay, right_decay):
+def own(ids, table, b, noise, flag, decay, right_decay):
     n = b.shape[1]
     return pl.pallas_call(
         own_body,
@@ -218,22 +215,22 @@
             VMEM((1, n), F32),
             jax.ShapeDtypeStruct((SIDE, ROWS, LANES), F32),
         ),
-        in_specs=[sspec()] * 2 + [pl.BlockSpec(memory_space=pl.ANY)] * 7,
+        in_specs=[sspec()] * 2 + [pl.BlockSpec(memory_space=pl.ANY)] * 6,
         out_specs=(vspec(),) * 9,
         scratch_shapes=[
-            VMEM((2, *run.shape), jnp.int32),
+            VMEM(ids.shape, jnp.int32),
             VMEM(table.shape, F32),
             VMEM(b.shape, F32),
             VMEM((1, n), F32),
             VMEM(decay.shape, F32),
             VMEM((RANK, n), F32),
             VMEM((n, LANES), F32),
-            pltpu.SemaphoreType.DMA((6 + 4 * (table.shape[1] // GROUP),)),
+            pltpu.SemaphoreType.DMA((5 + 4 * (table.shape[1] // GROUP),)),
         ],
         compiler_params=params(12),
         cost_estimate=pl.CostEstimate(flops=n * 6000, bytes_accessed=4 * table.size, transcendentals=0),
         name="own",
-    )(run, flag, *(hbm(x) for x in (run, step, table, b, noise.reshape(1, n), decay, right_decay)))
+    )(ids, flag, ids, *(hbm(x) for x in (table, b, noise.reshape(1, n), decay, right_decay)))
 
 
 def build_body(idx_ref, other, decay, table, left, vec, small, scale, extra_b,
@@ -247,8 +244,8 @@
             t = jq * per + k
             o = slice(k * LANES, (k + 1) * LANES)
             fetch(lambda t, p: idx_ref[0, t, p], table, rows, t, k * LANES)
-            f = turn(rows[o, :], other[0, pl.ds(t, 1), :])
-            terms = jnp.dot(decay[...].astype(BF16), one_hot(other[1, pl.ds(t, 1), :]), preferred_element_type=F32)
+            f = turn(rows[o, :], other[1, pl.ds(t, 1), :])
+            terms = jnp.dot(decay[...].astype(BF16), one_hot(other[2, pl.ds(t, 1), :]), preferred_element_type=F32)
             right[slot, :, o] = jnp.concatenate([operand(f, False), terms], axis=0).astype(BF16)
 
     def column(jq, _):
@@ -475,8 +472,10 @@
     run = run_index.reshape(tiles, LANES)
     step = step_index.reshape(tiles, LANES)
     decays = (jnp.asarray(x) for x in decay_tables())
-    other = lax.ppermute(jnp.stack([run, step]), ("row", "col"), swap)
-    *mine, extra, packed = own(run, step, run_features, right_side, noise_level, flag, *decays)
+    plane = lax.broadcasted_iota(jnp.int32, (3, tiles, LANES), 0)
+    ids = jnp.where(plane == 0, run & (GROUP - 1), jnp.where(plane == 1, run >> 12, step))
+    other = lax.ppermute(ids, ("row", "col"), swap)
+    *mine, extra, packed = own(ids, run_features, right_side, noise_level, flag, *decays)
     khi, klo, part = build(other, *mine)
     product = exchange(first_sum(exchange(part, "row")), "row")
     both = exchange(apply(khi, klo, product, extra, flag), "col")

time: 113 us -> 113 us (level)
  transfers between devices with their start and end apart: 1 -> 1, of which waited for: 0 -> 0; matrix products, arithmetic and copies ran while one was open for 0% -> 0% of each run, Pallas kernels for 7% -> 6%
where the time goes in v8:
time: 113 us; the launch traced here: 112 us
  blocking collectives  72.4 us (64%)
  Pallas kernels  33.2 us (29%)
  starting transfers between devices  4.5 us (4%)
  other arithmetic  1.5 us (1%)
    all_to_all x5, blocking collectives, exchange(): return lax.all_to_all(x, axis, 0, 0)  72.4 us
    pallas_call x1, Pallas kernels, build(): pl.pallas_call(functools.partial(build_body, pt=pt, qt=qt), out_shape=(VM...  15.8 us
    pallas_call x1, Pallas kernels, apply(): pl.pallas_call(functools.partial(apply_body, pt=pt), out_shape=jax.ShapeD...  8.65 us
    pallas_call x1, Pallas kernels, own(): pl.pallas_call(own_body, out_shape=(VMEM(right_decay.shape, F32), VMEM((G...  7.2 us
    ppermute x1, starting transfers between devices, on_device(): other = lax.ppermute(ids, ('row', 'col'), swap)  4.5 us
  transfers between devices with their start and end apart: 1, of which 0 were waited for; matrix products, arithmetic and copies ran while one was open for 0% of the time, Pallas kernels for 6%

profile of v8, /device:TPU:1, one launch (start us, length us, event | category | flops | bytes accessed | tf_op | source)
XLA Modules:
  0.0 112.3 jit_solution(2857404651899804669)
XLA Ops:
  0.6 0.7 and_bitcast_fusion
  1.4 0.8 select_select_fusion.idx_ref.ids_ref
  2.1 4.5 %collective-permute-start = (s32[3,24,128]{2,1,0:T(8,128)S(1)}, s32[3,24,128]{2,1,0:T(8,128)S(1)}, u32[]{:S(2)}, u32[]{:S(2)}) collective-permute-start(s32[3,24,128]{2,1,0:T(8,128)S(1)} %select_select_fusion.idx_ref.ids_ref), channel_id=1, source_target_pairs={{0,0},{1,16},{2,32},{3,48},{4,64},{5,80},{6,96},{7,112},{8,128},{9... | collective-permute-start | bytes 110600 | tf_op jit(solution)/shard_map/ppermute | solution.py:477
  6.7 7.2 %own.1 = (f32[152,128]{1,0:T(8,128)S(1)}, f32[4096,128]{1,0:T(8,128)S(1)}, bf16[3072,256]{1,0:T(8,128)(2,1)S(1)}, bf16[32,3072]{1,0:T(8,128)(2,1)S(1)}, f8e4m3fn...) custom-call(s32[3,24,128]{2,1,0:T(8,128)S(1)} %select_select_fusion., ...), custom_call_target="tpu_custom_call" | custom-call | flops 18432000 | bytes 1572864 | tf_op jit(solution)/shard_map/own/pallas_call | solution.py:205
  13.9 0.0 collective-permute-done.idx_ref.other
  13.9 15.8 %build.1 = (bf16[3072,3072]{1,0:T(8,128)(2,1)S(1)}, f8e4m3fn[3072,3072]{1,0:T(32,128)(4,1)S(1)}, f32[16,16,128]{2,1,0:T(8,128)S(1)}) custom-call(s32[3,24,128]{2,1,0:T(8,128)S(1)} %collective-permute-done.idx_ref.other, s32[3,24,128]{2,1,0:T(8,128)S(1)} %collective-permute-done.idx_ref.other, f32[152,128]{1,0:T(8,128)S(1)} %get-tuple-element.16.decay, ...), custom_call_target="tpu_custom_call" | custom-call | flops 9437184000 | bytes 28311552 | tf_op jit(solution)/shard_map/build/pallas_call | solution.py:285
  29.7 19.1 %all_to_all.25.in_ref = f32[16,16,128]{2,1,0:T(8,128)S(1)} all-to-all(f32[16,16,128]{2,1,0:T(8,128)S(1)} %get-tuple-element.25), channel_id=1, replica_groups=mesh['row'=16,'col'=16] {'row'}, dimensions={0} | all-to-all | bytes 262144 | tf_op jit(solution)/shard_map/all_to_all | solution.py:467
  48.8 11.1 %all_to_all.26.w_ref = f32[16,16,128]{2,1,0:T(8,128)S(1)} all-to-all(f32[16,16,128]{2,1,0:T(8,128)S(1)} %first_sum.1), channel_id=1, replica_groups=mesh['row'=16,'col'=16] {'row'}, dimensions={0} | all-to-all | bytes 262144 | tf_op jit(solution)/shard_map/all_to_all | solution.py:467
  59.9 8.6 %apply.1 = f32[16,32,128]{2,1,0:T(8,128)S(1)} custom-call(bf16[3072,3072]{1,0:T(8,128)(2,1)S(1)} %get-tuple-element.23.khi_ref, f8e4m3fn[3072,3072]{1,0:T(32,128)(4,1)S(1)} %get-tuple-element.24.klo_ref, f32[16,16,128]{2,1,0:T(8,128)S(1)} %all_to_all.26.w_ref, f32[1,3072]{1,0:T(1,128)S(1)} %get-tuple-element.26.extra, f32[1]{0:T(128)} %bitcast.3.flag_ref), custom_call_target="tpu_custom_call" | custom-call | flops 5662310400 | bytes 28311552 | tf_op jit(solution)/shard_map/apply/pallas_call | solution.py:328
  68.6 0.0 copy-start
  68.6 17.8 %all_to_all.27.in_ref = f32[16,32,128]{2,1,0:T(8,128)S(1)} all-to-all(f32[16,32,128]{2,1,0:T(8,128)S(1)} %apply.1), channel_id=1, replica_groups=mesh['row'=16,'col'=16] {'col'}, dimensions={0} | all-to-all | bytes 524288 | tf_op jit(solution)/shard_map/all_to_all | solution.py:467
  86.4 0.3 chunk_sums.1
  86.8 10.6 %all_to_all.28.line_ref = f32[16,8,128]{2,1,0:T(8,128)S(1)} all-to-all(f32[16,8,128]{2,1,0:T(8,128)S(1)} %get-tuple-element.29), channel_id=1, replica_groups=mesh['row'=16,'col'=16] {'row'}, dimensions={0} | all-to-all | bytes 131072 | tf_op jit(solution)/shard_map/all_to_all | solution.py:467
  97.4 0.2 join.1
  97.6 13.7 %all_to_all.29.a_ref = f32[16,40,128]{2,1,0:T(8,128)S(1)} all-to-all(f32[16,40,128]{2,1,0:T(8,128)S(1)} %join.1), channel_id=1, replica_groups=mesh['row'=16,'col'=16] {'col'}, dimensions={0} | all-to-all | bytes 655360 | tf_op jit(solution)/shard_map/all_to_all | solution.py:467
  111.3 0.0 copy-done
  111.3 1.0 finish.1
  (2 shorter events, 0.0 us)
Async XLA Ops:
  2.1 11.7 %collective-permute-start = (s32[3,24,128]{2,1,0:T(8,128)S(1)}, s32[3,24,128]{2,1,0:T(8,128)S(1)}, u32[]{:S(2)}, u32[]{:S(2)}) collective-permute-start(s32[3,24,128]{2,1,0:T(8,128)S(1)} %select_select_fusion.idx_ref.ids_ref), channel_id=1, source_target_pairs={{0,0},{1,16},{2,32},{3,48},{4,64},{5,80},{6,96},{7,112},{8,128},{9... | collective-permute-start | bytes 110600 | tf_op jit(solution)/shard_map/ppermute | solution.py:477
  68.6 42.7 %copy-start = (f32[9,3072]{1,0:T(8,128)S(1)}, f32[9,3072]{1,0:T(8,128)}, u32[]{:S(2)}) copy-start(f32[9,3072]{1,0:T(8,128)} %b_ref.3) | copy-start | bytes 331780

commit v9 on v8

--- a/solution.py
+++ b/solution.py
@@ -473,7 +473,8 @@
     step = step_index.reshape(tiles, LANES)
     decays = (jnp.asarray(x) for x in decay_tables())
     plane = lax.broadcasted_iota(jnp.int32, (3, tiles, LANES), 0)
-    ids = jnp.where(plane == 0, run & (GROUP - 1), jnp.where(plane == 1, run >> 12, step))
+    ids = jnp.where(plane == 2, step, run)
+    ids = (ids >> jnp.where(plane == 1, 12, 0)) & jnp.where(plane == 0, GROUP - 1, -1)
     other = lax.ppermute(ids, ("row", "col"), swap)
     *mine, extra, packed = own(ids, run_features, right_side, noise_level, flag, *decays)
     khi, klo, part = build(other, *mine)

time: 113 us -> 112 us (level)
  no operation moved by 1% of the time
where the time goes in v9:
time: 112 us
  blocking collectives  72.4 us (65%)
  Pallas kernels  33.2 us (30%)
  starting transfers between devices  4.51 us (4%)
    all_to_all x5, blocking collectives, exchange(): return lax.all_to_all(x, axis, 0, 0)  72.4 us
    pallas_call x1, Pallas kernels, build(): pl.pallas_call(functools.partial(build_body, pt=pt, qt=qt), out_shape=(VM...  15.8 us
    pallas_call x1, Pallas kernels, apply(): pl.pallas_call(functools.partial(apply_body, pt=pt), out_shape=jax.ShapeD...  8.65 us
    pallas_call x1, Pallas kernels, own(): pl.pallas_call(own_body, out_shape=(VMEM(right_decay.shape, F32), VMEM((G...  7.2 us
    ppermute x1, starting transfers between devices, on_device(): other = lax.ppermute(ids, ('row', 'col'), swap)  4.51 us
  transfers between devices with their start and end apart: 1, of which 0 were waited for; matrix products, arithmetic and copies ran while one was open for 0% of the time, Pallas kernels for 6%

profile of v9, /device:TPU:1, one launch (start us, length us, event | category | flops | bytes accessed | tf_op | source)
XLA Modules:
  0.0 111.6 jit_solution(9447551174490728983)
XLA Ops:
  0.7 0.8 shift-right-arithmetic_and_fusion.idx_ref.ids_ref
  1.5 4.5 %collective-permute-start = (s32[3,24,128]{2,1,0:T(8,128)S(1)}, s32[3,24,128]{2,1,0:T(8,128)S(1)}, u32[]{:S(2)}, u32[]{:S(2)}) collective-permute-start(s32[3,24,128]{2,1,0:T(8,128)S(1)} %shift-right-arithmetic_and_fusion.idx_ref.ids_ref), channel_id=1, source_target_pairs={{0,0},{1,16},{2,32},{3,48},{4,64},{5,80},{6,96},{7,112},{8,128},{9... | collective-permute-start | bytes 110600 | tf_op jit(solution)/shard_map/ppermute | solution.py:478
  6.0 7.2 %own.1 = (f32[152,128]{1,0:T(8,128)S(1)}, f32[4096,128]{1,0:T(8,128)S(1)}, bf16[3072,256]{1,0:T(8,128)(2,1)S(1)}, bf16[32,3072]{1,0:T(8,128)(2,1)S(1)}, f8e4m3fn...) custom-call(s32[3,24,128]{2,1,0:T(8,128)S(1)} %shift-right-arithmeti, ...), custom_call_target="tpu_custom_call" | custom-call | flops 18432000 | bytes 1572864 | tf_op jit(solution)/shard_map/own/pallas_call | solution.py:205
  13.2 0.0 collective-permute-done.idx_ref.other
  13.2 15.8 %build.1 = (bf16[3072,3072]{1,0:T(8,128)(2,1)S(1)}, f8e4m3fn[3072,3072]{1,0:T(32,128)(4,1)S(1)}, f32[16,16,128]{2,1,0:T(8,128)S(1)}) custom-call(s32[3,24,128]{2,1,0:T(8,128)S(1)} %collective-permute-done.idx_ref.other, s32[3,24,128]{2,1,0:T(8,128)S(1)} %collective-permute-done.idx_ref.other, f32[152,128]{1,0:T(8,128)S(1)} %get-tuple-element.16.decay, ...), custom_call_target="tpu_custom_call" | custom-call | flops 9437184000 | bytes 28311552 | tf_op jit(solution)/shard_map/build/pallas_call | solution.py:285
  29.0 19.1 %all_to_all.25.in_ref = f32[16,16,128]{2,1,0:T(8,128)S(1)} all-to-all(f32[16,16,128]{2,1,0:T(8,128)S(1)} %get-tuple-element.25), channel_id=1, replica_groups=mesh['row'=16,'col'=16] {'row'}, dimensions={0} | all-to-all | bytes 262144 | tf_op jit(solution)/shard_map/all_to_all | solution.py:467
  48.1 11.1 %all_to_all.26.w_ref = f32[16,16,128]{2,1,0:T(8,128)S(1)} all-to-all(f32[16,16,128]{2,1,0:T(8,128)S(1)} %first_sum.1), channel_id=1, replica_groups=mesh['row'=16,'col'=16] {'row'}, dimensions={0} | all-to-all | bytes 262144 | tf_op jit(solution)/shard_map/all_to_all | solution.py:467
  59.3 8.6 %apply.1 = f32[16,32,128]{2,1,0:T(8,128)S(1)} custom-call(bf16[3072,3072]{1,0:T(8,128)(2,1)S(1)} %get-tuple-element.23.khi_ref, f8e4m3fn[3072,3072]{1,0:T(32,128)(4,1)S(1)} %get-tuple-element.24.klo_ref, f32[16,16,128]{2,1,0:T(8,128)S(1)} %all_to_all.26.w_ref, f32[1,3072]{1,0:T(1,128)S(1)} %get-tuple-element.26.extra, f32[1]{0:T(128)} %bitcast.2.flag_ref), custom_call_target="tpu_custom_call" | custom-call | flops 5662310400 | bytes 28311552 | tf_op jit(solution)/shard_map/apply/pallas_call | solution.py:328
  67.9 0.0 copy-start
  67.9 17.8 %all_to_all.27.in_ref = f32[16,32,128]{2,1,0:T(8,128)S(1)} all-to-all(f32[16,32,128]{2,1,0:T(8,128)S(1)} %apply.1), channel_id=1, replica_groups=mesh['row'=16,'col'=16] {'col'}, dimensions={0} | all-to-all | bytes 524288 | tf_op jit(solution)/shard_map/all_to_all | solution.py:467
  85.7 0.3 chunk_sums.1
  86.1 10.6 %all_to_all.28.line_ref = f32[16,8,128]{2,1,0:T(8,128)S(1)} all-to-all(f32[16,8,128]{2,1,0:T(8,128)S(1)} %get-tuple-element.29), channel_id=1, replica_groups=mesh['row'=16,'col'=16] {'row'}, dimensions={0} | all-to-all | bytes 131072 | tf_op jit(solution)/shard_map/all_to_all | solution.py:467
  96.7 0.2 join.1
  96.9 13.7 %all_to_all.29.a_ref = f32[16,40,128]{2,1,0:T(8,128)S(1)} all-to-all(f32[16,40,128]{2,1,0:T(8,128)S(1)} %join.1), channel_id=1, replica_groups=mesh['row'=16,'col'=16] {'col'}, dimensions={0} | all-to-all | bytes 655360 | tf_op jit(solution)/shard_map/all_to_all | solution.py:467
  110.6 0.0 copy-done
  110.6 1.0 finish.1
  (3 shorter events, 0.0 us)
Async XLA Ops:
  1.5 11.7 %collective-permute-start = (s32[3,24,128]{2,1,0:T(8,128)S(1)}, s32[3,24,128]{2,1,0:T(8,128)S(1)}, u32[]{:S(2)}, u32[]{:S(2)}) collective-permute-start(s32[3,24,128]{2,1,0:T(8,128)S(1)} %shift-right-arithmetic_and_fusion.idx_ref.ids_ref), channel_id=1, source_target_pairs={{0,0},{1,16},{2,32},{3,48},{4,64},{5,80},{6,96},{7,112},{8,128},{9... | collective-permute-start | bytes 110600 | tf_op jit(solution)/shard_map/ppermute | solution.py:478
  67.9 42.7 %copy-start = (f32[9,3072]{1,0:T(8,128)S(1)}, f32[9,3072]{1,0:T(8,128)}, u32[]{:S(2)}) copy-start(f32[9,3072]{1,0:T(8,128)} %b_ref.3) | copy-start | bytes 331780

commit v10 on v9

--- a/solution.py
+++ b/solution.py
@@ -415,7 +415,7 @@
 
 def join_body(chunk_ref, line_ref, out_ref):
     line = put(joined(jnp.concatenate([line_ref[s, 0:1, :] for s in range(SIDE)], axis=0), False))
-    for s in range(SIDE):
+    for s in range(SIDE // 2):
         out_ref[s, 0:BOTH, :] = chunk_ref[...]
         out_ref[s, BOTH:MORE, :] = jnp.broadcast_to(line, (MORE - BOTH, LANES))
 
@@ -423,7 +423,7 @@
 def join(chunk, line):
     return pl.pallas_call(
         join_body,
-        out_shape=jax.ShapeDtypeStruct((SIDE, MORE, LANES), F32),
+        out_shape=jax.ShapeDtypeStruct((SIDE // 2, MORE, LANES), F32),
         in_specs=[vspec(), vspec()],
         out_specs=vspec(),
         compiler_params=params(),
@@ -431,7 +431,11 @@
     )(chunk, line)
 
 
-def finish_body(b_ref, a_ref, x_ref, r_ref, nw, na):
+def finish_body(b_ref, mine, other, core_ref, x_ref, r_ref, a_ref, nw, na):
+    core = core_ref[0]
+    for h in range(SIDE // 2):
+        a_ref[2 * h + core] = mine[h]
+        a_ref[2 * h + 1 - core] = other[h]
     tiles = b_ref.shape[1] // LANES
     unpack(a_ref, na, tiles)
     unpack(a_ref, nw, tiles, ROWS)
@@ -446,18 +450,18 @@
     r_ref[...] = r - second * ((w - first * na[0:PROBES, :]) + beta * w)
 
 
-def finish(b, a):
+def finish(b, mine, other, core):
     n = b.shape[1]
     out = jax.ShapeDtypeStruct((PROBES, n), F32)
     return pl.pallas_call(
         finish_body,
         out_shape=(out, out),
-        in_specs=[vspec()] * 2,
+        in_specs=[vspec()] * 3 + [sspec()],
         out_specs=(vspec(), vspec()),
-        scratch_shapes=[VMEM((ROWS, n), F32), VMEM((ROWS, n), F32)],
-        compiler_params=params(),
+        scratch_shapes=[VMEM((SIDE, MORE, LANES), F32), VMEM((ROWS, n), F32), VMEM((ROWS, n), F32)],
+        compiler_params=params(4),
         name="finish",
-    )(b, a)
+    )(b, mine, other, core)
 
 
 def on_device(right_side, noise_level, run_index, step_index, run_features):
@@ -481,8 +485,10 @@
     product = exchange(first_sum(exchange(part, "row")), "row")
     both = exchange(apply(khi, klo, product, extra, flag), "col")
     chunk, line = chunk_sums(both, packed, which)
-    again = exchange(join(chunk, exchange(line, "row")), "col")
-    return finish(right_side, again)
+    halves = [list(range(k, SIDE, 2)) for k in range(2)]
+    mine = lax.all_to_all(join(chunk, exchange(line, "row")), "col", 0, 0, axis_index_groups=halves)
+    rest = lax.ppermute(mine, "col", [(k, k ^ 1) for k in range(SIDE)])
+    return finish(right_side, mine, rest, which & 1)
 
 
 def solution(mesh):

time: 112 us -> 112 us (level)
  blocking collectives: 72.4 us -> 68.3 us
  starting transfers between devices: 4.51 us -> 7.48 us
    all_to_all x5 -> x4, blocking collectives: 72.4 us -> 58.5 us  [exchange(): return lax.all_to_all(x, axis, 0, 0)]
    all_to_all x0 -> x1, blocking collectives: none -> 9.78 us  [on_device(): lax.all_to_all(join(chunk, exchange(line, 'row')), 'col', 0, 0, axis_inde...]
    ppermute x0 -> x1, starting transfers between devices: none -> 2.97 us  [on_device(): rest = lax.ppermute(mine, 'col', [(k, k ^ 1) for k in range(SIDE)])]
  transfers between devices with their start and end apart: 1 -> 2, of which waited for: 0 -> 1; matrix products, arithmetic and copies ran while one was open for 0% -> 0% of each run, Pallas kernels for 6% -> 6%
where the time goes in v10:
time: 112 us; the launch traced here: 111 us
  blocking collectives  68.3 us (61%)
  Pallas kernels  33.2 us (30%)
  starting transfers between devices  7.48 us (7%)
    all_to_all x4, blocking collectives, exchange(): return lax.all_to_all(x, axis, 0, 0)  58.5 us
    pallas_call x1, Pallas kernels, build(): pl.pallas_call(functools.partial(build_body, pt=pt, qt=qt), out_shape=(VM...  15.8 us
    all_to_all x1, blocking collectives, on_device(): lax.all_to_all(join(chunk, exchange(line, 'row')), 'col', 0, 0, axis_inde...  9.78 us
    pallas_call x1, Pallas kernels, apply(): pl.pallas_call(functools.partial(apply_body, pt=pt), out_shape=jax.ShapeD...  8.65 us
    pallas_call x1, Pallas kernels, own(): pl.pallas_call(own_body, out_shape=(VMEM(right_decay.shape, F32), VMEM((G...  7.2 us
    ppermute x1, starting transfers between devices, on_device(): other = lax.ppermute(ids, ('row', 'col'), swap)  4.51 us
    ppermute x1, starting transfers between devices, on_device(): rest = lax.ppermute(mine, 'col', [(k, k ^ 1) for k in range(SIDE)])  2.97 us
  transfers between devices with their start and end apart: 2, of which 1 were waited for; matrix products, arithmetic and copies ran while one was open for 0% of the time, Pallas kernels for 6%

profile of v10, /device:TPU:1, one launch (start us, length us, event | category | flops | bytes accessed | tf_op | source)
XLA Modules:
  0.0 111.5 jit_solution(12004126160860579141)
XLA Ops:
  0.7 0.8 shift-right-arithmetic_and_fusion.idx_ref.ids_ref
  1.5 4.5 %collective-permute-start = (s32[3,24,128]{2,1,0:T(8,128)S(1)}, s32[3,24,128]{2,1,0:T(8,128)S(1)}, u32[]{:S(2)}, u32[]{:S(2)}) collective-permute-start(s32[3,24,128]{2,1,0:T(8,128)S(1)} %shift-right-arithmetic_and_fusion.idx_ref.ids_ref), channel_id=1, source_target_pairs={{0,0},{1,16},{2,32},{3,48},{4,64},{5,80},{6,96},{7,112},{8,128},{9... | collective-permute-start | bytes 110600 | tf_op jit(solution)/shard_map/ppermute | solution.py:482
  6.0 7.2 %own.1 = (f32[152,128]{1,0:T(8,128)S(1)}, f32[4096,128]{1,0:T(8,128)S(1)}, bf16[3072,256]{1,0:T(8,128)(2,1)S(1)}, bf16[32,3072]{1,0:T(8,128)(2,1)S(1)}, f8e4m3fn...) custom-call(s32[3,24,128]{2,1,0:T(8,128)S(1)} %shift-right-arithmeti, ...), custom_call_target="tpu_custom_call" | custom-call | flops 18432000 | bytes 1572864 | tf_op jit(solution)/shard_map/own/pallas_call | solution.py:205
  13.2 0.0 collective-permute-done.idx_ref.other
  13.2 15.8 %build.1 = (bf16[3072,3072]{1,0:T(8,128)(2,1)S(1)}, f8e4m3fn[3072,3072]{1,0:T(32,128)(4,1)S(1)}, f32[16,16,128]{2,1,0:T(8,128)S(1)}) custom-call(s32[3,24,128]{2,1,0:T(8,128)S(1)} %collective-permute-done.idx_ref.other, s32[3,24,128]{2,1,0:T(8,128)S(1)} %collective-permute-done.idx_ref.other, f32[152,128]{1,0:T(8,128)S(1)} %get-tuple-element.16.decay, ...), custom_call_target="tpu_custom_call" | custom-call | flops 9437184000 | bytes 28311552 | tf_op jit(solution)/shard_map/build/pallas_call | solution.py:285
  29.0 19.1 %all_to_all.25.in_ref = f32[16,16,128]{2,1,0:T(8,128)S(1)} all-to-all(f32[16,16,128]{2,1,0:T(8,128)S(1)} %get-tuple-element.25), channel_id=1, replica_groups=mesh['row'=16,'col'=16] {'row'}, dimensions={0} | all-to-all | bytes 262144 | tf_op jit(solution)/shard_map/all_to_all | solution.py:471
  48.1 11.1 %all_to_all.26.w_ref = f32[16,16,128]{2,1,0:T(8,128)S(1)} all-to-all(f32[16,16,128]{2,1,0:T(8,128)S(1)} %first_sum.1), channel_id=1, replica_groups=mesh['row'=16,'col'=16] {'row'}, dimensions={0} | all-to-all | bytes 262144 | tf_op jit(solution)/shard_map/all_to_all | solution.py:471
  59.2 0.0 copy-start
  59.2 8.6 %apply.1 = f32[16,32,128]{2,1,0:T(8,128)S(1)} custom-call(bf16[3072,3072]{1,0:T(8,128)(2,1)S(1)} %get-tuple-element.23.khi_ref, f8e4m3fn[3072,3072]{1,0:T(32,128)(4,1)S(1)} %get-tuple-element.24.klo_ref, f32[16,16,128]{2,1,0:T(8,128)S(1)} %all_to_all.26.w_ref, f32[1,3072]{1,0:T(1,128)S(1)} %get-tuple-element.26.extra, f32[1]{0:T(128)} %bitcast.2.flag_ref), custom_call_target="tpu_custom_call" | custom-call | flops 5662310400 | bytes 28311552 | tf_op jit(solution)/shard_map/apply/pallas_call | solution.py:328
  67.9 17.7 %all_to_all.27.in_ref = f32[16,32,128]{2,1,0:T(8,128)S(1)} all-to-all(f32[16,32,128]{2,1,0:T(8,128)S(1)} %apply.1), channel_id=1, replica_groups=mesh['row'=16,'col'=16] {'col'}, dimensions={0} | all-to-all | bytes 524288 | tf_op jit(solution)/shard_map/all_to_all | solution.py:471
  85.6 0.3 chunk_sums.1
  85.9 10.6 %all_to_all.28.line_ref = f32[16,8,128]{2,1,0:T(8,128)S(1)} all-to-all(f32[16,8,128]{2,1,0:T(8,128)S(1)} %get-tuple-element.29), channel_id=1, replica_groups=mesh['row'=16,'col'=16] {'row'}, dimensions={0} | all-to-all | bytes 131072 | tf_op jit(solution)/shard_map/all_to_all | solution.py:471
  96.5 0.2 join.1
  96.7 9.8 %all_to_all.29.mine = f32[8,40,128]{2,1,0:T(8,128)S(1)} all-to-all(f32[8,40,128]{2,1,0:T(8,128)S(1)} %join.1), channel_id=1, replica_groups={{0,2,4,6,8,10,12,14},{1,3,5,7,9,11,13,15},{16,18,20,22,24,26,28,30},{17..., dimensions={0} | all-to-all | bytes 327680 | tf_op jit(solution)/shard_map/all_to_all | solution.py:489
  106.5 3.0 %collective-permute-start.1 = (f32[8,40,128]{2,1,0:T(8,128)S(1)}, f32[8,40,128]{2,1,0:T(8,128)S(1)}, u32[]{:S(2)}, u32[]{:S(2)}) collective-permute-start(f32[8,40,128]{2,1,0:T(8,128)S(1)} %all_to_all.29.mine), channel_id=1, source_target_pairs={{0,1},{1,0},{2,3},{3,2},{4,5},{5,4},{6,7},{7,6},{8,9},{9,8},{10,11... | collective-permute-start | bytes 491528 | tf_op jit(solution)/shard_map/ppermute | solution.py:490
  109.4 1.0 collective-permute-done.1.other
  110.5 0.0 copy-done
  110.5 1.0 finish.1
  (3 shorter events, 0.0 us)
Async XLA Ops:
  1.5 11.7 %collective-permute-start = (s32[3,24,128]{2,1,0:T(8,128)S(1)}, s32[3,24,128]{2,1,0:T(8,128)S(1)}, u32[]{:S(2)}, u32[]{:S(2)}) collective-permute-start(s32[3,24,128]{2,1,0:T(8,128)S(1)} %shift-right-arithmetic_and_fusion.idx_ref.ids_ref), channel_id=1, source_target_pairs={{0,0},{1,16},{2,32},{3,48},{4,64},{5,80},{6,96},{7,112},{8,128},{9... | collective-permute-start | bytes 110600 | tf_op jit(solution)/shard_map/ppermute | solution.py:482
  59.2 51.2 %copy-start = (f32[9,3072]{1,0:T(8,128)S(1)}, f32[9,3072]{1,0:T(8,128)}, u32[]{:S(2)}) copy-start(f32[9,3072]{1,0:T(8,128)} %b_ref.3) | copy-start | bytes 331780
  106.5 4.0 %collective-permute-start.1 = (f32[8,40,128]{2,1,0:T(8,128)S(1)}, f32[8,40,128]{2,1,0:T(8,128)S(1)}, u32[]{:S(2)}, u32[]{:S(2)}) collective-permute-start(f32[8,40,128]{2,1,0:T(8,128)S(1)} %all_to_all.29.mine), channel_id=1, source_target_pairs={{0,1},{1,0},{2,3},{3,2},{4,5},{5,4},{6,7},{7,6},{8,9},{9,8},{10,11... | collective-permute-start | bytes 491528 | tf_op jit(solution)/shard_map/ppermute | solution.py:490

commit v11 on v10

--- a/solution.py
+++ b/solution.py
@@ -299,7 +299,7 @@
     )(other, other, decay, table, left, vec, small, scale, extra_b)
 
 
-def apply_body(khi_ref, klo_ref, w_ref, extra, flag_ref, out_ref, nat, vec, small, *, pt):
+def apply_body(khi_ref, klo_ref, w_ref, extra, flag_ref, core_ref, keep, give, out_ref, nat, vec, small, *, pt):
     n, m = khi_ref.shape
     unpack(w_ref, nat, m // LANES)
     vec[...], small[...], scale = factors(nat[0:PROBES, :])
@@ -319,22 +319,26 @@
         return 0
 
     lax.fori_loop(0, n // pt, row, 0)
-
-
-def apply(khi, klo, w, extra, flag, pt=512):
+    core = core_ref[0]
+    for h in range(SIDE // 2):
+        keep[h] = out_ref[2 * h + core]
+        give[h] = out_ref[2 * h + 1 - core]
+
+
+def apply(khi, klo, w, extra, flag, core, pt=512):
     n, m = khi.shape
     khi = pltpu.with_memory_space_constraint(khi, VMEM)
     klo = pltpu.with_memory_space_constraint(klo, VMEM)
     return pl.pallas_call(
         functools.partial(apply_body, pt=pt),
-        out_shape=jax.ShapeDtypeStruct((SIDE, BOTH, LANES), F32),
-        in_specs=[vspec()] * 4 + [sspec()],
-        out_specs=vspec(),
-        scratch_shapes=[VMEM((ROWS, m), F32), VMEM((2 * ROWS, m), BF16), VMEM((2 * ROWS, m), F8)],
+        out_shape=(jax.ShapeDtypeStruct((SIDE // 2, BOTH, LANES), F32),) * 2,
+        in_specs=[vspec()] * 4 + [sspec()] * 2,
+        out_specs=(vspec(), vspec()),
+        scratch_shapes=[VMEM((SIDE, BOTH, LANES), F32), VMEM((ROWS, m), F32), VMEM((2 * ROWS, m), BF16), VMEM((2 * ROWS, m), F8)],
         compiler_params=params(4),
         cost_estimate=pl.CostEstimate(flops=n * m * 600, bytes_accessed=n * m * 3, transcendentals=0),
         name="apply",
-    )(khi, klo, w, extra, flag)
+    )(khi, klo, w, extra, flag, core)
 
 
 def first_sum_body(in_ref, out_ref):
@@ -382,6 +386,21 @@
         line = jnp.where(lane < PROBES, line, 0.0)
         out = out + (line if k == 0 else pltpu.roll(line, ROWS * k, 1))
     return out
+
+
+def add_body(a_ref, b_ref, out_ref):
+    out_ref[...] = a_ref[...] + b_ref[...]
+
+
+def add(a, b):
+    return pl.pallas_call(
+        add_body,
+        out_shape=jax.ShapeDtypeStruct(a.shape, F32),
+        in_specs=[vspec()] * 2,
+        out_specs=vspec(),
+        compiler_params=params(),
+        name="add",
+    )(a, b)
 
 
 def chunk_body(in_ref, b_ref, which_ref, chunk_ref, line_ref):
@@ -483,12 +502,19 @@
     *mine, extra, packed = own(ids, run_features, right_side, noise_level, flag, *decays)
     khi, klo, part = build(other, *mine)
     product = exchange(first_sum(exchange(part, "row")), "row")
-    both = exchange(apply(khi, klo, product, extra, flag), "col")
-    chunk, line = chunk_sums(both, packed, which)
     halves = [list(range(k, SIDE, 2)) for k in range(2)]
-    mine = lax.all_to_all(join(chunk, exchange(line, "row")), "col", 0, 0, axis_index_groups=halves)
-    rest = lax.ppermute(mine, "col", [(k, k ^ 1) for k in range(SIDE)])
-    return finish(right_side, mine, rest, which & 1)
+
+    def swapped(x):
+        return lax.ppermute(x, "col", [(k, k ^ 1) for k in range(SIDE)])
+
+    def half_exchange(x):
+        return lax.all_to_all(x, "col", 0, 0, axis_index_groups=halves)
+
+    core = which & 1
+    keep, give = apply(khi, klo, product, extra, flag, core)
+    chunk, line = chunk_sums(half_exchange(add(keep, swapped(give))), packed, which)
+    mine = half_exchange(join(chunk, exchange(line, "row")))
+    return finish(right_side, mine, swapped(mine), core)
 
 
 def solution(mesh):

time: 112 us -> 134 us (1.20)
  local copies, waits for them, and re-layouts: 0.01 us -> 20.2 us
  blocking collectives: 68.3 us -> 51.7 us
  waiting for transfers between devices: 1.03 us -> 10.5 us
  starting transfers between devices: 7.48 us -> 15.4 us
    all_to_all x4 -> x2, blocking collectives: 58.5 us -> 29.6 us  [exchange(): return lax.all_to_all(x, axis, 0, 0)]
    unnamed x2 -> x10, local copies, waits for them, and re-layouts: 0.01 us -> 20.2 us
    all_to_all x1 -> x2, blocking collectives: 9.78 us -> 22.1 us  [half_exchange(): return lax.all_to_all(x, 'col', 0, 0, axis_index_groups=halves)]
    all_to_all x0 -> x1, waiting for transfers between devices: none -> 8.51 us  [exchange(): return lax.all_to_all(x, axis, 0, 0)]
    ppermute x1 -> x2, starting transfers between devices: 2.97 us -> 7.43 us  [swapped(): return lax.ppermute(x, 'col', [(k, k ^ 1) for k in range(SIDE)])]
    all_to_all x0 -> x1, starting transfers between devices: none -> 3.51 us  [exchange(): return lax.all_to_all(x, axis, 0, 0)]
    pallas_call x1 -> x2, Pallas kernels: 8.65 us -> 8.68 us  [the longest x1 8.67 us: apply(): pl.pallas_call(functools.partial(apply_body, pt=pt), out_shape=(jax.Shape...]
  transfers between devices with their start and end apart: 2 -> 4, of which waited for: 1 -> 3; matrix products, arithmetic and copies ran while one was open for 0% -> 0% of each run, Pallas kernels for 6% -> 5%
where the time goes in v11:
time: 134 us; the launch traced here: 133 us
  blocking collectives  51.7 us (39%)
  Pallas kernels  33.9 us (25%)
  local copies, waits for them, and re-layouts  20.2 us (15%)
  starting transfers between devices  15.4 us (11%)
  waiting for transfers between devices  10.5 us (8%)
    all_to_all x2, blocking collectives, exchange(): return lax.all_to_all(x, axis, 0, 0)  29.6 us
    all_to_all x2, blocking collectives, half_exchange(): return lax.all_to_all(x, 'col', 0, 0, axis_index_groups=halves)  22.1 us
    unnamed x10, local copies, waits for them, and re-layouts  20.2 us
    pallas_call x1, Pallas kernels, build(): pl.pallas_call(functools.partial(build_body, pt=pt, qt=qt), out_shape=(VM...  15.8 us
    pallas_call x1, Pallas kernels, apply(): pl.pallas_call(functools.partial(apply_body, pt=pt), out_shape=(jax.Shape...  8.67 us
    all_to_all x1, waiting for transfers between devices, exchange(): return lax.all_to_all(x, axis, 0, 0)  8.51 us
    ppermute x2, starting transfers between devices, swapped(): return lax.ppermute(x, 'col', [(k, k ^ 1) for k in range(SIDE)])  7.43 us
    pallas_call x1, Pallas kernels, own(): pl.pallas_call(own_body, out_shape=(VMEM(right_decay.shape, F32), VMEM((G...  7.2 us
  transfers between devices with their start and end apart: 4, of which 3 were waited for; matrix products, arithmetic and copies ran while one was open for 0% of the time, Pallas kernels for 5%

profile of v11, /device:TPU:1, one launch (start us, length us, event | category | flops | bytes accessed | tf_op | source)
XLA Modules:
  0.0 133.4 jit_solution(13305776237252983133)
XLA Ops:
  0.7 0.8 shift-right-arithmetic_and_fusion.idx_ref.ids_ref
  1.5 4.5 %collective-permute-start = (s32[3,24,128]{2,1,0:T(8,128)S(1)}, s32[3,24,128]{2,1,0:T(8,128)S(1)}, u32[]{:S(2)}, u32[]{:S(2)}) collective-permute-start(s32[3,24,128]{2,1,0:T(8,128)S(1)} %shift-right-arithmetic_and_fusion.idx_ref.ids_ref), channel_id=1, source_target_pairs={{0,0},{1,16},{2,32},{3,48},{4,64},{5,80},{6,96},{7,112},{8,128},{9... | collective-permute-start | bytes 110600 | tf_op jit(solution)/shard_map/ppermute | solution.py:501
  6.0 7.2 %own.1 = (f32[152,128]{1,0:T(8,128)S(1)}, f32[4096,128]{1,0:T(8,128)S(1)}, bf16[3072,256]{1,0:T(8,128)(2,1)S(1)}, bf16[32,3072]{1,0:T(8,128)(2,1)S(1)}, f8e4m3fn...) custom-call(s32[3,24,128]{2,1,0:T(8,128)S(1)} %shift-right-arithmeti, ...), custom_call_target="tpu_custom_call" | custom-call | flops 18432000 | bytes 1572864 | tf_op jit(solution)/shard_map/own/pallas_call | solution.py:205
  13.2 0.0 collective-permute-done.idx_ref.other
  13.2 15.8 %build.1 = (bf16[3072,3072]{1,0:T(8,128)(2,1)S(1)}, f8e4m3fn[3072,3072]{1,0:T(32,128)(4,1)S(1)}, f32[16,16,128]{2,1,0:T(8,128)S(1)}) custom-call(s32[3,24,128]{2,1,0:T(8,128)S(1)} %collective-permute-done.idx_ref.other, s32[3,24,128]{2,1,0:T(8,128)S(1)} %collective-permute-done.idx_ref.other, f32[152,128]{1,0:T(8,128)S(1)} %get-tuple-element.18.decay, ...), custom_call_target="tpu_custom_call" | custom-call | flops 9437184000 | bytes 28311552 | tf_op jit(solution)/shard_map/build/pallas_call | solution.py:285
  29.1 0.0 copy-start
  29.1 6.4 %copy-done = bf16[3072,3072]{1,0:T(8,128)(2,1)} copy-done((bf16[3072,3072]{1,0:T(8,128)(2,1)}, bf16[3072,3072]{1,0:T(8,128)(2,1)S(1)}, u32[]{:S(2)}) %copy-start) | copy-done | bytes 18874392
  35.5 0.0 copy-start.2
  35.5 3.7 %copy-done.2 = f8e4m3fn[3072,3072]{1,0:T(32,128)(4,1)} copy-done((f8e4m3fn[3072,3072]{1,0:T(32,128)(4,1)}, f8e4m3fn[3072,3072]{1,0:T(32,128)(4,1)S(1)}, u32[]{:S(2)}) %copy-start.2) | copy-done | bytes 9437208
  39.2 19.1 %all_to_all.25.in_ref = f32[16,16,128]{2,1,0:T(8,128)S(1)} all-to-all(f32[16,16,128]{2,1,0:T(8,128)S(1)} %get-tuple-element.27), channel_id=1, replica_groups=mesh['row'=16,'col'=16] {'row'}, dimensions={0} | all-to-all | bytes 262144 | tf_op jit(solution)/shard_map/all_to_all | solution.py:490
  58.3 0.7 first_sum.1
  59.0 3.5 %all-to-all-start.1 = ((f32[16,16,128]{2,1,0:T(8,128)}), f32[16,16,128]{2,1,0:T(8,128)S(1)}, u32[]{:S(2)}, u32[]{:S(2)}) async-start(f32[16,16,128]{2,1,0:T(8,128)} %first_sum.1), calls=%async_computation.1 | async-start | bytes 262144 | tf_op jit(solution)/shard_map/all_to_all | solution.py:490
  62.5 8.5 %all-to-all-done.1.w_ref = f32[16,16,128]{2,1,0:T(8,128)S(1)} async-done(((f32[16,16,128]{2,1,0:T(8,128)}), f32[16,16,128]{2,1,0:T(8,128)S(1)}, u32[]{:S(2)}, u32[]{:S(2)}) %all-to-all-start.1) | async-done | bytes 131104 | tf_op jit(solution)/shard_map/all_to_all | solution.py:490
  71.0 0.0 copy-start.1
  71.0 6.4 %copy-done.1 = bf16[3072,3072]{1,0:T(8,128)(2,1)S(1)} copy-done((bf16[3072,3072]{1,0:T(8,128)(2,1)S(1)}, bf16[3072,3072]{1,0:T(8,128)(2,1)}, u32[]{:S(2)}) %copy-start.1) | copy-done | bytes 18874392
  77.4 0.0 copy-start.3
  77.4 3.7 %copy-done.3 = f8e4m3fn[3072,3072]{1,0:T(32,128)(4,1)S(1)} copy-done((f8e4m3fn[3072,3072]{1,0:T(32,128)(4,1)S(1)}, f8e4m3fn[3072,3072]{1,0:T(32,128)(4,1)}, u32[]{:S(2)}) %copy-start.3) | copy-done | bytes 9437208
  81.1 0.0 copy-start.4
  81.1 8.7 %apply.1 = (f32[8,32,128]{2,1,0:T(8,128)S(1)}, f32[8,32,128]{2,1,0:T(8,128)S(1)}) custom-call(bf16[3072,3072]{1,0:T(8,128)(2,1)S(1)} %copy-done.1, f8e4m3fn[3072,3072]{1,0:T(32,128)(4,1)S(1)} %copy-done.3, f32[16,16,128]{2,1,0:T(8,128)S(1)} %all-to-all-done.1.w_ref, f32[1,3072]{1,0:T(1,128)S(1)} %get-tuple-element.28.extra, f32[1]{0:T(128)} %bitcast.2.flag_ref, ...), custom_call_target="tpu_custom_call" | custom-call | flops 5662310400 | bytes 28311552 | tf_op jit(solution)/shard_map/apply/pallas_call | solution.py:332
  89.8 3.3 %collective-permute-start.1 = (f32[8,32,128]{2,1,0:T(8,128)S(1)}, f32[8,32,128]{2,1,0:T(8,128)S(1)}, u32[]{:S(2)}, u32[]{:S(2)}) collective-permute-start(f32[8,32,128]{2,1,0:T(8,128)S(1)} %get-tuple-element.30), channel_id=1, source_target_pairs={{0,1},{1,0},{2,3},{3,2},{4,5},{5,4},{6,7},{7,6},{8,9},{9,8},{10,11... | collective-permute-start | bytes 393224 | tf_op jit(solution)/shard_map/ppermute | solution.py:508
  93.1 1.0 collective-permute-done.1.b_ref
  94.1 12.5 %all_to_all.26.in_ref = f32[8,32,128]{2,1,0:T(8,128)S(1)} all-to-all(f32[8,32,128]{2,1,0:T(8,128)S(1)} %add.1), channel_id=1, replica_groups={{0,2,4,6,8,10,12,14},{1,3,5,7,9,11,13,15},{16,18,20,22,24,26,28,30},{17..., dimensions={0} | all-to-all | bytes 262144 | tf_op jit(solution)/shard_map/all_to_all | solution.py:511
  106.6 0.3 chunk_sums.1
  107.0 10.6 %all_to_all.27.line_ref = f32[16,8,128]{2,1,0:T(8,128)S(1)} all-to-all(f32[16,8,128]{2,1,0:T(8,128)S(1)} %get-tuple-element.33), channel_id=1, replica_groups=mesh['row'=16,'col'=16] {'row'}, dimensions={0} | all-to-all | bytes 131072 | tf_op jit(solution)/shard_map/all_to_all | solution.py:490
  117.5 0.2 join.1
  117.7 9.6 %all_to_all.28.mine = f32[8,40,128]{2,1,0:T(8,128)S(1)} all-to-all(f32[8,40,128]{2,1,0:T(8,128)S(1)} %join.1), channel_id=1, replica_groups={{0,2,4,6,8,10,12,14},{1,3,5,7,9,11,13,15},{16,18,20,22,24,26,28,30},{17..., dimensions={0} | all-to-all | bytes 327680 | tf_op jit(solution)/shard_map/all_to_all | solution.py:511
  127.3 4.1 %collective-permute-start.2 = (f32[8,40,128]{2,1,0:T(8,128)S(1)}, f32[8,40,128]{2,1,0:T(8,128)S(1)}, u32[]{:S(2)}, u32[]{:S(2)}) collective-permute-start(f32[8,40,128]{2,1,0:T(8,128)S(1)} %all_to_all.28.mine), channel_id=1, source_target_pairs={{0,1},{1,0},{2,3},{3,2},{4,5},{5,4},{6,7},{7,6},{8,9},{9,8},{10,11... | collective-permute-start | bytes 491528 | tf_op jit(solution)/shard_map/ppermute | solution.py:508
  131.3 1.0 collective-permute-done.2.other
  132.4 0.0 copy-done.4
  132.4 1.0 finish.1
  (3 shorter events, 0.0 us)
Async XLA Ops:
  1.5 11.7 %collective-permute-start = (s32[3,24,128]{2,1,0:T(8,128)S(1)}, s32[3,24,128]{2,1,0:T(8,128)S(1)}, u32[]{:S(2)}, u32[]{:S(2)}) collective-permute-start(s32[3,24,128]{2,1,0:T(8,128)S(1)} %shift-right-arithmetic_and_fusion.idx_ref.ids_ref), channel_id=1, source_target_pairs={{0,0},{1,16},{2,32},{3,48},{4,64},{5,80},{6,96},{7,112},{8,128},{9... | collective-permute-start | bytes 110600 | tf_op jit(solution)/shard_map/ppermute | solution.py:501
  29.1 6.5 %copy-start = (bf16[3072,3072]{1,0:T(8,128)(2,1)}, bf16[3072,3072]{1,0:T(8,128)(2,1)S(1)}, u32[]{:S(2)}) copy-start(bf16[3072,3072]{1,0:T(8,128)(2,1)S(1)} %get-tuple-element.25.khi_ref) | copy-start | bytes 56623108
  35.5 3.7 %copy-start.2 = (f8e4m3fn[3072,3072]{1,0:T(32,128)(4,1)}, f8e4m3fn[3072,3072]{1,0:T(32,128)(4,1)S(1)}, u32[]{:S(2)}) copy-start(f8e4m3fn[3072,3072]{1,0:T(32,128)(4,1)S(1)} %get-tuple-element.26.klo_ref) | copy-start | bytes 28311556
  59.0 12.0 %all-to-all-start.1 = ((f32[16,16,128]{2,1,0:T(8,128)}), f32[16,16,128]{2,1,0:T(8,128)S(1)}, u32[]{:S(2)}, u32[]{:S(2)}) async-start(f32[16,16,128]{2,1,0:T(8,128)} %first_sum.1), calls=%async_computation.1 | async-start | bytes 262144 | tf_op jit(solution)/shard_map/all_to_all | solution.py:490
  71.0 6.4 %copy-start.1 = (bf16[3072,3072]{1,0:T(8,128)(2,1)S(1)}, bf16[3072,3072]{1,0:T(8,128)(2,1)}, u32[]{:S(2)}) copy-start(bf16[3072,3072]{1,0:T(8,128)(2,1)} %copy-done) | copy-start | bytes 56623108
  77.4 3.7 %copy-start.3 = (f8e4m3fn[3072,3072]{1,0:T(32,128)(4,1)S(1)}, f8e4m3fn[3072,3072]{1,0:T(32,128)(4,1)}, u32[]{:S(2)}) copy-start(f8e4m3fn[3072,3072]{1,0:T(32,128)(4,1)} %copy-done.2) | copy-start | bytes 28311556
  81.1 51.3 %copy-start.4 = (f32[9,3072]{1,0:T(8,128)S(1)}, f32[9,3072]{1,0:T(8,128)}, u32[]{:S(2)}) copy-start(f32[9,3072]{1,0:T(8,128)} %b_ref.3) | copy-start | bytes 331780
  89.8 4.3 %collective-permute-start.1 = (f32[8,32,128]{2,1,0:T(8,128)S(1)}, f32[8,32,128]{2,1,0:T(8,128)S(1)}, u32[]{:S(2)}, u32[]{:S(2)}) collective-permute-start(f32[8,32,128]{2,1,0:T(8,128)S(1)} %get-tuple-element.30), channel_id=1, source_target_pairs={{0,1},{1,0},{2,3},{3,2},{4,5},{5,4},{6,7},{7,6},{8,9},{9,8},{10,11... | collective-permute-start | bytes 393224 | tf_op jit(solution)/shard_map/ppermute | solution.py:508
  127.3 5.1 %collective-permute-start.2 = (f32[8,40,128]{2,1,0:T(8,128)S(1)}, f32[8,40,128]{2,1,0:T(8,128)S(1)}, u32[]{:S(2)}, u32[]{:S(2)}) collective-permute-start(f32[8,40,128]{2,1,0:T(8,128)S(1)} %all_to_all.28.mine), channel_id=1, source_target_pairs={{0,1},{1,0},{2,3},{3,2},{4,5},{5,4},{6,7},{7,6},{8,9},{9,8},{10,11... | collective-permute-start | bytes 491528 | tf_op jit(solution)/shard_map/ppermute | solution.py:508
